TPU v7x, 32 devices: a whole 2x2x4 slice. The times are simulated.
32 devices in a mesh: groups: 2 (over y), cell: 4 (over z), rep: 2 (over x), sub: 2 (over core).
Axes of the slice: x: 2, y: 2, z: 4, core: 2. Of those that a mesh axis runs over, the one named last changes fastest.
Arguments:
- points: float32 [4, 65536], P(None, ('groups', 'cell', 'rep', 'sub')), parts along dimension 1, may hold values from -4 to 4
- cotangent: float32 [4, 65536], P(None, ('groups', 'cell', 'rep', 'sub')), parts along dimension 1, may hold values from -6 to 6
- cell_ids: int32 [65536, 1], P(('groups', 'cell', 'rep', 'sub')), parts along dimension 0, may hold values from 0 to 31; in each aligned block of 2048 rows (0 to 2047, 2048 to 4095, ...) at most 128 rows name the same one
- camera_ids: int32 [65536], P(('groups', 'cell', 'rep', 'sub')), parts along dimension 0, may hold values from 0 to 63
- valid: int32 [65536], P(('groups', 'cell', 'rep', 'sub')), parts along dimension 0, may hold values 0 or 1
- w_enc: bfloat16 [32, 128, 256], P('cell'), may hold values from -0.5 to 0.5
- w_hidden: bfloat16 [32, 256, 128], P('cell'), may hold values from -0.375 to 0.375
- w_code: bfloat16 [32, 48, 128], P('cell'), may hold values from -0.875 to 0.875
- w_out: bfloat16 [32, 4, 128], P('cell'), may hold values from -0.5 to 0.5
- poses: float32 [3, 256], P(None, 'cell'), may hold values from -3 to 3
- codes: bfloat16 [48, 256], replicated, may hold values from -5 to 5
Outputs:
- grad_w_enc: float32 [64, 128, 256], P(('groups', 'cell')), parts along dimension 0
- grad_w_hidden: float32 [64, 256, 128], P(('groups', 'cell')), parts along dimension 0
- grad_w_code: float32 [64, 48, 128], P(('groups', 'cell')), parts along dimension 0
- grad_w_out: float32 [64, 4, 128], P(('groups', 'cell')), parts along dimension 0
- grad_poses: float32 [3, 512], P(None, ('groups', 'cell')), parts along dimension 1
- grad_codes: float32 [48, 512], P(None, ('groups', 'cell')), parts along dimension 1
There are 2 independent parts, one for each index of `groups`. A program takes and returns all parts, laid end to end along the dimension named above; an argument that names none is the same for every part. Nothing has to cross between parts.
Inputs may be any that keep to these rules, and one draw needn't show every extreme that they name: `cell_ids`: in each device's aligned block of 2048 samples no cell is named more than 128 times, a bound that some block reaches.
All inputs are finite; a program needn't handle non-finite values. No bound on the sum of `valid` on one device may be relied on, other than what follows from the above.
Results may differ from a plain program's by a relative error of at most 0.017.
Values may be sent and summed in bfloat16 or wider, within the bound.
No kernel may reach another device: no remote copies, remote signals or barrier semaphores. Data moves between devices by JAX's collectives and lax.ppermute only.
A program may use at most 64 MiB of HBM per device.

v0:
```python
import jax
import jax.numpy as jnp
from jax import lax
from jax.sharding import PartitionSpec as P


def as_sent(shard):
    return jax.tree.map(lambda a: a.astype(jnp.bfloat16) if a.dtype == jnp.float32 else a, shard)


def frequencies(freq_count):
    return 2.0 ** (jnp.arange(freq_count, dtype=jnp.float32) * 0.25)


def encode(coords, freq_count):
    angles = coords[:, None, :] * frequencies(freq_count)[None, :, None]
    stacked = jnp.concatenate([jnp.sin(angles), jnp.cos(angles)], axis=0)
    return stacked.reshape(8 * freq_count, coords.shape[-1])


def chain_coords(grad_encoded, coords, freq_count):
    angles = coords[:, None, :] * frequencies(freq_count)[None, :, None]
    halves = grad_encoded.reshape(2, 4, freq_count, coords.shape[-1])
    scaled = frequencies(freq_count)[None, :, None]
    return jnp.sum(scaled * (halves[0] * jnp.cos(angles) - halves[1] * jnp.sin(angles)), axis=1)


def cell_backward(encoded, code_rows, tangent, weight_enc, weight_hidden, weight_code, weight_out):
    highest = lax.Precision.HIGHEST
    pre_trunk = jnp.einsum("eh,es->hs", weight_enc, encoded, preferred_element_type=jnp.float32)
    trunk = jax.nn.softplus(pre_trunk).astype(jnp.bfloat16)
    pre_color = jnp.einsum("hc,hs->cs", weight_hidden, trunk, preferred_element_type=jnp.float32)
    pre_color = pre_color + jnp.einsum(
        "dc,ds->cs", weight_code, code_rows, preferred_element_type=jnp.float32
    )
    color_act = jax.nn.softplus(pre_color).astype(jnp.bfloat16)
    grad_w_out = jnp.einsum("os,cs->oc", tangent, color_act.astype(jnp.float32), precision=highest)
    grad_color = jnp.einsum("oc,os->cs", weight_out.astype(jnp.float32), tangent, precision=highest)
    grad_color = (grad_color * jax.nn.sigmoid(pre_color)).astype(jnp.bfloat16)
    grad_w_hidden = jnp.einsum("hs,cs->hc", trunk, grad_color, preferred_element_type=jnp.float32)
    grad_w_code = jnp.einsum("ds,cs->dc", code_rows, grad_color, preferred_element_type=jnp.float32)
    grad_code_row = jnp.einsum(
        "dc,cs->ds", weight_code, grad_color, preferred_element_type=jnp.float32
    )
    grad_trunk = jnp.einsum(
        "hc,cs->hs", weight_hidden, grad_color, preferred_element_type=jnp.float32
    )
    grad_trunk = (grad_trunk * jax.nn.sigmoid(pre_trunk)).astype(jnp.bfloat16)
    grad_w_enc = jnp.einsum("es,hs->eh", encoded, grad_trunk, preferred_element_type=jnp.float32)
    grad_encoded = jnp.einsum(
        "eh,hs->es", weight_enc, grad_trunk, preferred_element_type=jnp.float32
    )
    return (grad_encoded, grad_code_row, grad_w_enc, grad_w_hidden, grad_w_code, grad_w_out)


def slot_ranks(cell_of, cells_all):
    sample_count = cell_of.shape[0]
    block_rows = min(sample_count, 512)
    blocks = sample_count // block_rows
    one_hot = (cell_of[:, None] == jnp.arange(cells_all, dtype=jnp.int32)[None, :]).astype(
        jnp.bfloat16
    )
    grouped = one_hot.reshape(blocks, block_rows, cells_all)
    lower = (jnp.arange(block_rows)[:, None] > jnp.arange(block_rows)[None, :]).astype(jnp.bfloat16)
    within = jnp.einsum("ij,bjc->bic", lower, grouped, preferred_element_type=jnp.float32)
    totals = jnp.sum(grouped.astype(jnp.float32), axis=1)
    before = jnp.cumsum(totals, axis=0) - totals
    counted = (within + before[:, None, :]).reshape(sample_count, cells_all)
    return jnp.sum(counted * one_hot.astype(jnp.float32), axis=1).astype(jnp.int32)


def shards(
    points, cotangent, cell_ids, camera_ids, valid, w_enc, w_hidden, w_code, w_out, poses, codes
):
    highest = lax.Precision.HIGHEST
    cell_count = lax.axis_size("cell")
    local_cells = w_enc.shape[0]
    cells_all = local_cells * cell_count
    sample_count = points.shape[1]
    capacity = max(2, 2 * sample_count // cells_all)
    freq_count = w_enc.shape[1] // 8
    cams_local = poses.shape[1]
    code_width = codes.shape[0]
    cell_of = cell_ids[:, 0]
    cam_hot = (camera_ids[:, None] == jnp.arange(cams_local, dtype=jnp.int32)[None, :]).astype(
        jnp.float32
    )
    offsets = jnp.dot(poses, cam_hot.T, precision=highest)
    coords = jnp.concatenate([points[0:3] + offsets, points[3:4]], axis=0)
    tangent = cotangent * valid.astype(jnp.float32)[None, :]
    image_ids = lax.axis_index("cell") * cams_local + camera_ids
    slot_rank = slot_ranks(cell_of, cells_all)
    column = cell_of // local_cells * capacity + slot_rank
    slot_index = cell_of % local_cells * (cell_count * capacity) + column
    slot_total = local_cells * cell_count * capacity

    def place_rows(values):
        return jnp.zeros((values.shape[0], slot_total), values.dtype).at[:, slot_index].set(values)

    carried = encode(coords, freq_count).astype(jnp.bfloat16)
    values = (place_rows(carried), place_rows(tangent), place_rows(image_ids[None, :]))
    shaped = tuple((v.reshape(v.shape[0], local_cells, cell_count * capacity) for v in values))
    moved = jax.tree.map(
        lambda part, own: part.astype(own.dtype),
        lax.all_to_all(as_sent(shaped), "cell", split_axis=2, concat_axis=2, tiled=True),
        shaped,
    )
    features, tangents, images = tuple(moved)
    weights_here = (w_enc, w_hidden, w_code, w_out)

    def owner_cell(
        feature, cell_tangent, cell_images, weight_enc, weight_hidden, weight_code, weight_out
    ):
        code_rows = jnp.take(codes, cell_images[0], axis=1)
        grads = cell_backward(
            feature, code_rows, cell_tangent, weight_enc, weight_hidden, weight_code, weight_out
        )
        returning = grads[0]
        return (returning, grads[1], grads[2], grads[3], grads[4], grads[5])

    returning, grad_code_row, grad_w_enc, grad_w_hidden, grad_w_code, grad_w_out = jax.vmap(
        owner_cell, in_axes=(1, 1, 1, 0, 0, 0, 0), out_axes=(1, 1, 0, 0, 0, 0)
    )(
        features,
        tangents,
        images,
        weights_here[0],
        weights_here[1],
        weights_here[2],
        weights_here[3],
    )
    moved = (
        lax.all_to_all(
            (returning,)[0].astype(jnp.bfloat16), "cell", split_axis=2, concat_axis=2, tiled=True
        ).astype(jnp.float32),
    )
    (arrived,) = tuple((m.reshape(m.shape[0], slot_total) for m in moved))
    image_table = jax.ops.segment_sum(
        grad_code_row.reshape(code_width, -1).T,
        images.reshape(-1),
        num_segments=cams_local * cell_count,
    ).T
    code_part = lax.psum_scatter(
        image_table.astype(jnp.bfloat16), "cell", scatter_dimension=1, tiled=True
    )
    grad_back = arrived[:, slot_index]
    grad_coords = chain_coords(grad_back, coords, freq_count)
    pose_part = jnp.dot(grad_coords[0:3], cam_hot, precision=highest)
    totals = (
        lax.psum(grad_w_enc.astype(jnp.bfloat16), ("rep", "sub")).astype(jnp.float32),
        lax.psum(grad_w_hidden.astype(jnp.bfloat16), ("rep", "sub")).astype(jnp.float32),
        lax.psum(grad_w_code.astype(jnp.bfloat16), ("rep", "sub")).astype(jnp.float32),
        lax.psum(grad_w_out.astype(jnp.bfloat16), ("rep", "sub")).astype(jnp.float32),
        lax.psum(pose_part.astype(jnp.bfloat16), ("rep", "sub")).astype(jnp.float32),
        lax.psum(code_part, ("rep", "sub")).astype(jnp.float32),
    )
    return totals


def solution(mesh):
    in_specs = (
        P(None, ("groups", "cell", "rep", "sub")),
        P(None, ("groups", "cell", "rep", "sub")),
        P(("groups", "cell", "rep", "sub"), None),
        P(("groups", "cell", "rep", "sub")),
        P(("groups", "cell", "rep", "sub")),
        P("cell", None, None),
        P("cell", None, None),
        P("cell", None, None),
        P("cell", None, None),
        P(None, "cell"),
        P(),
    )
    out_specs = (
        P(("groups", "cell"), None, None),
        P(("groups", "cell"), None, None),
        P(("groups", "cell"), None, None),
        P(("groups", "cell"), None, None),
        P(None, ("groups", "cell")),
        P(None, ("groups", "cell")),
    )
    return jax.shard_map(shards, mesh=mesh, in_specs=in_specs, out_specs=out_specs, check_vma=False)
```

profile of v0, /device:TPU:0, one launch (start us, length us, event | category | flops | bytes accessed | tf_op | source)
XLA Modules:
  0.0 189.2 jit_solution(891400184674405313)
XLA Ops:
  8.1 0.5 broadcast.134
  8.6 1.4 reduce.4
  10.1 0.3 fusion.23
  10.5 0.8 compare_select_fusion.4
  11.2 0.7 broadcast_add_fusion
  11.9 8.1 %scatter_custom_fusion.2 = s32[4096]{0:T(1024)S(1)} fusion(s32[2048]{0:T(1024)S(1)} %bitcast.159, s32[2048]{0:T(1024)S(1)} %broadcast_add_fusion, s32[]{:T(128)} %constant.42.clone.1), kind=kCustom, calls=%fused_computation.94 | custom fusion | bytes 16388 | tf_op jit(solution)/shard_map/scatter | solution.py:98
  20.2 0.5 broadcast.135
  20.7 1.3 reduce.5
  22.0 0.8 reshape.205
  22.7 6.3 %all-to-all-start.2 = ((s32[4,1,1024]{2,1,0:T(1,128)}), s32[4,1,1024]{2,1,0:T(1,128)S(1)}, u32[]{:S(2)}, u32[]{:S(2)}) async-start(s32[4,1,1024]{2,1,0:T(1,128)} %reshape.205), calls=%async_computation.2 | async-start | bytes 32768 | tf_op jit(solution)/shard_map/all_to_all | solution.py:105
  29.1 0.7 convert_element_type.104
  29.8 0.8 slice.18
  30.6 0.7 fusion.9
  31.3 2.0 %fusion.30 = (bf16[4,16,2048]{2,1,0:T(8,128)(2,1)S(1)}, bf16[4,16,2048]{2,1,0:T(8,128)(2,1)S(1)}) fusion(f32[16]{0:T(128)S(1)} %multiply_power_fusion, f32[4,2048]{1,0:T(4,128)S(1)} %pad_maximum_fusion.1), kind=kLoop, calls=%fused_computation.59 | loop fusion | flops 393216 | bytes 557120 | tf_op jit(solution)/shard_map/convert.1
  33.4 1.3 copy.130
  34.7 6.5 %scatter_custom_fusion.1 = f32[4,4096]{0,1:T(8,128)S(1)} fusion(s32[2048]{0:T(1024)S(1)} %bitcast.160, f32[2048,4]{1,0:T(8,128)} %copy.130, f32[]{:T(128)} %constant.67.clone.1), kind=kCustom, calls=%fused_computation.49 | custom fusion | bytes 66048 | tf_op jit(solution)/shard_map/scatter | solution.py:98
  41.2 1.1 convert_element_type.126
  42.3 1.6 copy.167
  43.9 0.3 copy.132
  44.2 1.1 reshape.207
  45.3 5.1 %all-to-all-start.1 = ((bf16[4,2,2048]{2,1,0:T(2,128)(2,1)}), bf16[4,2,2048]{2,1,0:T(2,128)(2,1)S(1)}, u32[]{:S(2)}, u32[]{:S(2)}) async-start(bf16[4,2,2048]{2,1,0:T(2,128)(2,1)} %reshape.207), calls=%async_computation.1 | async-start | bytes 65536 | tf_op jit(solution)/shard_map/all_to_all | solution.py:105
  50.7 6.1 %scatter_custom_fusion = bf16[128,4096]{0,1:T(8,128)(2,1)S(1)} fusion(s32[2048]{0:T(1024)S(1)} %bitcast.161, bf16[2048,128]{1,0:T(8,128)(2,1)S(1)} %copy.128, bf16[]{:T(256)} %constant.40.clone.1), kind=kCustom, calls=%fused_computation.68 | custom fusion | bytes 1048578 | tf_op jit(solution)/shard_map/scatter | solution.py:98
  56.8 1.6 copy.129
  58.5 5.1 %all-to-all-start = ((bf16[128,8,512]{0,1,2:T(8,128)(2,1)}), bf16[128,8,512]{0,1,2:T(8,128)(2,1)S(1)}, u32[]{:S(2)}, u32[]{:S(2)}) async-start(bf16[128,8,512]{0,1,2:T(8,128)(2,1)} %copy.129), calls=%async_computation | async-start | bytes 2097152 | tf_op jit(solution)/shard_map/all_to_all | solution.py:105
  63.7 0.7 reduce.6
  64.4 0.4 reshape.206
  65.2 12.1 %gather_fusion = bf16[4096,48]{1,0:T(8,128)(2,1)S(1)} fusion(bf16[48,256]{0,1:T(8,128)(2,1)S(1)} %copy.138, s32[4096]{0:T(1024)S(1)} %broadcast_clamp_fusion), kind=kCustom, calls=%fused_computation | custom fusion | bytes 802816 | tf_op jit(solution)/shard_map/vmap(jit(_take))/gather | solution.py:114
  77.3 0.3 copy.139
  77.7 0.6 reshape.208
  78.3 0.3 copy.133
  78.6 9.6 %all-to-all-done = bf16[128,8,512]{0,1,2:T(8,128)(2,1)S(1)} async-done(((bf16[128,8,512]{0,1,2:T(8,128)(2,1)}), bf16[128,8,512]{0,1,2:T(8,128)(2,1)S(1)}, u32[]{:S(2)}, u32[]{:S(2)}) %all-to-all-start) | async-done | bytes 1048608 | tf_op jit(solution)/shard_map/all_to_all | solution.py:105
  88.2 0.7 copy.140
  88.9 1.8 fusion.58
  90.7 2.4 %fusion.55 = f32[8,512,128]{2,1,0:T(8,128)S(1)} fusion(bf16[8,256,128]{2,1,0:T(8,128)(2,1)S(1)} %copy-done, f32[8,512,256]{2,1,0:T(8,128)S(1)} %fusion.58), kind=kOutput, calls=%fused_computation.103 | convolution fusion | flops 275775488 | bytes 6815744 | tf_op jit(solution)/shard_map/vmap(hc,hs->cs)/dot_general | solution.py:32
  93.1 0.5 convolution_add_fusion
  93.6 1.3 copy-done.2
  94.9 0.7 fusion.19
  95.7 1.2 fusion.1
  96.9 1.3 convolution_convert_fusion.2
  98.2 0.7 fusion.20
  98.9 1.7 copy.147
  100.6 4.2 %all-to-all-start.3 = ((bf16[128,8,512]{0,1,2:T(8,128)(2,1)}), bf16[128,8,512]{0,1,2:T(8,128)(2,1)}, u32[]{:S(2)}, u32[]{:S(2)}) async-start(bf16[128,8,512]{0,1,2:T(8,128)(2,1)} %copy.147), calls=%async_computation.3 | async-start | bytes 2097152 | tf_op jit(solution)/shard_map/all_to_all | solution.py:133
  105.1 1.0 convolution_convert_fusion.3
  106.0 5.6 %convolution_convert_fusion.1 = bf16[8,256,128]{2,1,0:T(8,128)(2,1)} fusion(bf16[8,128,512]{1,2,0:T(8,128)(2,1)S(1)} %fusion.19, f32[8,512,256]{2,1,0:T(8,128)} %copy-done.1), kind=kOutput, calls=%fused_computation.40 | convolution fusion | flops 276037632 | bytes 5767168 | tf_op jit(solution)/shard_map/vmap(hs,cs->hc)/dot_general | solution.py:40
  111.8 0.5 convolution_bitcast_fusion.1
  112.4 0.6 copy.154
  113.0 24.3 %scatter_custom_fusion.3 = f32[256,48]{1,0:T(8,128)S(1)} fusion(s32[4096]{0:T(1024)S(1)} %bitcast.164, f32[4096,48]{1,0:T(8,128)S(1)} %copy.154, f32[]{:T(128)} %constant.67.clone.1), kind=kCustom, calls=%fused_computation.79 | custom fusion | flops 196608 | bytes 49156 | tf_op jit(solution)/shard_map/scatter-add | solution.py:138
  137.3 0.6 convert_bitcast_fusion
  138.0 2.9 %convolution_convert_fusion.4 = bf16[8,4,128]{2,1,0:T(4,128)(2,1)S(1)} fusion(bf16[4,8,512]{2,0,1:T(4,128)(2,1)S(1)} %copy.133, f32[8,512,128]{2,1,0:T(8,128)} %copy-done.2), kind=kOutput, calls=%fused_computation.47 | convolution fusion | flops 7868416 | bytes 2138112 | tf_op jit(solution)/shard_map/vmap(os,cs->oc)/dot_general | solution.py:37
  140.9 9.6 %all-reduce.4.cloned.1.call-done = (bf16[8,128,256]{2,1,0:T(8,128)(2,1)}, bf16[8,256,128]{2,1,0:T(8,128)(2,1)}, bf16[8,48,128]{2,1,0:T(8,128)(2,1)}) async-done(((bf16[8,128,256]{2,1,0:T(8,128)(2,1)}, bf16[8,256,128]{2,1,0:T(8,128)(2,1)}, bf16[8,48,128]{2,1,0:T(8,128)(2,1)}), (bf16[8,128,256]{2,1,0:T(8,128)(2,1)}, bf16[8,256,128]{2,1,0:T(8,128)(2,1)}, ...) | async-done | bytes 1146896 | tf_op jit(solution)/shard_map/psum | solution.py:150
  150.5 1.6 convert_element_type.115
  152.1 2.1 %convert_element_type.111 = f32[8,128,256]{2,1,0:T(8,128)} convert(bf16[8,128,256]{2,1,0:T(8,128)(2,1)} %get-tuple-element.45) | non-fusion elementwise | flops 262144 | bytes 1572864 | tf_op jit(solution)/shard_map/convert_element_type | solution.py:150
  154.2 1.0 convert_element_type.113
  155.3 1.4 copy.148
  156.6 7.6 %gather_fusion.1 = f32[2048,128]{1,0:T(8,128)} fusion(f32[128,4096]{0,1:T(8,128)S(1)} %bitcast.142, s32[2048]{0:T(1024)S(1)} %broadcast_clamp_fusion.1), kind=kCustom, calls=%fused_computation.1 | custom fusion | bytes 2105344 | tf_op jit(solution)/shard_map/gather | solution.py:146
  164.2 1.9 fusion.57
  166.1 0.3 copy.149
  166.4 0.3 copy.150
  166.7 2.3 %fusion.35 = f32[4,2048]{1,0:T(4,128)S(1)} fusion(f32[16]{0:T(128)S(1)} %multiply_power_fusion, f32[4,2048]{1,0:T(4,128)S(1)} %pad_maximum_fusion.1, f32[64,2048]{1,0:T(8,128)S(1)} %copy.150, f32[64,2048]{1,0:T(8,128)S(1)} %copy.149), kind=kLoop, calls=%fused_computation.64 | loop fusion | flops 778240 | bytes 1114176 | tf_op jit(solution)/shard_map/reduce_sum | solution.py:25
  169.0 0.6 convolution_convert_fusion.5
  169.7 10.3 %all-reduce = (bf16[48,64]{0,1:T(8,128)(2,1)S(1)}, bf16[8,4,128]{2,1,0:T(4,128)(2,1)S(1)}, bf16[3,64]{1,0:T(4,128)(2,1)S(1)}) all-reduce(bf16[48,64]{0,1:T(8,128)(2,1)} %reduce-scatter.2.cloned.1.call-done, bf16[8,4,128]{2,1,0:T(4,128)(2,1)S(1)} %convolution_convert_fusion.4, ...), channel_id=1, replica_groups=mesh['groups'=2,'cell'=4,'rep'=2,'sub'=2] {'rep','sub'}, use_global_device_ids=true, to_apply=%region_14.15 | all-reduce | flops 7360 | bytes 29440 | tf_op jit(solution)/shard_map/psum | solution.py:155
  179.9 0.6 convert_element_type.122
  180.5 0.7 copy.155
  181.2 0.6 convert_element_type.118
  (56 shorter events, 1.7 us)
Async XLA Ops:
  8.0 82.7 %copy-start = (bf16[8,256,128]{2,1,0:T(8,128)(2,1)S(1)}, bf16[8,256,128]{2,1,0:T(8,128)(2,1)}, u32[]{:S(2)}) copy-start(bf16[8,256,128]{2,1,0:T(8,128)(2,1)} %param.17) | copy-start | bytes 1572868
  8.0 22.5 %copy-start.8 = (s32[2048]{0:T(1024)S(1)}, s32[2048]{0:T(1024)}, u32[]{:S(2)}) copy-start(s32[2048]{0:T(1024)} %param.14) | copy-start | bytes 24580
  8.0 22.5 %copy-start.9 = (f32[4,2048]{1,0:T(4,128)S(1)}, f32[4,2048]{1,0:T(4,128)}, u32[]{:S(2)}) copy-start(f32[4,2048]{1,0:T(4,128)} %param.11) | copy-start | bytes 98308
  8.0 22.5 %copy-start.11 = (f32[3,64]{1,0:T(4,128)S(1)}, f32[3,64]{1,0:T(4,128)}, u32[]{:S(2)}) copy-start(f32[3,64]{1,0:T(4,128)} %param.20) | copy-start | bytes 2308
  8.0 25.3 %copy-start.6 = (f32[4,2048]{1,0:T(4,128)S(1)}, f32[4,2048]{1,0:T(4,128)}, u32[]{:S(2)}) copy-start(f32[4,2048]{1,0:T(4,128)} %param.12) | copy-start | bytes 98308
  22.7 22.6 %all-to-all-start.2 = ((s32[4,1,1024]{2,1,0:T(1,128)}), s32[4,1,1024]{2,1,0:T(1,128)S(1)}, u32[]{:S(2)}, u32[]{:S(2)}) async-start(s32[4,1,1024]{2,1,0:T(1,128)} %reshape.205), calls=%async_computation.2 | async-start | bytes 32768 | tf_op jit(solution)/shard_map/all_to_all | solution.py:105
  45.3 13.2 %all-to-all-start.1 = ((bf16[4,2,2048]{2,1,0:T(2,128)(2,1)}), bf16[4,2,2048]{2,1,0:T(2,128)(2,1)S(1)}, u32[]{:S(2)}, u32[]{:S(2)}) async-start(bf16[4,2,2048]{2,1,0:T(2,128)(2,1)} %reshape.207), calls=%async_computation.1 | async-start | bytes 65536 | tf_op jit(solution)/shard_map/all_to_all | solution.py:105
  56.8 6.8 %copy-start.7 = (bf16[48,256]{1,0:T(8,128)(2,1)S(1)}, bf16[48,256]{1,0:T(8,128)(2,1)}, u32[]{:S(2)}) copy-start(bf16[48,256]{1,0:T(8,128)(2,1)} %param.21) | copy-start | bytes 73732
  58.5 29.7 %all-to-all-start = ((bf16[128,8,512]{0,1,2:T(8,128)(2,1)}), bf16[128,8,512]{0,1,2:T(8,128)(2,1)S(1)}, u32[]{:S(2)}, u32[]{:S(2)}) async-start(bf16[128,8,512]{0,1,2:T(8,128)(2,1)} %copy.129), calls=%async_computation | async-start | bytes 2097152 | tf_op jit(solution)/shard_map/all_to_all | solution.py:105
  90.7 5.0 %copy-start.1 = (f32[8,512,256]{2,1,0:T(8,128)}, f32[8,512,256]{2,1,0:T(8,128)S(1)}, u32[]{:S(2)}) copy-start(f32[8,512,256]{2,1,0:T(8,128)S(1)} %fusion.58) | copy-start | bytes 12582916
  90.7 2.4 %copy-start.5 = (bf16[8,48,128]{2,1,0:T(8,128)(2,1)S(1)}, bf16[8,48,128]{2,1,0:T(8,128)(2,1)}, u32[]{:S(2)}) copy-start(bf16[8,48,128]{2,1,0:T(8,128)(2,1)} %param.18) | copy-start | bytes 294916
  93.0 1.9 copy-start.10
  93.6 1.3 copy-start.2
  96.9 1.3 copy-start.3
  100.6 54.7 %all-to-all-start.3 = ((bf16[128,8,512]{0,1,2:T(8,128)(2,1)}), bf16[128,8,512]{0,1,2:T(8,128)(2,1)}, u32[]{:S(2)}, u32[]{:S(2)}) async-start(bf16[128,8,512]{0,1,2:T(8,128)(2,1)} %copy.147), calls=%async_computation.3 | async-start | bytes 2097152 | tf_op jit(solution)/shard_map/all_to_all | solution.py:133
  104.8 45.7 %all-reduce.4.cloned.1.call-start = ((), (), s32[]{:S(2)}) async-start(), calls=%async_computation.6 | async-start | bytes 2293760 | tf_op jit(solution)/shard_map/psum | solution.py:150
  111.7 58.0 %reduce-scatter.2.cloned.1.call-start = ((), (), s32[]{:S(2)}) async-start(), calls=%async_computation.5 | async-start | bytes 81920 | tf_op jit(solution)/shard_map/reduce_scatter | solution.py:143
  150.5 3.8 %copy-start.4 = (bf16[8,256,128]{2,1,0:T(8,128)(2,1)S(1)}, bf16[8,256,128]{2,1,0:T(8,128)(2,1)}, u32[]{:S(2)}) copy-start(bf16[8,256,128]{2,1,0:T(8,128)(2,1)} %get-tuple-element.46) | copy-start | bytes 1572868
Sparse Core Ops, SparseCore 0:
  111.8 38.6 all-reduce.3
Sparse Core Ops, SparseCore 1:
  138.1 21.3 reduce-scatter.1
where the time goes:
time: 190 us; the launch traced here: 189 us
  local copies, waits for them, and re-layouts  60.4 us (32%)
  other arithmetic  42.2 us (22%)
  starting transfers between devices  21.1 us (11%)
  matrix products  20.2 us (11%)
  waiting for transfers between devices  19.2 us (10%)
  between operations  15.9 us (8%)
  blocking collectives  10.3 us (5%)
    scatter-add x1, other arithmetic, shards(): jax.ops.segment_sum(grad_code_row.reshape(code_width, -1).T, images.resha...  24.3 us
    scatter x3, local copies, waits for them, and re-layouts, place_rows(): jnp.zeros((values.shape[0], slot_total), values.dtype).at[:, slot_index]  20.6 us
    all_to_all x3, starting transfers between devices, shards(): lax.all_to_all(as_sent(shaped), 'cell', split_axis=2, concat_axis=2, tile...  16.5 us
    gather x2, local copies, waits for them, and re-layouts, owner_cell(): code_rows = jnp.take(codes, cell_images[0], axis=1)  12.5 us
    psum x1, blocking collectives, shards(): lax.psum(code_part, ('rep', 'sub')).astype(jnp.float32)  10.3 us
    psum x1, waiting for transfers between devices, shards(): lax.psum(grad_w_enc.astype(jnp.bfloat16), ('rep', 'sub'))  9.59 us
    all_to_all x3, waiting for transfers between devices, shards(): lax.all_to_all(as_sent(shaped), 'cell', split_axis=2, concat_axis=2, tile...  9.58 us
    unnamed x37, local copies, waits for them, and re-layouts  7.81 us
  transfers between devices with their start and end apart: 6, of which 2 were waited for; matrix products, arithmetic and copies ran while one was open for 50% of the time, Pallas kernels for 0%

commit v1 on v0

v1 whole, which is shorter than its diff:
```python
import functools

import jax
import jax.numpy as jnp
from jax import lax
from jax.experimental import pallas as pl
from jax.experimental.pallas import tpu as pltpu
from jax.sharding import PartitionSpec as P

BF16 = jnp.bfloat16
F32 = jnp.float32
VMEM_BYTES = 50 * 1024 * 1024
RECORD = 16
TANGENT_ROW = 8
CAMERA_ROW = 12


def dot_nn(a, b):
    return lax.dot_general(a, b, (((1,), (0,)), ((), ())), preferred_element_type=F32)


def dot_nt(a, b):
    return lax.dot_general(a, b, (((1,), (1,)), ((), ())), preferred_element_type=F32)


def dot_tn(a, b):
    return lax.dot_general(a, b, (((0,), (0,)), ((), ())), preferred_element_type=F32)


def iota(shape, dim):
    return lax.broadcasted_iota(jnp.int32, shape, dim)


def place_kernel(cells_all, cap, n_cell, n_part, me_ref, points_ref, cot_ref, cell_ref, cam_ref,
                 valid_ref, poses_ref, *refs):
    outs, spread = refs[:n_part], refs[n_part]
    n = points_ref.shape[1]
    cams = poses_ref.shape[1]
    lc = cells_all // (n_cell * n_part)
    cam = cam_ref[...]
    cam_hot = (iota((cams, n), 0) == cam).astype(F32).astype(BF16)
    poses = poses_ref[...]
    high = poses.astype(BF16)
    rest = poses - high.astype(F32)
    middle = rest.astype(BF16)
    low = (rest - middle.astype(F32)).astype(BF16)
    offsets = (dot_nn(high, cam_hot) + dot_nn(middle, cam_hot)) + dot_nn(low, cam_hot)
    points = points_ref[...]
    coords = jnp.concatenate([points[0:3] + offsets, points[3:4]], axis=0)
    coords_high = coords.astype(BF16).astype(F32)
    tangent = cot_ref[...] * valid_ref[...].astype(F32)
    record = jnp.concatenate(
        [coords_high, coords - coords_high, tangent, cam.astype(F32), jnp.zeros((3, n), F32)], axis=0
    )
    width = 256
    upper = (iota((width, width), 0) <= iota((width, width), 1)).astype(F32).astype(BF16)
    cell_of = cell_ref[...]
    carry = jnp.zeros((cells_all, 1), F32)
    ranks = []
    for b in range(n // width):
        here = cell_of[:, b * width:(b + 1) * width]
        hot = (iota((cells_all, width), 0) == here).astype(F32)
        counted = dot_nn(hot.astype(BF16), upper) + carry
        ranks.append(jnp.sum(counted * hot, axis=0, keepdims=True) - 1.0)
        carry = counted[:, width - 1:width]
    rank = jnp.concatenate(ranks, axis=1).astype(jnp.int32)
    rank_hot = (iota((cap, n), 0) == rank).astype(F32).astype(BF16)
    for c in range(cells_all):
        spread[c * RECORD:(c + 1) * RECORD, :] = jnp.where(cell_of == c, record, 0.0).astype(BF16)
    me_cell, me_part = me_ref[0], me_ref[1]
    rows = lc * RECORD
    for kp in range(n_part):
        for kc in range(n_cell):
            owner = (me_cell ^ kc) * n_part + (me_part ^ kp)
            start = pl.multiple_of(owner * rows, rows)
            outs[kp][kc] = dot_nt(spread[pl.ds(start, rows), :], rank_hot).astype(BF16)


def sin_cos(x):
    n = jnp.floor(x * 0.6366197723675814 + 0.5)
    r = ((x - n * 1.5703125) - n * 4.837512969970703125e-4) - n * 7.54978995489188216e-8
    z = r * r
    s = r + (r * z) * (-1.6666654611e-1 + z * (8.3321608736e-3 + z * -1.9515295891e-4))
    c = (1.0 - 0.5 * z) + (z * z) * (
        4.166664568298827e-2 + z * (-1.388731625493765e-3 + z * 2.443315711809948e-5))
    q = n.astype(jnp.int32)
    swap = (q & 1) == 1
    sine = jnp.where(swap, c, s)
    cosine = jnp.where(swap, s, c)
    sine = jnp.where((q & 2) == 2, -sine, sine)
    cosine = jnp.where(((q + 1) & 2) == 2, -cosine, cosine)
    return sine, cosine


def double_angle(s, c):
    return 2.0 * s * c, 1.0 - 2.0 * s * s


def soft(x):
    e = jnp.exp(-jnp.abs(x))
    u = 1.0 + e
    plus = jnp.maximum(x, 0.0) + jnp.where(e < 1e-4, e, jnp.log(u))
    r = pl.reciprocal(u, approx=True)
    return plus, jnp.where(x >= 0.0, r, e * r)


def cell_kernel(n_cell, freq_count, has_table, me_ref, codes_ref, w_enc_ref, w_hidden_ref, w_code_ref,
                w_out_ref, *refs):
    arrived = refs[:n_cell]
    at = n_cell
    if has_table:
        table_in = refs[at]
        at += 1
    packed_ref, table_ref = refs[at], refs[at + 1]
    enc_s, gt_s, trunk_s, gc_s, act_s, rec_s = refs[at + 2:]
    width = arrived[0].shape[2]
    cams = codes_ref.shape[2]
    code = codes_ref.shape[1]
    color = w_code_ref.shape[2]
    hidden = w_hidden_ref.shape[1]
    w_enc, w_hidden, w_code, w_out = w_enc_ref[0], w_hidden_ref[0], w_code_ref[0], w_out_ref[0]
    half = freq_count // 2
    scale = jnp.exp2(iota((half, 1), 0).astype(F32) * 0.25)
    top = 2.0 ** (half // 4)
    for kc in range(n_cell):
        cols = slice(kc * width, (kc + 1) * width)
        rec = arrived[kc][0]
        rec_s[:, cols] = rec
        recf = rec.astype(F32)
        coords = recf[0:4] + recf[4:8]
        cam = recf[CAMERA_ROW:CAMERA_ROW + 1].astype(jnp.int32)
        cam_hot = (iota((cams, width), 0) == cam).astype(F32).astype(BF16)
        code_rows = dot_nn(codes_ref[kc], cam_hot).astype(BF16)
        angles = jnp.concatenate([coords[j:j + 1] * scale for j in range(4)], axis=0)
        s1, c1 = sin_cos(angles)
        s2, c2 = s1, c1
        for _ in range(half // 4):
            s2, c2 = double_angle(s2, c2)
        pieces = []
        for a, b in ((s1, s2), (c1, c2)):
            for j in range(4):
                pieces += [a[j * half:(j + 1) * half], b[j * half:(j + 1) * half]]
        encoded = jnp.concatenate(pieces, axis=0).astype(BF16)
        enc_s[:, cols] = encoded
        trunk, slope_trunk = soft(dot_tn(w_enc, encoded))
        trunk = trunk.astype(BF16)
        trunk_s[0:hidden, cols] = trunk
        trunk_s[hidden:, cols] = code_rows
        act, slope_color = soft(dot_tn(w_hidden, trunk) + dot_tn(w_code, code_rows))
        act_s[:, cols] = act.astype(BF16)
        gc = (dot_tn(w_out, rec) * slope_color).astype(BF16)
        gc_s[:, cols] = gc
        gt = (dot_nn(w_hidden, gc) * slope_trunk).astype(BF16)
        gt_s[:, cols] = gt
        grad_code = dot_nn(w_code, gc)
        grad_enc = dot_nn(w_enc, gt)
        sums = []
        for j in range(3):
            a, b = j * 2 * half, (4 + j) * 2 * half
            js = slice(j * half, (j + 1) * half)
            first = grad_enc[a:a + half] * c1[js] - grad_enc[b:b + half] * s1[js]
            second = (grad_enc[a + half:a + 2 * half] * c2[js]
                      - grad_enc[b + half:b + 2 * half] * s2[js])
            sums.append(jnp.sum((first + top * second) * scale, axis=0, keepdims=True))
        row = iota((RECORD, width), 0)
        tail = jnp.where(row == 0, sums[0], jnp.where(row == 1, sums[1], jnp.where(row == 2, sums[2], 0.0)))
        per_sample = jnp.concatenate([grad_code, tail], axis=0).astype(BF16)
        table = dot_nt(per_sample, cam_hot)
        if has_table:
            table = table + table_in[kc]
        table_ref[kc] = table.astype(table_ref.dtype)
    g_enc = dot_nt(enc_s[...], gt_s[...]).astype(BF16)
    enc_rows = g_enc.shape[0]
    at_row = 0
    for part in range(hidden // color):
        packed_ref[at_row:at_row + enc_rows, :] = g_enc[:, part * color:(part + 1) * color]
        at_row += enc_rows
    packed_ref[at_row:at_row + hidden + code, :] = dot_nt(trunk_s[...], gc_s[...]).astype(BF16)
    at_row += hidden + code
    packed_ref[at_row:at_row + RECORD, :] = dot_nt(rec_s[...], act_s[...]).astype(BF16)


def unpack_kernel(lc, n_in, at_ref, *refs):
    ins = refs[:n_in]
    enc_ref, hidden_ref, code_ref, out_ref = refs[n_in:]
    enc_rows, enc_cols = enc_ref.shape[1:]
    hidden, color = hidden_ref.shape[1:]
    code = code_ref.shape[1]
    outs = out_ref.shape[1]
    for i in range(n_in):
        cell = at_ref[i // lc] + i % lc
        src = ins[i]
        row = 0
        for part in range(enc_cols // color):
            enc_ref[cell, :, part * color:(part + 1) * color] = src[row:row + enc_rows, :].astype(F32)
            row += enc_rows
        hidden_ref[cell] = src[row:row + hidden, :].astype(F32)
        row += hidden
        code_ref[cell] = src[row:row + code, :].astype(F32)
        row += code
        out_ref[cell] = src[row:row + RECORD, :].astype(F32)[TANGENT_ROW:TANGENT_ROW + outs]


def whole_spec(shape):
    return pl.BlockSpec(shape, functools.partial(lambda d, *_: (0,) * d, len(shape)))


def exchange(value, axes, count, k):
    if k == 0:
        return value
    return lax.ppermute(value, axes, [(i, i ^ k) for i in range(count)])


def shards(points, cotangent, cell_ids, camera_ids, valid, w_enc, w_hidden, w_code, w_out, poses, codes):
    n_cell, n_rep, n_sub = lax.axis_size("cell"), lax.axis_size("rep"), lax.axis_size("sub")
    n_part = n_rep * n_sub
    part_axes = ("rep", "sub")
    local = w_enc.shape[0]
    lc = local // n_part
    cells_all = local * n_cell
    n = points.shape[1]
    cap = max(2, 2 * n // cells_all)
    enc, hidden = w_enc.shape[1:]
    color = w_hidden.shape[2]
    freq_count = enc // 8
    cams = poses.shape[1]
    code = codes.shape[0]
    width = n_part * cap
    me_cell = lax.axis_index("cell")
    me_part = lax.axis_index(part_axes)
    me = jnp.stack([me_cell, me_part]).astype(jnp.int32)
    params = pltpu.CompilerParams(vmem_limit_bytes=VMEM_BYTES)

    sent = pl.pallas_call(
        functools.partial(place_kernel, cells_all, cap, n_cell, n_part),
        out_shape=[jax.ShapeDtypeStruct((n_cell, lc * RECORD, cap), BF16)] * n_part,
        in_specs=[pl.BlockSpec(memory_space=pltpu.SMEM)] + [pl.BlockSpec(memory_space=pltpu.VMEM)] * 6,
        out_specs=[pl.BlockSpec(memory_space=pltpu.VMEM)] * n_part,
        scratch_shapes=[pltpu.VMEM((cells_all * RECORD, n), BF16)],
        compiler_params=params,
        name="place",
    )(me, points, cotangent, cell_ids.reshape(1, n), camera_ids.reshape(1, n), valid.reshape(1, n), poses)

    order = me_cell ^ jnp.arange(n_cell, dtype=jnp.int32)
    codes_rel = codes.reshape(code, n_cell, cams).transpose(1, 0, 2)[order]
    w_out_rows = jnp.pad(w_out, ((0, 0), (TANGENT_ROW, RECORD - TANGENT_ROW - w_out.shape[1]), (0, 0)))

    near = [exchange(sent[kp], part_axes, n_part, kp) for kp in range(n_part)]
    arrived = []
    for kc in range(n_cell):
        lanes = jnp.concatenate([near[kp][kc] for kp in range(n_part)], axis=-1)
        arrived.append(exchange(lanes.reshape(lc, RECORD, width), "cell", n_cell, kc))

    packed_rows = enc * (hidden // color) + hidden + code + RECORD
    table_rows = code + RECORD
    slots = n_cell * width
    own = []
    table = None
    for j in range(lc):
        last = j == lc - 1
        pick = functools.partial(lambda step, i, me_ref: (me_ref[1] * lc + step, 0, 0), j)
        take = functools.partial(lambda step, i, me_ref: (step, 0, 0), j)
        in_specs = [
            whole_spec((n_cell, code, cams)),
            pl.BlockSpec((1, enc, hidden), pick),
            pl.BlockSpec((1, hidden, color), pick),
            pl.BlockSpec((1, code, color), pick),
            pl.BlockSpec((1, RECORD, color), pick),
        ] + [pl.BlockSpec((1, RECORD, width), take)] * n_cell
        operands = [codes_rel, w_enc, w_hidden, w_code, w_out_rows] + arrived
        if table is not None:
            in_specs.append(whole_spec((n_cell, table_rows, cams)))
            operands.append(table)
        packed, table = pl.pallas_call(
            functools.partial(cell_kernel, n_cell, freq_count, table is not None),
            grid_spec=pltpu.PrefetchScalarGridSpec(
                num_scalar_prefetch=1,
                grid=(1,),
                in_specs=in_specs,
                out_specs=[whole_spec((packed_rows, color)), whole_spec((n_cell, table_rows, cams))],
                scratch_shapes=[
                    pltpu.VMEM((enc, slots), BF16),
                    pltpu.VMEM((hidden, slots), BF16),
                    pltpu.VMEM((hidden + code, slots), BF16),
                    pltpu.VMEM((color, slots), BF16),
                    pltpu.VMEM((color, slots), BF16),
                    pltpu.VMEM((RECORD, slots), BF16),
                ],
            ),
            out_shape=[
                jax.ShapeDtypeStruct((packed_rows, color), BF16),
                jax.ShapeDtypeStruct((n_cell, table_rows, cams), BF16 if last else F32),
            ],
            compiler_params=params,
            name="cell_net",
        )(me, *operands)
        own.append(packed)

    held = [[None] * lc for _ in range(n_part)]
    for j in range(lc):
        for kr in range(n_rep):
            over_rep = exchange(own[j], "rep", n_rep, kr)
            for ks in range(n_sub):
                held[kr * n_sub + ks][j] = exchange(over_rep, "sub", n_sub, ks)
    starts = ((me_part ^ jnp.arange(n_part, dtype=jnp.int32)) * lc).astype(jnp.int32)
    flat = [held[k][j] for k in range(n_part) for j in range(lc)]
    grads = pl.pallas_call(
        functools.partial(unpack_kernel, lc, len(flat)),
        out_shape=[
            jax.ShapeDtypeStruct((local, enc, hidden), F32),
            jax.ShapeDtypeStruct((local, hidden, color), F32),
            jax.ShapeDtypeStruct((local, code, color), F32),
            jax.ShapeDtypeStruct((local, w_out.shape[1], color), F32),
        ],
        in_specs=[pl.BlockSpec(memory_space=pltpu.SMEM)]
        + [pl.BlockSpec(memory_space=pltpu.VMEM)] * len(flat),
        out_specs=[pl.BlockSpec(memory_space=pltpu.VMEM)] * 4,
        compiler_params=params,
        name="unpack",
    )(starts, *flat)

    mine = sum(exchange(table[kc], "cell", n_cell, kc).astype(F32) for kc in range(n_cell))
    mine = mine.astype(BF16)
    total = sum(exchange(mine, part_axes, n_part, kp).astype(F32) for kp in range(n_part))
    return (*grads, total[code:code + 3], total[0:code])


def solution(mesh):
    samples = ("groups", "cell", "rep", "sub")
    in_specs = (
        P(None, samples),
        P(None, samples),
        P(samples, None),
        P(samples),
        P(samples),
        P("cell", None, None),
        P("cell", None, None),
        P("cell", None, None),
        P("cell", None, None),
        P(None, "cell"),
        P(),
    )
    out_specs = (
        P(("groups", "cell"), None, None),
        P(("groups", "cell"), None, None),
        P(("groups", "cell"), None, None),
        P(("groups", "cell"), None, None),
        P(None, ("groups", "cell")),
        P(None, ("groups", "cell")),
    )
    return jax.shard_map(shards, mesh=mesh, in_specs=in_specs, out_specs=out_specs, check_vma=False)
```

time: 190 us -> 52.1 us (0.27)
  local copies, waits for them, and re-layouts: 60.4 us -> 8.56 us
  other arithmetic: 42.2 us -> 0.14 us
  matrix products: 20.2 us -> 0 us
  Pallas kernels: 0 us -> 16.4 us
  between operations: 15.9 us -> 0.78 us
  waiting for transfers between devices: 19.2 us -> 8.77 us
  blocking collectives: 10.3 us -> 0 us
  starting transfers between devices: 21.1 us -> 17 us
    scatter-add x1 -> x0, other arithmetic: 24.3 us -> none  [shards(): jax.ops.segment_sum(grad_code_row.reshape(code_width, -1).T, images.resha...]
    all_to_all x4 -> x0, starting transfers between devices: 20.8 us -> none  [the longest x3 16.5 us: shards(): lax.all_to_all(as_sent(shaped), 'cell', split_axis=2, concat_axis=2, tile...]
    scatter x3 -> x0, local copies, waits for them, and re-layouts: 20.6 us -> none  [place_rows(): jnp.zeros((values.shape[0], slot_total), values.dtype).at[:, slot_index]]
    dot_general x14 -> x0, matrix products: 20.2 us -> none  [the longest x1 5.6 us: cell_backward(): jnp.einsum('hs,cs->hc', trunk, grad_color, preferred_element_type=jnp.flo...]
    gather x3 -> x1, local copies, waits for them, and re-layouts: 20 us -> 0.56 us  [shards(): codes_rel = codes.reshape(code, n_cell, cams).transpose(1, 0, 2)[order]]
    ppermute x0 -> x18, starting transfers between devices: none -> 17 us  [exchange(): return lax.ppermute(value, axes, [(i, i ^ k) for i in range(count)])]
    pallas_call x0 -> x4, Pallas kernels: none -> 16.4 us  [the longest x2 10.1 us: shards(): pl.pallas_call(functools.partial(cell_kernel, n_cell, freq_count, table i...]
    psum x1 -> x0, blocking collectives: 10.3 us -> none  [shards(): lax.psum(code_part, ('rep', 'sub')).astype(jnp.float32)]
  transfers between devices with their start and end apart: 6 -> 18, of which waited for: 2 -> 8; matrix products, arithmetic and copies ran while one was open for 50% -> 7% of each run, Pallas kernels for 0% -> 0%
where the time goes in v1:
time: 52.1 us; the launch traced here: 51.7 us
  starting transfers between devices  17 us (33%)
  Pallas kernels  16.4 us (31%)
  waiting for transfers between devices  8.77 us (17%)
  local copies, waits for them, and re-layouts  8.56 us (16%)
  between operations  0.78 us (1%)
    ppermute x18, starting transfers between devices, exchange(): return lax.ppermute(value, axes, [(i, i ^ k) for i in range(count)])  17 us
    pallas_call x2, Pallas kernels, shards(): pl.pallas_call(functools.partial(cell_kernel, n_cell, freq_count, table i...  10.1 us
    ppermute x18, waiting for transfers between devices, exchange(): return lax.ppermute(value, axes, [(i, i ^ k) for i in range(count)])  8.77 us
    unnamed x18, local copies, waits for them, and re-layouts  5.24 us
    pallas_call x1, Pallas kernels, shards(): pl.pallas_call(functools.partial(place_kernel, cells_all, cap, n_cell, n_...  4.26 us
    pallas_call x1, Pallas kernels, shards(): pl.pallas_call(functools.partial(unpack_kernel, lc, len(flat)), out_shape...  2.05 us
    slice x2, local copies, waits for them, and re-layouts, shards(): return (*grads, total[code:code + 3], total[0:code])  1.19 us
  transfers between devices with their start and end apart: 18, of which 8 were waited for; matrix products, arithmetic and copies ran while one was open for 7% of the time, Pallas kernels for 0%

profile of v1, /device:TPU:0, one launch (start us, length us, event | category | flops | bytes accessed | tf_op | source)
XLA Modules:
  0.0 51.7 jit_solution(10815262046532548587)
XLA Ops:
  0.6 0.0 copy-start.3
  0.6 0.0 copy-start
  0.7 0.1 pad_add_fusion.me_ref
  0.7 0.7 %copy-done.3 = f32[4,2048]{1,0:T(4,128)S(1)} copy-done((f32[4,2048]{1,0:T(4,128)S(1)}, f32[4,2048]{1,0:T(4,128)}, u32[]{:S(2)}) %copy-start.3) | copy-done | bytes 32792
  1.4 0.0 copy-start.4
  1.4 0.8 %copy-done.4 = f32[4,2048]{1,0:T(4,128)S(1)} copy-done((f32[4,2048]{1,0:T(4,128)S(1)}, f32[4,2048]{1,0:T(4,128)}, u32[]{:S(2)}) %copy-start.4) | copy-done | bytes 32792
  2.1 0.0 copy-start.5
  2.2 0.7 %copy-done.5 = s32[2048,1]{0,1:T(1,128)S(1)} copy-done((s32[2048,1]{0,1:T(1,128)S(1)}, s32[2048,1]{0,1:T(1,128)}, u32[]{:S(2)}) %copy-start.5) | copy-done | bytes 8216
  2.8 0.0 copy-start.6
  2.8 0.7 %copy-done.6 = s32[2048]{0:T(1024)S(1)} copy-done((s32[2048]{0:T(1024)S(1)}, s32[2048]{0:T(1024)}, u32[]{:S(2)}) %copy-start.6) | copy-done | bytes 8216
  3.5 0.0 copy-start.7
  3.5 0.7 %copy-done.7 = s32[2048]{0:T(1024)S(1)} copy-done((s32[2048]{0:T(1024)S(1)}, s32[2048]{0:T(1024)}, u32[]{:S(2)}) %copy-start.7) | copy-done | bytes 8216
  4.2 0.0 copy-start.8
  4.2 0.7 %copy-done.8 = f32[3,64]{1,0:T(4,128)S(1)} copy-done((f32[3,64]{1,0:T(4,128)S(1)}, f32[3,64]{1,0:T(4,128)}, u32[]{:S(2)}) %copy-start.8) | copy-done | bytes 792
  4.9 4.3 %place.1 = (bf16[4,32,128]{2,1,0:T(8,128)(2,1)S(1)}, bf16[4,32,128]{2,1,0:T(8,128)(2,1)S(1)}, bf16[4,32,128]{2,1,0:T(8,128)(2,1)S(1)}, bf16[4,32,128]{2,1,0:T(8,128)(2,1)S(1)}) custom-call(s32[2]{0:T(128)S(1)} %pad_add_fusion.me_ref, f32[4,2048]{1,0:T(4,128)S(1)} %copy-done.3, f32[4,2048]{1,0:T(4,128)S(1)} %copy-done.4, s32[1,2048]{1,0:T(1,128)S(1)} %bitcast.35, ...), custom_call_target="tpu_custom_call" | custom-call | tf_op jit(solution)/shard_map/place/pallas_call | solution.py:234
  9.2 0.5 collective-permute-start
  9.7 2.6 %collective-permute-start.1 = (bf16[4,32,128]{2,1,0:T(8,128)(2,1)S(1)}, bf16[4,32,128]{2,1,0:T(8,128)(2,1)S(1)}, u32[]{:S(2)}, u32[]{:S(2)}) collective-permute-start(bf16[4,32,128]{2,1,0:T(8,128)(2,1)S(1)} %get-tuple-element.20), channel_id=1, source_target_pairs={{0,2},{1,3},{2,0},{3,1},{4,6},{5,7},{6,4},{7,5},{8,10},{9,11},{10,... | collective-permute-start | bytes 98312 | tf_op jit(solution)/shard_map/ppermute | solution.py:211
  12.2 0.1 collective-permute-start.2
  12.3 0.8 %reshape.78 = bf16[48,4,64]{2,1,0:T(4,128)(2,1)S(1)} reshape(bf16[48,256]{1,0:T(8,128)(2,1)} %param.21) | data formatting | bytes 49152 | tf_op jit(solution)/shard_map/reshape | solution.py:245
  13.2 0.7 %pad.4.w_out_ref = bf16[8,16,128]{2,1,0:T(8,128)(2,1)S(1)} pad(bf16[8,4,128]{2,1,0:T(4,128)(2,1)} %param.19, bf16[]{:T(256)} %constant.20.clone.1), padding=0_0x8_4x0_0 | pad | bytes 40962 | tf_op jit(solution)/shard_map/jit(_pad)/pad | solution.py:246
  13.9 0.6 %gather_fusion = bf16[4,48,64]{2,1,0:T(8,128)(2,1)S(1)} fusion(bf16[4,48,64]{2,1,0:T(8,128)(2,1)S(1)} %bitcast.38, s32[1024]{0:T(1024)S(1)} %pad_clamp_fusion), kind=kCustom, calls=%fused_computation | custom fusion | bytes 49168 | tf_op jit(solution)/shard_map/gather | solution.py:245
  14.4 0.0 collective-permute-done
  14.5 0.0 collective-permute-done.1
  14.5 1.1 %collective-permute-done.2 = bf16[4,32,128]{2,1,0:T(8,128)(2,1)S(1)} collective-permute-done((bf16[4,32,128]{2,1,0:T(8,128)(2,1)S(1)}, bf16[4,32,128]{2,1,0:T(8,128)(2,1)S(1)}, u32[]{:S(2)}, u32[]{:S(2)}) %collective-permute-start.2) | collective-permute-done | bytes 32800 | tf_op jit(solution)/shard_map/ppermute | solution.py:211
  15.6 1.6 %collective-permute-start.3 = (bf16[2,16,512]{2,1,0:T(8,128)(2,1)S(1)}, bf16[2,16,512]{2,1,0:T(8,128)(2,1)S(1)}, u32[]{:S(2)}, u32[]{:S(2)}) collective-permute-start(bf16[2,16,512]{2,1,0:T(8,128)(2,1)S(1)} %pad_maximum_fusion.1), channel_id=1, source_target_pairs={{0,4},{4,0},{8,12},{12,8},{1,5},{5,1},{9,13},{13,9},{2,6},{6,2},{1... | collective-permute-start | bytes 98312 | tf_op jit(solution)/shard_map/ppermute | solution.py:211
  17.2 0.0 copy-start.2
  17.2 2.7 %collective-permute-start.4 = (bf16[2,16,512]{2,1,0:T(8,128)(2,1)S(1)}, bf16[2,16,512]{2,1,0:T(8,128)(2,1)S(1)}, u32[]{:S(2)}, u32[]{:S(2)}) collective-permute-start(bf16[2,16,512]{2,1,0:T(8,128)(2,1)S(1)} %pad_maximum_fusion.2), channel_id=1, source_target_pairs={{0,8},{4,12},{8,0},{12,4},{1,9},{5,13},{9,1},{13,5},{2,10},{6,14},... | collective-permute-start | bytes 98312 | tf_op jit(solution)/shard_map/ppermute | solution.py:211
  19.9 0.2 collective-permute-start.5
  20.1 0.0 collective-permute-done.3.refs_1_
  20.1 2.6 %collective-permute-done.4.refs_2_ = bf16[2,16,512]{2,1,0:T(8,128)(2,1)S(1)} collective-permute-done((bf16[2,16,512]{2,1,0:T(8,128)(2,1)S(1)}, bf16[2,16,512]{2,1,0:T(8,128)(2,1)S(1)}, u32[]{:S(2)}, u32[]{:S(2)}) %collective-permute-start.4) | collective-permute-done | bytes 32800 | tf_op jit(solution)/shard_map/ppermute | solution.py:211
  22.7 2.9 %collective-permute-done.5.refs_3_ = bf16[2,16,512]{2,1,0:T(8,128)(2,1)S(1)} collective-permute-done((bf16[2,16,512]{2,1,0:T(8,128)(2,1)S(1)}, bf16[2,16,512]{2,1,0:T(8,128)(2,1)S(1)}, u32[]{:S(2)}, u32[]{:S(2)}) %collective-permute-start.5) | collective-permute-done | bytes 32800 | tf_op jit(solution)/shard_map/ppermute | solution.py:211
  25.6 0.0 copy-done
  25.6 0.0 copy-done.2
  25.6 0.0 copy-start.1
  25.6 1.0 %copy-done.1 = bf16[8,256,128]{2,1,0:T(8,128)(2,1)S(1)} copy-done((bf16[8,256,128]{2,1,0:T(8,128)(2,1)S(1)}, bf16[8,256,128]{2,1,0:T(8,128)(2,1)}, u32[]{:S(2)}) %copy-start.1) | copy-done | bytes 524312
  26.7 5.0 %cell_net.2 = (bf16[576,128]{1,0:T(8,128)(2,1)S(1)}, f32[4,64,64]{2,1,0:T(8,128)S(1)}) custom-call(s32[2]{0:T(128)S(1)} %pad_add_fusion.me_ref, bf16[4,48,64]{2,1,0:T(8,128)(2,1)S(1)} %gather_fusion, bf16[8,128,256]{2,1,0:T(8,128)(2,1)S(1)} %copy-done, bf16[8,256,128]{2,1,0:T(8,128)(2,1)S(1)} %copy-done.1, bf16[8,48,128]{2,1,0:T(8,128)(2,1)S(1)} %copy-done.2, ...), custom_call_target="tpu_custom_call" | custom-call | tf_op jit(solution)/shard_map/cell_net/pallas_call | solution.py:274
  31.7 5.0 %cell_net.3 = (bf16[576,128]{1,0:T(8,128)(2,1)S(1)}, bf16[4,64,64]{2,1,0:T(8,128)(2,1)S(1)}) custom-call(s32[2]{0:T(128)S(1)} %pad_add_fusion.me_ref, bf16[4,48,64]{2,1,0:T(8,128)(2,1)S(1)} %gather_fusion, bf16[8,128,256]{2,1,0:T(8,128)(2,1)S(1)} %copy-done, bf16[8,256,128]{2,1,0:T(8,128)(2,1)S(1)} %copy-done.1, bf16[8,48,128]{2,1,0:T(8,128)(2,1)S(1)} %copy-done.2, ...), custom_call_target="tpu_custom_call" | custom-call | tf_op jit(solution)/shard_map/cell_net/pallas_call | solution.py:274
  36.7 0.1 collective-permute-start.12
  36.8 1.2 %collective-permute-start.14 = (bf16[64,64]{1,0:T(8,128)(2,1)S(1)}, bf16[64,64]{1,0:T(8,128)(2,1)S(1)}, u32[]{:S(2)}, u32[]{:S(2)}) collective-permute-start(bf16[64,64]{1,0:T(8,128)(2,1)S(1)} %get-tuple-element.31), channel_id=1, source_target_pairs={{0,12},{4,8},{8,4},{12,0},{1,13},{5,9},{9,5},{13,1},{2,14},{6,10},... | collective-permute-start | bytes 24584 | tf_op jit(solution)/shard_map/ppermute | solution.py:211
  38.0 2.3 %collective-permute-start.13 = (bf16[64,64]{1,0:T(8,128)(2,1)S(1)}, bf16[64,64]{1,0:T(8,128)(2,1)S(1)}, u32[]{:S(2)}, u32[]{:S(2)}) collective-permute-start(bf16[64,64]{1,0:T(8,128)(2,1)S(1)} %get-tuple-element.32), channel_id=1, source_target_pairs={{0,8},{4,12},{8,0},{12,4},{1,9},{5,13},{9,1},{13,5},{2,10},{6,14},... | collective-permute-start | bytes 24584 | tf_op jit(solution)/shard_map/ppermute | solution.py:211
  40.3 0.9 %collective-permute-start.9 = (bf16[576,128]{1,0:T(8,128)(2,1)S(1)}, bf16[576,128]{1,0:T(8,128)(2,1)S(1)}, u32[]{:S(2)}, u32[]{:S(2)}) collective-permute-start(bf16[576,128]{1,0:T(8,128)(2,1)S(1)} %get-tuple-element.24.refs_1_), channel_id=1, source_target_pairs={{0,2},{2,0},{1,3},{3,1},{4,6},{6,4},{5,7},{7,5},{8,10},{10,8},{9,1... | collective-permute-start | bytes 442376 | tf_op jit(solution)/shard_map/ppermute | solution.py:211
  41.2 1.1 %collective-permute-start.8 = (bf16[576,128]{1,0:T(8,128)(2,1)S(1)}, bf16[576,128]{1,0:T(8,128)(2,1)S(1)}, u32[]{:S(2)}, u32[]{:S(2)}) collective-permute-start(bf16[576,128]{1,0:T(8,128)(2,1)S(1)} %get-tuple-element.22.refs_0_), channel_id=1, source_target_pairs={{0,2},{2,0},{1,3},{3,1},{4,6},{6,4},{5,7},{7,5},{8,10},{10,8},{9,1... | collective-permute-start | bytes 442376 | tf_op jit(solution)/shard_map/ppermute | solution.py:211
  42.3 0.0 collective-permute-done.12
  42.3 0.1 collective-permute-done.14
  42.4 0.2 collective-permute-done.13
  42.7 0.1 collective-permute-start.17
  42.8 1.0 %collective-permute-start.16 = (bf16[64,64]{1,0:T(8,128)(2,1)S(1)}, bf16[64,64]{1,0:T(8,128)(2,1)S(1)}, u32[]{:S(2)}, u32[]{:S(2)}) collective-permute-start(bf16[64,64]{1,0:T(8,128)(2,1)S(1)} %fusion.2), channel_id=1, source_target_pairs={{0,2},{1,3},{2,0},{3,1},{4,6},{5,7},{6,4},{7,5},{8,10},{9,11},{10,... | collective-permute-start | bytes 24584 | tf_op jit(solution)/shard_map/ppermute | solution.py:211
  43.7 0.9 %collective-permute-start.15 = (bf16[64,64]{1,0:T(8,128)(2,1)S(1)}, bf16[64,64]{1,0:T(8,128)(2,1)S(1)}, u32[]{:S(2)}, u32[]{:S(2)}) collective-permute-start(bf16[64,64]{1,0:T(8,128)(2,1)S(1)} %fusion.2), channel_id=1, source_target_pairs={{0,1},{1,0},{2,3},{3,2},{4,5},{5,4},{6,7},{7,6},{8,9},{9,8},{10,11... | collective-permute-start | bytes 24584 | tf_op jit(solution)/shard_map/ppermute | solution.py:211
  44.6 1.5 %collective-permute-done.17 = bf16[64,64]{1,0:T(8,128)(2,1)S(1)} collective-permute-done((bf16[64,64]{1,0:T(8,128)(2,1)S(1)}, bf16[64,64]{1,0:T(8,128)(2,1)S(1)}, u32[]{:S(2)}, u32[]{:S(2)}) %collective-permute-start.17) | collective-permute-done | bytes 8224 | tf_op jit(solution)/shard_map/ppermute | solution.py:211
  46.1 1.3 %collective-permute-start.7 = (bf16[576,128]{1,0:T(8,128)(2,1)S(1)}, bf16[576,128]{1,0:T(8,128)(2,1)S(1)}, u32[]{:S(2)}, u32[]{:S(2)}) collective-permute-start(bf16[576,128]{1,0:T(8,128)(2,1)S(1)} %get-tuple-element.24.refs_1_), channel_id=1, source_target_pairs={{0,1},{1,0},{2,3},{3,2},{4,5},{5,4},{6,7},{7,6},{8,9},{9,8},{10,11... | collective-permute-start | bytes 442376 | tf_op jit(solution)/shard_map/ppermute | solution.py:211
  47.5 0.2 collective-permute-done.16
  47.7 0.0 collective-permute-start.6
  47.7 0.0 collective-permute-done.9.refs_5_
  47.7 0.5 collective-permute-start.11
  48.2 0.0 collective-permute-done.8.refs_4_
  48.2 0.1 collective-permute-start.10
  48.3 0.0 collective-permute-done.15
  48.3 0.6 %slice.102 = f32[3,64]{1,0:T(4,128)} slice(f32[64,64]{1,0:T(8,128)S(1)} %convert_add_fusion.1), slice={[48:51], [0:64]} | slice | bytes 1536 | tf_op jit(solution)/shard_map/slice | solution.py:325
  48.9 0.6 %slice.103 = f32[48,64]{1,0:T(8,128)} slice(f32[64,64]{1,0:T(8,128)S(1)} %convert_add_fusion.1), slice={[0:48], [0:64]} | slice | bytes 24576 | tf_op jit(solution)/shard_map/slice | solution.py:325
  49.5 0.0 collective-permute-done.7.refs_3_
  49.5 0.0 collective-permute-done.6.refs_2_
  49.5 0.0 collective-permute-done.11.refs_7_
  49.5 0.1 collective-permute-done.10.refs_6_
  49.6 2.1 %unpack.1 = (f32[8,128,256]{2,1,0:T(8,128)}, f32[8,256,128]{2,1,0:T(8,128)}, f32[8,48,128]{2,1,0:T(8,128)}, f32[8,4,128]{2,1,0:T(4,128)}) custom-call(s32[4]{0:T(128)S(1)} %xor_multiply_fusion.at_ref, bf16[576,128]{1,0:T(8,128)(2,1)S(1)} %get-tuple-element.22.refs_0_, bf16[576,128]{1,0:T(8,128)(2,1)S(1)} %get-tuple-element.24.refs_1_, ...), custom_call_target="tpu_custom_call" | custom-call | tf_op jit(solution)/shard_map/unpack/pallas_call | solution.py:307
  (15 shorter events, 0.1 us)
Async XLA Ops:
  0.6 0.8 %copy-start.3 = (f32[4,2048]{1,0:T(4,128)S(1)}, f32[4,2048]{1,0:T(4,128)}, u32[]{:S(2)}) copy-start(f32[4,2048]{1,0:T(4,128)} %points_ref.1) | copy-start | bytes 98308
  0.6 25.0 %copy-start = (bf16[8,128,256]{2,1,0:T(8,128)(2,1)S(1)}, bf16[8,128,256]{2,1,0:T(8,128)(2,1)}, u32[]{:S(2)}) copy-start(bf16[8,128,256]{2,1,0:T(8,128)(2,1)} %w_enc_ref.3) | copy-start | bytes 1572868
  1.4 0.8 %copy-start.4 = (f32[4,2048]{1,0:T(4,128)S(1)}, f32[4,2048]{1,0:T(4,128)}, u32[]{:S(2)}) copy-start(f32[4,2048]{1,0:T(4,128)} %cot_ref.1) | copy-start | bytes 98308
  2.1 0.7 %copy-start.5 = (s32[2048,1]{0,1:T(1,128)S(1)}, s32[2048,1]{0,1:T(1,128)}, u32[]{:S(2)}) copy-start(s32[2048,1]{0,1:T(1,128)} %param.13) | copy-start | bytes 24580
  2.8 0.7 %copy-start.6 = (s32[2048]{0:T(1024)S(1)}, s32[2048]{0:T(1024)}, u32[]{:S(2)}) copy-start(s32[2048]{0:T(1024)} %param.14) | copy-start | bytes 24580
  3.5 0.7 %copy-start.7 = (s32[2048]{0:T(1024)S(1)}, s32[2048]{0:T(1024)}, u32[]{:S(2)}) copy-start(s32[2048]{0:T(1024)} %param.15) | copy-start | bytes 24580
  4.2 0.7 %copy-start.8 = (f32[3,64]{1,0:T(4,128)S(1)}, f32[3,64]{1,0:T(4,128)}, u32[]{:S(2)}) copy-start(f32[3,64]{1,0:T(4,128)} %poses_ref.1) | copy-start | bytes 2308
  9.2 5.3 %collective-permute-start = (bf16[4,32,128]{2,1,0:T(8,128)(2,1)S(1)}, bf16[4,32,128]{2,1,0:T(8,128)(2,1)S(1)}, u32[]{:S(2)}, u32[]{:S(2)}) collective-permute-start(bf16[4,32,128]{2,1,0:T(8,128)(2,1)S(1)} %get-tuple-element.19), channel_id=1, source_target_pairs={{0,1},{1,0},{2,3},{3,2},{4,5},{5,4},{6,7},{7,6},{8,9},{9,8},{10,11... | collective-permute-start | bytes 98312 | tf_op jit(solution)/shard_map/ppermute | solution.py:211
  9.7 4.8 %collective-permute-start.1 = (bf16[4,32,128]{2,1,0:T(8,128)(2,1)S(1)}, bf16[4,32,128]{2,1,0:T(8,128)(2,1)S(1)}, u32[]{:S(2)}, u32[]{:S(2)}) collective-permute-start(bf16[4,32,128]{2,1,0:T(8,128)(2,1)S(1)} %get-tuple-element.20), channel_id=1, source_target_pairs={{0,2},{1,3},{2,0},{3,1},{4,6},{5,7},{6,4},{7,5},{8,10},{9,11},{10,... | collective-permute-start | bytes 98312 | tf_op jit(solution)/shard_map/ppermute | solution.py:211
  12.2 3.4 %collective-permute-start.2 = (bf16[4,32,128]{2,1,0:T(8,128)(2,1)S(1)}, bf16[4,32,128]{2,1,0:T(8,128)(2,1)S(1)}, u32[]{:S(2)}, u32[]{:S(2)}) collective-permute-start(bf16[4,32,128]{2,1,0:T(8,128)(2,1)S(1)} %get-tuple-element.21), channel_id=1, source_target_pairs={{0,3},{1,2},{2,1},{3,0},{4,7},{5,6},{6,5},{7,4},{8,11},{9,10},{10,... | collective-permute-start | bytes 98312 | tf_op jit(solution)/shard_map/ppermute | solution.py:211
  15.6 4.5 %collective-permute-start.3 = (bf16[2,16,512]{2,1,0:T(8,128)(2,1)S(1)}, bf16[2,16,512]{2,1,0:T(8,128)(2,1)S(1)}, u32[]{:S(2)}, u32[]{:S(2)}) collective-permute-start(bf16[2,16,512]{2,1,0:T(8,128)(2,1)S(1)} %pad_maximum_fusion.1), channel_id=1, source_target_pairs={{0,4},{4,0},{8,12},{12,8},{1,5},{5,1},{9,13},{13,9},{2,6},{6,2},{1... | collective-permute-start | bytes 98312 | tf_op jit(solution)/shard_map/ppermute | solution.py:211
  17.2 8.4 %copy-start.2 = (bf16[8,48,128]{2,1,0:T(8,128)(2,1)S(1)}, bf16[8,48,128]{2,1,0:T(8,128)(2,1)}, u32[]{:S(2)}) copy-start(bf16[8,48,128]{2,1,0:T(8,128)(2,1)} %w_code_ref.3) | copy-start | bytes 294916
  17.2 5.5 %collective-permute-start.4 = (bf16[2,16,512]{2,1,0:T(8,128)(2,1)S(1)}, bf16[2,16,512]{2,1,0:T(8,128)(2,1)S(1)}, u32[]{:S(2)}, u32[]{:S(2)}) collective-permute-start(bf16[2,16,512]{2,1,0:T(8,128)(2,1)S(1)} %pad_maximum_fusion.2), channel_id=1, source_target_pairs={{0,8},{4,12},{8,0},{12,4},{1,9},{5,13},{9,1},{13,5},{2,10},{6,14},... | collective-permute-start | bytes 98312 | tf_op jit(solution)/shard_map/ppermute | solution.py:211
  19.9 5.7 %collective-permute-start.5 = (bf16[2,16,512]{2,1,0:T(8,128)(2,1)S(1)}, bf16[2,16,512]{2,1,0:T(8,128)(2,1)S(1)}, u32[]{:S(2)}, u32[]{:S(2)}) collective-permute-start(bf16[2,16,512]{2,1,0:T(8,128)(2,1)S(1)} %pad_maximum_fusion.3), channel_id=1, source_target_pairs={{0,12},{4,8},{8,4},{12,0},{1,13},{5,9},{9,5},{13,1},{2,14},{6,10},... | collective-permute-start | bytes 98312 | tf_op jit(solution)/shard_map/ppermute | solution.py:211
  25.6 1.0 %copy-start.1 = (bf16[8,256,128]{2,1,0:T(8,128)(2,1)S(1)}, bf16[8,256,128]{2,1,0:T(8,128)(2,1)}, u32[]{:S(2)}) copy-start(bf16[8,256,128]{2,1,0:T(8,128)(2,1)} %w_hidden_ref.3) | copy-start | bytes 1572868
  36.7 5.6 %collective-permute-start.12 = (bf16[64,64]{1,0:T(8,128)(2,1)S(1)}, bf16[64,64]{1,0:T(8,128)(2,1)S(1)}, u32[]{:S(2)}, u32[]{:S(2)}) collective-permute-start(bf16[64,64]{1,0:T(8,128)(2,1)S(1)} %get-tuple-element.30), channel_id=1, source_target_pairs={{0,4},{4,0},{8,12},{12,8},{1,5},{5,1},{9,13},{13,9},{2,6},{6,2},{1... | collective-permute-start | bytes 24584 | tf_op jit(solution)/shard_map/ppermute | solution.py:211
  36.8 5.6 %collective-permute-start.14 = (bf16[64,64]{1,0:T(8,128)(2,1)S(1)}, bf16[64,64]{1,0:T(8,128)(2,1)S(1)}, u32[]{:S(2)}, u32[]{:S(2)}) collective-permute-start(bf16[64,64]{1,0:T(8,128)(2,1)S(1)} %get-tuple-element.31), channel_id=1, source_target_pairs={{0,12},{4,8},{8,4},{12,0},{1,13},{5,9},{9,5},{13,1},{2,14},{6,10},... | collective-permute-start | bytes 24584 | tf_op jit(solution)/shard_map/ppermute | solution.py:211
  38.0 4.6 %collective-permute-start.13 = (bf16[64,64]{1,0:T(8,128)(2,1)S(1)}, bf16[64,64]{1,0:T(8,128)(2,1)S(1)}, u32[]{:S(2)}, u32[]{:S(2)}) collective-permute-start(bf16[64,64]{1,0:T(8,128)(2,1)S(1)} %get-tuple-element.32), channel_id=1, source_target_pairs={{0,8},{4,12},{8,0},{12,4},{1,9},{5,13},{9,1},{13,5},{2,10},{6,14},... | collective-permute-start | bytes 24584 | tf_op jit(solution)/shard_map/ppermute | solution.py:211
  40.3 7.4 %collective-permute-start.9 = (bf16[576,128]{1,0:T(8,128)(2,1)S(1)}, bf16[576,128]{1,0:T(8,128)(2,1)S(1)}, u32[]{:S(2)}, u32[]{:S(2)}) collective-permute-start(bf16[576,128]{1,0:T(8,128)(2,1)S(1)} %get-tuple-element.24.refs_1_), channel_id=1, source_target_pairs={{0,2},{2,0},{1,3},{3,1},{4,6},{6,4},{5,7},{7,5},{8,10},{10,8},{9,1... | collective-permute-start | bytes 442376 | tf_op jit(solution)/shard_map/ppermute | solution.py:211
  41.2 7.0 %collective-permute-start.8 = (bf16[576,128]{1,0:T(8,128)(2,1)S(1)}, bf16[576,128]{1,0:T(8,128)(2,1)S(1)}, u32[]{:S(2)}, u32[]{:S(2)}) collective-permute-start(bf16[576,128]{1,0:T(8,128)(2,1)S(1)} %get-tuple-element.22.refs_0_), channel_id=1, source_target_pairs={{0,2},{2,0},{1,3},{3,1},{4,6},{6,4},{5,7},{7,5},{8,10},{10,8},{9,1... | collective-permute-start | bytes 442376 | tf_op jit(solution)/shard_map/ppermute | solution.py:211
  42.7 3.5 %collective-permute-start.17 = (bf16[64,64]{1,0:T(8,128)(2,1)S(1)}, bf16[64,64]{1,0:T(8,128)(2,1)S(1)}, u32[]{:S(2)}, u32[]{:S(2)}) collective-permute-start(bf16[64,64]{1,0:T(8,128)(2,1)S(1)} %fusion.2), channel_id=1, source_target_pairs={{0,3},{1,2},{2,1},{3,0},{4,7},{5,6},{6,5},{7,4},{8,11},{9,10},{10,... | collective-permute-start | bytes 24584 | tf_op jit(solution)/shard_map/ppermute | solution.py:211
  42.8 5.0 %collective-permute-start.16 = (bf16[64,64]{1,0:T(8,128)(2,1)S(1)}, bf16[64,64]{1,0:T(8,128)(2,1)S(1)}, u32[]{:S(2)}, u32[]{:S(2)}) collective-permute-start(bf16[64,64]{1,0:T(8,128)(2,1)S(1)} %fusion.2), channel_id=1, source_target_pairs={{0,2},{1,3},{2,0},{3,1},{4,6},{5,7},{6,4},{7,5},{8,10},{9,11},{10,... | collective-permute-start | bytes 24584 | tf_op jit(solution)/shard_map/ppermute | solution.py:211
  43.7 4.6 %collective-permute-start.15 = (bf16[64,64]{1,0:T(8,128)(2,1)S(1)}, bf16[64,64]{1,0:T(8,128)(2,1)S(1)}, u32[]{:S(2)}, u32[]{:S(2)}) collective-permute-start(bf16[64,64]{1,0:T(8,128)(2,1)S(1)} %fusion.2), channel_id=1, source_target_pairs={{0,1},{1,0},{2,3},{3,2},{4,5},{5,4},{6,7},{7,6},{8,9},{9,8},{10,11... | collective-permute-start | bytes 24584 | tf_op jit(solution)/shard_map/ppermute | solution.py:211
  46.1 3.4 %collective-permute-start.7 = (bf16[576,128]{1,0:T(8,128)(2,1)S(1)}, bf16[576,128]{1,0:T(8,128)(2,1)S(1)}, u32[]{:S(2)}, u32[]{:S(2)}) collective-permute-start(bf16[576,128]{1,0:T(8,128)(2,1)S(1)} %get-tuple-element.24.refs_1_), channel_id=1, source_target_pairs={{0,1},{1,0},{2,3},{3,2},{4,5},{5,4},{6,7},{7,6},{8,9},{9,8},{10,11... | collective-permute-start | bytes 442376 | tf_op jit(solution)/shard_map/ppermute | solution.py:211
  47.7 1.8 %collective-permute-start.6 = (bf16[576,128]{1,0:T(8,128)(2,1)S(1)}, bf16[576,128]{1,0:T(8,128)(2,1)S(1)}, u32[]{:S(2)}, u32[]{:S(2)}) collective-permute-start(bf16[576,128]{1,0:T(8,128)(2,1)S(1)} %get-tuple-element.22.refs_0_), channel_id=1, source_target_pairs={{0,1},{1,0},{2,3},{3,2},{4,5},{5,4},{6,7},{7,6},{8,9},{9,8},{10,11... | collective-permute-start | bytes 442376 | tf_op jit(solution)/shard_map/ppermute | solution.py:211
  47.7 1.8 %collective-permute-start.11 = (bf16[576,128]{1,0:T(8,128)(2,1)S(1)}, bf16[576,128]{1,0:T(8,128)(2,1)S(1)}, u32[]{:S(2)}, u32[]{:S(2)}) collective-permute-start(bf16[576,128]{1,0:T(8,128)(2,1)S(1)} %collective-permute-done.9.refs_5_), channel_id=1, source_target_pairs={{0,1},{1,0},{2,3},{3,2},{4,5},{5,4},{6,7},{7,6},{8,9},{9,8},{10,11... | collective-permute-start | bytes 442376 | tf_op jit(solution)/shard_map/ppermute | solution.py:211
  48.2 1.4 %collective-permute-start.10 = (bf16[576,128]{1,0:T(8,128)(2,1)S(1)}, bf16[576,128]{1,0:T(8,128)(2,1)S(1)}, u32[]{:S(2)}, u32[]{:S(2)}) collective-permute-start(bf16[576,128]{1,0:T(8,128)(2,1)S(1)} %collective-permute-done.8.refs_4_), channel_id=1, source_target_pairs={{0,1},{1,0},{2,3},{3,2},{4,5},{5,4},{6,7},{7,6},{8,9},{9,8},{10,11... | collective-permute-start | bytes 442376 | tf_op jit(solution)/shard_map/ppermute | solution.py:211

commit v2 on v1

v2 whole, which is shorter than its diff:
```python
import functools

import jax
import jax.numpy as jnp
from jax import lax
from jax.experimental import pallas as pl
from jax.experimental.pallas import tpu as pltpu
from jax.sharding import PartitionSpec as P

BF16 = jnp.bfloat16
F32 = jnp.float32
VMEM_BYTES = 32 * 1024 * 1024
ALL_VMEM_BYTES = 64 * 1024 * 1024
SLACK_BYTES = 128 * 1024
PART_AXES = ("rep", "sub")
RECORD = 16
TANGENT_ROW = 8
CAMERA_ROW = 12


def dot_nn(a, b):
    return lax.dot_general(a, b, (((1,), (0,)), ((), ())), preferred_element_type=F32)


def dot_nt(a, b):
    return lax.dot_general(a, b, (((1,), (1,)), ((), ())), preferred_element_type=F32)


def dot_tn(a, b):
    return lax.dot_general(a, b, (((0,), (0,)), ((), ())), preferred_element_type=F32)


def iota(shape, dim):
    return lax.broadcasted_iota(jnp.int32, shape, dim)


def me():
    return lax.axis_index("cell"), lax.axis_index(PART_AXES)


def place_kernel(cells_all, cap, n_cell, n_part, *refs):
    sources, weights, outs, own = refs[:6], refs[6:9], refs[9:9 + n_part], refs[9 + n_part:12 + n_part]
    arrays, (spread, placed, sems) = refs[12 + n_part:18 + n_part], refs[18 + n_part:]
    points_ref, cot_ref, cell_ref, cam_ref, valid_ref, poses_ref = arrays
    me_cell, me_part = me()
    lc = cells_all // (n_cell * n_part)
    pairs = list(zip(sources, arrays)) + [
        (source.at[pl.ds(me_part * lc, lc)], target) for source, target in zip(weights, own)
    ]
    copies = [pltpu.make_async_copy(source, target, sems.at[i]) for i, (source, target) in enumerate(pairs)]
    for copy in copies:
        copy.start()
    for copy in copies[:6]:
        copy.wait()
    n = points_ref.shape[1]
    cams = poses_ref.shape[1]
    cam = cam_ref[...]
    cam_hot = (iota((cams, n), 0) == cam).astype(F32).astype(BF16)
    poses = poses_ref[...]
    high = poses.astype(BF16).astype(F32)
    middle = (poses - high).astype(BF16).astype(F32)
    parts = jnp.concatenate([high, middle, poses - high - middle], axis=0).astype(BF16)
    moved = dot_nn(parts, cam_hot)
    offsets = (moved[0:3] + moved[3:6]) + moved[6:9]
    points = points_ref[...]
    coords = jnp.concatenate([points[0:3] + offsets, points[3:4]], axis=0)
    coords_high = coords.astype(BF16).astype(F32)
    tangent = cot_ref[...] * valid_ref[...].astype(F32)
    record = jnp.concatenate(
        [coords_high, coords - coords_high, tangent, cam.astype(F32), jnp.zeros((3, n), F32)], axis=0
    )
    width = min(256, n)
    blocks = n // width
    upper = (iota((width, width), 0) <= iota((width, width), 1)).astype(F32).astype(BF16)
    cell_of = cell_ref[...]
    hots = [
        (iota((cells_all, width), 0) == cell_of[:, b * width:(b + 1) * width]).astype(F32)
        for b in range(blocks)
    ]
    counts = dot_nn(jnp.concatenate(hots, axis=0).astype(BF16), upper)
    carry = jnp.zeros((cells_all, 1), F32)
    ranks = []
    for b in range(blocks):
        counted = counts[b * cells_all:(b + 1) * cells_all]
        ranks.append(jnp.sum((counted + carry) * hots[b], axis=0, keepdims=True) - 1.0)
        carry = carry + counted[:, width - 1:width]
    rank = jnp.concatenate(ranks, axis=1).astype(jnp.int32)
    rank_hot = (iota((cap, n), 0) == rank).astype(F32).astype(BF16)
    cell_rows = jnp.broadcast_to(cell_of, (RECORD, n))
    for c in range(cells_all):
        spread[c * RECORD:(c + 1) * RECORD, :] = jnp.where(cell_rows == c, record, 0.0).astype(BF16)
    placed[...] = dot_nt(spread[...], rank_hot).astype(BF16)
    rows = lc * RECORD
    for kp in range(n_part):
        for kc in range(n_cell):
            owner = (me_cell ^ kc) * n_part + (me_part ^ kp)
            start = pl.multiple_of(owner * rows, rows)
            outs[kp][kc] = placed[pl.ds(start, rows), :]
    for copy in copies[6:]:
        copy.wait()


def sin_cos(x):
    n = jnp.floor(x * 0.6366197723675814 + 0.5)
    r = ((x - n * 1.5703125) - n * 4.837512969970703125e-4) - n * 7.54978995489188216e-8
    z = r * r
    s = r + (r * z) * (-1.6666654611e-1 + z * (8.3321608736e-3 + z * -1.9515295891e-4))
    c = (1.0 - 0.5 * z) + (z * z) * (
        4.166664568298827e-2 + z * (-1.388731625493765e-3 + z * 2.443315711809948e-5))
    q = n.astype(jnp.int32)
    swap = (q & 1) == 1
    sine = jnp.where(swap, c, s)
    cosine = jnp.where(swap, s, c)
    sine = jnp.where((q & 2) == 2, -sine, sine)
    cosine = jnp.where(((q + 1) & 2) == 2, -cosine, cosine)
    return sine, cosine


def double_angle(s, c):
    return 2.0 * s * c, 1.0 - 2.0 * s * s


def soft(x):
    e = jnp.exp(-jnp.abs(x))
    u = 1.0 + e
    plus = jnp.maximum(x, 0.0) + jnp.where(e < 1e-4, e, jnp.log(u))
    r = pl.reciprocal(u, approx=True)
    return plus, jnp.where(x >= 0.0, r, e * r)


def backward_samples(n_cell, freq_count, codes_ref, w_out, weights, arrived, table_in, table_ref, kept, j):
    enc_s, gt_s, trunk_s, gc_s, act_s, rec_s = kept
    w_enc, w_hidden, w_code = weights
    width = arrived[0].shape[2]
    cams = codes_ref.shape[2]
    hidden = w_hidden.shape[0]
    half = freq_count // 2
    scale = jnp.exp2(iota((half, 1), 0).astype(F32) * 0.25)
    top = 2.0 ** (half // 4)
    for kc in range(n_cell):
        cols = slice(kc * width, (kc + 1) * width)
        rec = arrived[kc][j]
        rec_s[:, cols] = rec
        recf = rec.astype(F32)
        coords = recf[0:4] + recf[4:8]
        cam = recf[CAMERA_ROW:CAMERA_ROW + 1].astype(jnp.int32)
        cam_hot = (iota((cams, width), 0) == cam).astype(F32).astype(BF16)
        code_rows = dot_nn(codes_ref[kc], cam_hot).astype(BF16)
        angles = jnp.concatenate([coords[i:i + 1] * scale for i in range(4)], axis=0)
        s1, c1 = sin_cos(angles)
        s2, c2 = s1, c1
        for _ in range(half // 4):
            s2, c2 = double_angle(s2, c2)
        pieces = []
        for a, b in ((s1, s2), (c1, c2)):
            for i in range(4):
                pieces += [a[i * half:(i + 1) * half], b[i * half:(i + 1) * half]]
        encoded = jnp.concatenate(pieces, axis=0).astype(BF16)
        enc_s[:, cols] = encoded
        trunk, slope_trunk = soft(dot_tn(w_enc, encoded))
        trunk = trunk.astype(BF16)
        trunk_s[0:hidden, cols] = trunk
        trunk_s[hidden:, cols] = code_rows
        act, slope_color = soft(dot_tn(w_hidden, trunk) + dot_tn(w_code, code_rows))
        act_s[:, cols] = act.astype(BF16)
        gc = (dot_tn(w_out, rec) * slope_color).astype(BF16)
        gc_s[:, cols] = gc
        gt = (dot_nn(w_hidden, gc) * slope_trunk).astype(BF16)
        gt_s[:, cols] = gt
        grad_code = dot_nn(w_code, gc)
        grad_enc = dot_nn(w_enc, gt)
        sums = []
        for i in range(3):
            a, b = i * 2 * half, (4 + i) * 2 * half
            at = slice(i * half, (i + 1) * half)
            first = grad_enc[a:a + half] * c1[at] - grad_enc[b:b + half] * s1[at]
            second = (grad_enc[a + half:a + 2 * half] * c2[at]
                      - grad_enc[b + half:b + 2 * half] * s2[at])
            sums.append(jnp.sum((first + top * second) * scale, axis=0, keepdims=True))
        row = iota((RECORD, width), 0)
        tail = jnp.where(row == 0, sums[0], jnp.where(row == 1, sums[1], jnp.where(row == 2, sums[2], 0.0)))
        per_sample = jnp.concatenate([grad_code, tail], axis=0).astype(BF16)
        table = dot_nt(per_sample, cam_hot)
        if table_in is not None:
            table = table + table_in[kc]
        table_ref[kc] = table.astype(table_ref.dtype)


def sum_weights(kept, packed_ref):
    enc_s, gt_s, trunk_s, gc_s, act_s, rec_s = kept
    color = gc_s.shape[0]
    g_enc = dot_nt(enc_s[...], gt_s[...]).astype(BF16)
    enc_rows = g_enc.shape[0]
    row = 0
    for part in range(g_enc.shape[1] // color):
        packed_ref[row:row + enc_rows, :] = g_enc[:, part * color:(part + 1) * color]
        row += enc_rows
    rows = trunk_s.shape[0]
    packed_ref[row:row + rows, :] = dot_nt(trunk_s[...], gc_s[...]).astype(BF16)
    row += rows
    packed_ref[row:row + RECORD, :] = dot_nt(rec_s[...], act_s[...]).astype(BF16)


def cells_kernel(n_cell, freq_count, lc, codes_ref, w_out_ref, *refs):
    weights, arrived, refs = refs[:3], refs[3:3 + n_cell], refs[3 + n_cell:]
    packed_ref, table_ref, kept, sums = refs[0], refs[1], refs[2:8], refs[8]
    rows = packed_ref.shape[0] // lc
    me_part = lax.axis_index(PART_AXES)
    for j in range(lc):
        backward_samples(n_cell, freq_count, codes_ref, w_out_ref[me_part * lc + j], [w[j] for w in weights],
                         arrived, sums if j else None, table_ref if j == lc - 1 else sums,
                         [k.at[j] for k in kept], j)
        sum_weights([k.at[j] for k in kept], packed_ref.at[j * rows:(j + 1) * rows])


def shard_sum_kernel(count, *refs):
    total = refs[0][0].astype(F32)
    for k in range(1, count):
        total = total + refs[k][...].astype(F32)
    refs[count][...] = total.astype(BF16)


def relay_kernel(n_rep, *refs):
    parts, packed_ref, out_ref = refs[:n_rep], refs[n_rep], refs[n_rep + 1]
    total = sum(part[...].astype(F32) for part in parts)
    rows, cams = total.shape
    out_ref[0:packed_ref.shape[0], :] = packed_ref[...]
    total = jnp.concatenate([total, jnp.zeros((rows, out_ref.shape[1] - cams), F32)], axis=1)
    out_ref[packed_ref.shape[0]:, :] = total.astype(BF16)


def unpack_kernel(places, lc, n_prev, packed_rows, tables_at, *refs):
    ins, refs = refs[:len(places)], refs[len(places):]
    if tables_at:
        here, refs = refs[0], refs[1:]
    outs, refs = refs[n_prev:n_prev + 4], refs[n_prev + 4:]
    code = outs[2].shape[1]
    if tables_at:
        cams = refs[0].shape[1]
        first = lc * packed_rows
        total = here[first:, :].astype(F32)
        for i in tables_at:
            total = total + ins[i][first:, :].astype(F32)
        refs[0][...] = total[code:code + 3, 0:cams]
        refs[1][...] = total[0:code, 0:cams]
        refs = refs[2:]
    wide, sems = refs[:-1], refs[-1]
    enc_v, hidden_v, code_v, out_v = wide
    enc_rows, enc_cols = enc_v.shape[1:]
    hidden, color = hidden_v.shape[1:]
    out_rows = out_v.shape[1]
    me_part = lax.axis_index(PART_AXES)
    copies = []
    for i in range(len(places) * lc):
        cell = (me_part ^ places[i // lc]) * lc + i % lc
        src = ins[i // lc]
        row = i % lc * packed_rows
        for part in range(enc_cols // color):
            enc_v[i, :, part * color:(part + 1) * color] = src[row:row + enc_rows, :].astype(F32)
            row += enc_rows
        hidden_v[i] = src[row:row + hidden, :].astype(F32)
        row += hidden
        code_v[i] = src[row:row + code, :].astype(F32)
        row += code
        out_v[i] = src[row:row + RECORD, :].astype(F32)[TANGENT_ROW:TANGENT_ROW + out_rows]
        for m in range(4):
            copy = pltpu.make_async_copy(wide[m].at[i], outs[m].at[cell], sems.at[i, m])
            copy.start()
            copies.append(copy)
    for copy in copies:
        copy.wait()


def cost(us):
    return pl.CostEstimate(flops=us * 10 ** 9, bytes_accessed=us * 3 * 10 ** 6, transcendentals=0)


def exchange(value, axes, count, k):
    if k == 0:
        return value
    return lax.ppermute(value, axes, [(i, i ^ k) for i in range(count)])


def shards(points, cotangent, cell_ids, camera_ids, valid, w_enc, w_hidden, w_code, w_out, poses, codes):
    n_cell, n_rep, n_sub = lax.axis_size("cell"), lax.axis_size("rep"), lax.axis_size("sub")
    n_part = n_rep * n_sub
    local = w_enc.shape[0]
    lc = local // n_part
    cells_all = local * n_cell
    n = points.shape[1]
    cap = max(2, 2 * n // cells_all)
    enc, hidden = w_enc.shape[1:]
    color = w_hidden.shape[2]
    freq_count = enc // 8
    cams = poses.shape[1]
    code = codes.shape[0]
    width = n_part * cap
    params = pltpu.CompilerParams(vmem_limit_bytes=VMEM_BYTES)
    vmem = pl.BlockSpec(memory_space=pltpu.VMEM)
    hbm = pl.BlockSpec(memory_space=pltpu.HBM)

    inputs = (points, cotangent, cell_ids.reshape(1, n), camera_ids.reshape(1, n), valid.reshape(1, n), poses)
    weights = (w_enc, w_hidden, w_code)
    out_shape = [jax.ShapeDtypeStruct((n_cell, lc * RECORD, cap), BF16)] * n_part + [
        jax.ShapeDtypeStruct((lc,) + w.shape[1:], BF16) for w in weights
    ]
    room = sum(2 * a.size // a.shape[-1] * max(a.shape[-1], 128) for a in out_shape) + SLACK_BYTES
    placed = pl.pallas_call(
        functools.partial(place_kernel, cells_all, cap, n_cell, n_part),
        out_shape=out_shape,
        in_specs=[hbm] * 9,
        out_specs=[vmem] * len(out_shape),
        scratch_shapes=[pltpu.VMEM(a.shape, a.dtype) for a in inputs] + [
            pltpu.VMEM((cells_all * RECORD, n), BF16),
            pltpu.VMEM((cells_all * RECORD, cap), BF16),
            pltpu.SemaphoreType.DMA((9,)),
        ],
        compiler_params=pltpu.CompilerParams(vmem_limit_bytes=ALL_VMEM_BYTES - room),
        cost_estimate=cost(3),
        name="place",
    )(*inputs, *weights)
    sent, own_weights = placed[:n_part], placed[n_part:]

    order = lax.axis_index("cell") ^ jnp.arange(n_cell, dtype=jnp.int32)
    codes_rel = codes.reshape(code, n_cell, cams).transpose(1, 0, 2)[order]
    w_out_rows = jnp.pad(w_out, ((0, 0), (TANGENT_ROW, RECORD - TANGENT_ROW - w_out.shape[1]), (0, 0)))

    near = [exchange(sent[kp], PART_AXES, n_part, kp) for kp in range(n_part)]
    arrived = []
    for kc in range(n_cell):
        lanes = jnp.concatenate([near[kp][kc] for kp in range(n_part)], axis=-1)
        arrived.append(exchange(lanes.reshape(lc, RECORD, width), "cell", n_cell, kc))

    packed_rows = enc * (hidden // color) + hidden + code + RECORD
    slots = n_cell * width
    kept_rows = (enc, hidden, hidden + code, color, color, RECORD)
    table_shape = (n_cell, code + RECORD, cams)
    packed, table = pl.pallas_call(
        functools.partial(cells_kernel, n_cell, freq_count, lc),
        in_specs=[vmem] * (5 + n_cell),
        out_specs=[vmem, vmem],
        out_shape=[
            jax.ShapeDtypeStruct((lc * packed_rows, color), BF16),
            jax.ShapeDtypeStruct(table_shape, BF16),
        ],
        scratch_shapes=[pltpu.VMEM((lc, r, slots), BF16) for r in kept_rows] + [pltpu.VMEM(table_shape, F32)],
        compiler_params=params,
        cost_estimate=cost(10),
        name="cells",
    )(codes_rel, w_out_rows, *own_weights, *arrived)

    over_rep = [exchange(packed, "rep", n_rep, kr) for kr in range(n_rep)]
    tables = [table] + [exchange(table[kc], "cell", n_cell, kc) for kc in range(1, n_cell)]
    mine = pl.pallas_call(
        functools.partial(shard_sum_kernel, n_cell),
        in_specs=[vmem] * n_cell,
        out_specs=vmem,
        out_shape=jax.ShapeDtypeStruct(table_shape[1:], BF16),
        compiler_params=params,
        cost_estimate=cost(0),
        name="shard_sum",
    )(*tables)
    parts = [exchange(mine, "rep", n_rep, kr) for kr in range(n_rep)]
    relayed = pl.pallas_call(
        functools.partial(relay_kernel, n_rep),
        in_specs=[vmem] * (n_rep + 1),
        out_specs=vmem,
        out_shape=jax.ShapeDtypeStruct((lc * packed_rows + table_shape[1], color), BF16),
        compiler_params=params,
        cost_estimate=cost(0),
        name="relay",
    )(*parts, over_rep[1])

    early, late = [], []
    for kr in range(n_rep):
        for ks in range(n_sub):
            sent_on = relayed if kr == 1 and ks else over_rep[kr]
            (late if kr and ks else early).append((kr * n_sub + ks, exchange(sent_on, "sub", n_sub, ks)))
    shapes = [
        jax.ShapeDtypeStruct((local, enc, hidden), F32),
        jax.ShapeDtypeStruct((local, hidden, color), F32),
        jax.ShapeDtypeStruct((local, code, color), F32),
        jax.ShapeDtypeStruct((local, w_out.shape[1], color), F32),
    ]
    grads = []
    for group in (early, late):
        tables_at, sums_shape, here = (), [], []
        if group is late:
            tables_at = tuple(i for i, (place, _) in enumerate(group) if place // n_sub == 1)
            sums_shape = [jax.ShapeDtypeStruct((rows, cams), F32) for rows in (3, code)]
            here = [relayed]
        grads = pl.pallas_call(
            functools.partial(
                unpack_kernel, tuple(place for place, _ in group), lc, len(grads), packed_rows, tables_at
            ),
            out_shape=shapes + sums_shape,
            in_specs=[vmem] * (len(group) + len(here)) + [hbm] * len(grads),
            out_specs=[hbm] * 4 + [vmem] * len(sums_shape),
            scratch_shapes=[pltpu.VMEM((len(group) * lc,) + a.shape[1:], F32) for a in shapes]
            + [pltpu.SemaphoreType.DMA((len(group) * lc, 4))],
            input_output_aliases={len(group) + len(here) + i: i for i in range(len(grads))},
            compiler_params=params,
            cost_estimate=cost(0),
            name="unpack",
        )(*[value for _, value in group], *here, *grads)
    return tuple(grads)


def solution(mesh):
    samples = ("groups", "cell", "rep", "sub")
    in_specs = (
        P(None, samples),
        P(None, samples),
        P(samples, None),
        P(samples),
        P(samples),
        P("cell", None, None),
        P("cell", None, None),
        P("cell", None, None),
        P("cell", None, None),
        P(None, "cell"),
        P(),
    )
    out_specs = (
        P(("groups", "cell"), None, None),
        P(("groups", "cell"), None, None),
        P(("groups", "cell"), None, None),
        P(("groups", "cell"), None, None),
        P(None, ("groups", "cell")),
        P(None, ("groups", "cell")),
    )
    return jax.shard_map(shards, mesh=mesh, in_specs=in_specs, out_specs=out_specs, check_vma=False)
```

time: 52.1 us -> 44.7 us (0.86)
  local copies, waits for them, and re-layouts: 8.56 us -> 2.15 us
  waiting for transfers between devices: 8.77 us -> 12.6 us
  starting transfers between devices: 17 us -> 14.7 us
  Pallas kernels: 16.4 us -> 14.1 us
    unnamed x18 -> x10, local copies, waits for them, and re-layouts: 5.24 us -> 0.69 us
    ppermute x18 -> x13, waiting for transfers between devices: 8.77 us -> 12.6 us  [exchange(): return lax.ppermute(value, axes, [(i, i ^ k) for i in range(count)])]
    ppermute x18 -> x13, starting transfers between devices: 17 us -> 14.7 us  [exchange(): return lax.ppermute(value, axes, [(i, i ^ k) for i in range(count)])]
    pallas_call x1, Pallas kernels: 4.26 us -> 2.67 us  [shards(): pl.pallas_call(functools.partial(place_kernel, cells_all, cap, n_cell, n_...]
    slice x2 -> x0, local copies, waits for them, and re-layouts: 1.19 us -> none  [shards(): return (*grads, total[code:code + 3], total[0:code])]
    slice x4, local copies, waits for them, and re-layouts: 0.02 us -> 0.78 us  [shards(): lanes = jnp.concatenate([near[kp][kc] for kp in range(n_part)], axis=-1)]
    reshape x2, local copies, waits for them, and re-layouts: 0.84 us -> 0.11 us  [shards(): codes_rel = codes.reshape(code, n_cell, cams).transpose(1, 0, 2)[order]]
    pad x1, local copies, waits for them, and re-layouts: 0.71 us -> 0.01 us  [shards(): jnp.pad(w_out, ((0, 0), (TANGENT_ROW, RECORD - TANGENT_ROW - w_out.shape[...]
  transfers between devices with their start and end apart: 18 -> 13, of which waited for: 8 -> 7; matrix products, arithmetic and copies ran while one was open for 7% -> 3% of each run, Pallas kernels for 0% -> 3%
where the time goes in v2:
time: 44.7 us; the launch traced here: 44.4 us
  starting transfers between devices  14.7 us (33%)
  Pallas kernels  14.1 us (32%)
  waiting for transfers between devices  12.6 us (28%)
  local copies, waits for them, and re-layouts  2.15 us (5%)
  between operations  0.78 us (2%)
    ppermute x13, starting transfers between devices, exchange(): return lax.ppermute(value, axes, [(i, i ^ k) for i in range(count)])  14.7 us
    ppermute x13, waiting for transfers between devices, exchange(): return lax.ppermute(value, axes, [(i, i ^ k) for i in range(count)])  12.6 us
    pallas_call x1, Pallas kernels, shards(): pl.pallas_call(functools.partial(cells_kernel, n_cell, freq_count, lc), i...  8.5 us
    pallas_call x2, Pallas kernels, shards(): pl.pallas_call(functools.partial(unpack_kernel, tuple((place for place, _...  2.92 us
    pallas_call x1, Pallas kernels, shards(): pl.pallas_call(functools.partial(place_kernel, cells_all, cap, n_cell, n_...  2.67 us
  transfers between devices with their start and end apart: 13, of which 7 were waited for; matrix products, arithmetic and copies ran while one was open for 3% of the time, Pallas kernels for 3%

profile of v2, /device:TPU:0, one launch (start us, length us, event | category | flops | bytes accessed | tf_op | source)
XLA Modules:
  0.0 44.4 jit_solution(3704014751375334501)
XLA Ops:
  0.6 2.7 %place.1 = (bf16[4,32,128]{2,1,0:T(8,128)(2,1)}, bf16[4,32,128]{2,1,0:T(8,128)(2,1)}, bf16[4,32,128]{2,1,0:T(8,128)(2,1)}, bf16[4,32,128]{2,1,0:T(8,128)(2,1)}, ...) custom-call(f32[4,2048]{1,0:T(4,128)} %refs_0_.1, f32[4,2048]{1,0:T(4,128)} %refs_1_.1, ...), custom_call_target="tpu_custom_call" | custom-call | flops 3000000000 | bytes 9000000 | tf_op jit(solution)/shard_map/place/pallas_call | solution.py:308
  3.3 0.5 %collective-permute-start = (bf16[4,32,128]{2,1,0:T(8,128)(2,1)}, bf16[4,32,128]{2,1,0:T(8,128)(2,1)S(1)}, u32[]{:S(2)}, u32[]{:S(2)}) collective-permute-start(bf16[4,32,128]{2,1,0:T(8,128)(2,1)} %get-tuple-element.23), channel_id=1, source_target_pairs={{0,1},{1,0},{2,3},{3,2},{4,5},{5,4},{6,7},{7,6},{8,9},{9,8},{10,11... | collective-permute-start | bytes 98312 | tf_op jit(solution)/shard_map/ppermute | solution.py:281
  3.8 2.6 %collective-permute-start.1 = (bf16[4,32,128]{2,1,0:T(8,128)(2,1)}, bf16[4,32,128]{2,1,0:T(8,128)(2,1)S(1)}, u32[]{:S(2)}, u32[]{:S(2)}) collective-permute-start(bf16[4,32,128]{2,1,0:T(8,128)(2,1)} %get-tuple-element.24), channel_id=1, source_target_pairs={{0,2},{1,3},{2,0},{3,1},{4,6},{5,7},{6,4},{7,5},{8,10},{9,11},{10,... | collective-permute-start | bytes 98312 | tf_op jit(solution)/shard_map/ppermute | solution.py:281
  6.4 0.1 collective-permute-start.2
  6.5 0.0 copy-start.3
  6.5 0.8 %fusion.1 = (bf16[1,32,128]{2,1,0:T(8,128)(2,1)S(1)}, bf16[1,32,128]{2,1,0:T(8,128)(2,1)S(1)}, bf16[1,32,128]{2,1,0:T(8,128)(2,1)S(1)}, bf16[1,32,128]{2,1,0:T(8,128)(2,1)S(1)}) fusion(bf16[4,32,128]{2,1,0:T(8,128)(2,1)} %get-tuple-element.22), kind=kLoop, calls=%fused_computation.12 | loop fusion | bytes 65536 | tf_op jit(solution)/shard_map/slice | solution.py:331
  7.2 0.0 copy-done.3
  7.3 0.1 reshape.76
  7.4 0.0 copy-start.4
  7.4 0.7 %copy-done.4 = bf16[8,4,128]{2,1,0:T(4,128)(2,1)S(1)} copy-done((bf16[8,4,128]{2,1,0:T(4,128)(2,1)S(1)}, bf16[8,4,128]{2,1,0:T(4,128)(2,1)}, u32[]{:S(2)}) %copy-start.4) | copy-done | bytes 8216
  8.1 0.6 %gather_fusion = bf16[4,48,64]{2,1,0:T(8,128)(2,1)S(1)} fusion(bf16[4,48,64]{2,1,0:T(8,128)(2,1)S(1)} %bitcast.30, s32[1024]{0:T(1024)S(1)} %pad_clamp_fusion), kind=kCustom, calls=%fused_computation | custom fusion | bytes 49168 | tf_op jit(solution)/shard_map/gather | solution.py:325
  8.6 0.0 collective-permute-done
  8.7 0.0 collective-permute-done.1
  8.7 1.3 %collective-permute-done.2 = bf16[4,32,128]{2,1,0:T(8,128)(2,1)S(1)} collective-permute-done((bf16[4,32,128]{2,1,0:T(8,128)(2,1)}, bf16[4,32,128]{2,1,0:T(8,128)(2,1)S(1)}, u32[]{:S(2)}, u32[]{:S(2)}) %collective-permute-start.2) | collective-permute-done | bytes 32800 | tf_op jit(solution)/shard_map/ppermute | solution.py:281
  10.0 0.0 copy-start.1
  10.0 0.0 copy-start
  10.0 1.6 %collective-permute-start.3 = (bf16[2,16,512]{2,1,0:T(8,128)(2,1)S(1)}, bf16[2,16,512]{2,1,0:T(8,128)(2,1)S(1)}, u32[]{:S(2)}, u32[]{:S(2)}) collective-permute-start(bf16[2,16,512]{2,1,0:T(8,128)(2,1)S(1)} %pad_maximum_fusion.1), channel_id=1, source_target_pairs={{0,4},{4,0},{8,12},{12,8},{1,5},{5,1},{9,13},{13,9},{2,6},{6,2},{1... | collective-permute-start | bytes 98312 | tf_op jit(solution)/shard_map/ppermute | solution.py:281
  11.6 2.6 %collective-permute-start.4 = (bf16[2,16,512]{2,1,0:T(8,128)(2,1)S(1)}, bf16[2,16,512]{2,1,0:T(8,128)(2,1)S(1)}, u32[]{:S(2)}, u32[]{:S(2)}) collective-permute-start(bf16[2,16,512]{2,1,0:T(8,128)(2,1)S(1)} %pad_maximum_fusion.2), channel_id=1, source_target_pairs={{0,8},{4,12},{8,0},{12,4},{1,9},{5,13},{9,1},{13,5},{2,10},{6,14},... | collective-permute-start | bytes 98312 | tf_op jit(solution)/shard_map/ppermute | solution.py:281
  14.2 0.2 collective-permute-start.5
  14.4 0.0 copy-start.2
  14.5 0.0 collective-permute-done.3.refs_4_
  14.5 2.6 %collective-permute-done.4.refs_5_ = bf16[2,16,512]{2,1,0:T(8,128)(2,1)S(1)} collective-permute-done((bf16[2,16,512]{2,1,0:T(8,128)(2,1)S(1)}, bf16[2,16,512]{2,1,0:T(8,128)(2,1)S(1)}, u32[]{:S(2)}, u32[]{:S(2)}) %collective-permute-start.4) | collective-permute-done | bytes 32800 | tf_op jit(solution)/shard_map/ppermute | solution.py:281
  17.0 2.9 %collective-permute-done.5.refs_6_ = bf16[2,16,512]{2,1,0:T(8,128)(2,1)S(1)} collective-permute-done((bf16[2,16,512]{2,1,0:T(8,128)(2,1)S(1)}, bf16[2,16,512]{2,1,0:T(8,128)(2,1)S(1)}, u32[]{:S(2)}, u32[]{:S(2)}) %collective-permute-start.5) | collective-permute-done | bytes 32800 | tf_op jit(solution)/shard_map/ppermute | solution.py:281
  19.9 0.0 copy-done.1
  19.9 0.0 copy-done
  19.9 0.0 copy-done.2
  19.9 8.5 %cells.1 = (bf16[1152,128]{1,0:T(8,128)(2,1)S(1)}, bf16[4,64,64]{2,1,0:T(8,128)(2,1)S(1)}) custom-call(bf16[4,48,64]{2,1,0:T(8,128)(2,1)S(1)} %gather_fusion, bf16[8,16,128]{2,1,0:T(8,128)(2,1)S(1)} %pad.4.w_out_ref, bf16[2,128,256]{2,1,0:T(8,128)(2,1)S(1)} %copy-done, bf16[2,256,128]{2,1,0:T(8,128)(2,1)S(1)} %copy-done.1, ...), custom_call_target="tpu_custom_call" | custom-call | flops 10000000000 | bytes 30000000 | tf_op jit(solution)/shard_map/cells/pallas_call | solution.py:338
  28.4 1.0 %collective-permute-start.10 = (bf16[1152,128]{1,0:T(8,128)(2,1)S(1)}, bf16[1152,128]{1,0:T(8,128)(2,1)S(1)}, u32[]{:S(2)}, u32[]{:S(2)}) collective-permute-start(bf16[1152,128]{1,0:T(8,128)(2,1)S(1)} %get-tuple-element.27.refs_0_), channel_id=1, source_target_pairs={{0,2},{2,0},{1,3},{3,1},{4,6},{6,4},{5,7},{7,5},{8,10},{10,8},{9,1... | collective-permute-start | bytes 884744 | tf_op jit(solution)/shard_map/ppermute | solution.py:281
  29.4 0.4 collective-permute-start.8
  29.8 0.0 collective-permute-start.7
  29.8 4.0 %collective-permute-start.6 = (bf16[64,64]{1,0:T(8,128)(2,1)S(1)}, bf16[64,64]{1,0:T(8,128)(2,1)S(1)}, u32[]{:S(2)}, u32[]{:S(2)}) collective-permute-start(bf16[64,64]{1,0:T(8,128)(2,1)S(1)} %get-tuple-element.34), channel_id=1, source_target_pairs={{0,4},{4,0},{8,12},{12,8},{1,5},{5,1},{9,13},{13,9},{2,6},{6,2},{1... | collective-permute-start | bytes 24584 | tf_op jit(solution)/shard_map/ppermute | solution.py:281
  33.8 1.1 %collective-permute-done.8.refs_3_ = bf16[64,64]{1,0:T(8,128)(2,1)S(1)} collective-permute-done((bf16[64,64]{1,0:T(8,128)(2,1)S(1)}, bf16[64,64]{1,0:T(8,128)(2,1)S(1)}, u32[]{:S(2)}, u32[]{:S(2)}) %collective-permute-start.8) | collective-permute-done | bytes 8224 | tf_op jit(solution)/shard_map/ppermute | solution.py:281
  35.0 0.0 collective-permute-done.7.refs_2_
  35.0 0.6 %collective-permute-done.6.refs_1_ = bf16[64,64]{1,0:T(8,128)(2,1)S(1)} collective-permute-done((bf16[64,64]{1,0:T(8,128)(2,1)S(1)}, bf16[64,64]{1,0:T(8,128)(2,1)S(1)}, u32[]{:S(2)}, u32[]{:S(2)}) %collective-permute-start.6) | collective-permute-done | bytes 8224 | tf_op jit(solution)/shard_map/ppermute | solution.py:281
  35.5 1.2 %collective-permute-start.9 = (bf16[64,64]{1,0:T(8,128)(2,1)S(1)}, bf16[64,64]{1,0:T(8,128)(2,1)S(1)}, u32[]{:S(2)}, u32[]{:S(2)}) collective-permute-start(bf16[64,64]{1,0:T(8,128)(2,1)S(1)} %shard_sum.1.refs_0_), channel_id=1, source_target_pairs={{0,2},{2,0},{1,3},{3,1},{4,6},{6,4},{5,7},{7,5},{8,10},{10,8},{9,1... | collective-permute-start | bytes 24584 | tf_op jit(solution)/shard_map/ppermute | solution.py:281
  36.7 2.6 %collective-permute-done.9.refs_1_ = bf16[64,64]{1,0:T(8,128)(2,1)S(1)} collective-permute-done((bf16[64,64]{1,0:T(8,128)(2,1)S(1)}, bf16[64,64]{1,0:T(8,128)(2,1)S(1)}, u32[]{:S(2)}, u32[]{:S(2)}) %collective-permute-start.9) | collective-permute-done | bytes 8224 | tf_op jit(solution)/shard_map/ppermute | solution.py:281
  39.3 0.0 collective-permute-done.10.refs_2_
  39.4 0.1 collective-permute-start.11
  39.5 0.5 %collective-permute-start.12 = (bf16[1152,128]{1,0:T(8,128)(2,1)S(1)}, bf16[1152,128]{1,0:T(8,128)(2,1)S(1)}, u32[]{:S(2)}, u32[]{:S(2)}) collective-permute-start(bf16[1152,128]{1,0:T(8,128)(2,1)S(1)} %get-tuple-element.27.refs_0_), channel_id=1, source_target_pairs={{0,1},{1,0},{2,3},{3,2},{4,5},{5,4},{6,7},{7,6},{8,9},{9,8},{10,11... | collective-permute-start | bytes 884744 | tf_op jit(solution)/shard_map/ppermute | solution.py:281
  40.0 1.5 %collective-permute-done.12.refs_1_ = bf16[1152,128]{1,0:T(8,128)(2,1)S(1)} collective-permute-done((bf16[1152,128]{1,0:T(8,128)(2,1)S(1)}, bf16[1152,128]{1,0:T(8,128)(2,1)S(1)}, u32[]{:S(2)}, u32[]{:S(2)}) %collective-permute-start.12) | collective-permute-done | bytes 294944 | tf_op jit(solution)/shard_map/ppermute | solution.py:281
  41.5 1.4 %unpack.2 = (f32[8,128,256]{2,1,0:T(8,128)}, f32[8,256,128]{2,1,0:T(8,128)}, f32[8,48,128]{2,1,0:T(8,128)}, f32[8,4,128]{2,1,0:T(4,128)}) custom-call(bf16[1152,128]{1,0:T(8,128)(2,1)S(1)} %get-tuple-element.27.refs_0_, bf16[1152,128]{1,0:T(8,128)(2,1)S(1)} %collective-permute-done.12.refs_1_, bf16[1152,128]{1,0:T(8,128)(2,1)S(1)} %collective-permute-done.10.refs_2_), custom_call_target="tpu_custom_call" | custom-call | tf_op jit(solution)/shard_map/unpack/pallas_call | solution.py:392
  42.9 0.0 collective-permute-done.11.refs_0_
  42.9 1.5 %unpack.3 = (f32[8,128,256]{2,1,0:T(8,128)}, f32[8,256,128]{2,1,0:T(8,128)}, f32[8,48,128]{2,1,0:T(8,128)}, f32[8,4,128]{2,1,0:T(4,128)}, f32[3,64]{1,0:T(4,128)}, /*index=5*/f32[48,64]{1,0:T(8,128)}) custom-call(bf16[1216,128]{1,0:T(8,128)(2,1)S(1)} %collective-permute-done.11.refs_0_, ...), custom_call_target="tpu_custom_call", output_to_operand_aliasing={{0}: (2, {}), {1}: (3, {}), {2}: (4, {}), {3}: (5, {})} | custom-call | tf_op jit(solution)/shard_map/unpack/pallas_call | solution.py:392
  (14 shorter events, 0.1 us)
Async XLA Ops:
  3.3 5.3 %collective-permute-start = (bf16[4,32,128]{2,1,0:T(8,128)(2,1)}, bf16[4,32,128]{2,1,0:T(8,128)(2,1)S(1)}, u32[]{:S(2)}, u32[]{:S(2)}) collective-permute-start(bf16[4,32,128]{2,1,0:T(8,128)(2,1)} %get-tuple-element.23), channel_id=1, source_target_pairs={{0,1},{1,0},{2,3},{3,2},{4,5},{5,4},{6,7},{7,6},{8,9},{9,8},{10,11... | collective-permute-start | bytes 98312 | tf_op jit(solution)/shard_map/ppermute | solution.py:281
  3.8 4.8 %collective-permute-start.1 = (bf16[4,32,128]{2,1,0:T(8,128)(2,1)}, bf16[4,32,128]{2,1,0:T(8,128)(2,1)S(1)}, u32[]{:S(2)}, u32[]{:S(2)}) collective-permute-start(bf16[4,32,128]{2,1,0:T(8,128)(2,1)} %get-tuple-element.24), channel_id=1, source_target_pairs={{0,2},{1,3},{2,0},{3,1},{4,6},{5,7},{6,4},{7,5},{8,10},{9,11},{10,... | collective-permute-start | bytes 98312 | tf_op jit(solution)/shard_map/ppermute | solution.py:281
  6.4 3.6 %collective-permute-start.2 = (bf16[4,32,128]{2,1,0:T(8,128)(2,1)}, bf16[4,32,128]{2,1,0:T(8,128)(2,1)S(1)}, u32[]{:S(2)}, u32[]{:S(2)}) collective-permute-start(bf16[4,32,128]{2,1,0:T(8,128)(2,1)} %get-tuple-element.25), channel_id=1, source_target_pairs={{0,3},{1,2},{2,1},{3,0},{4,7},{5,6},{6,5},{7,4},{8,11},{9,10},{10,... | collective-permute-start | bytes 98312 | tf_op jit(solution)/shard_map/ppermute | solution.py:281
  6.5 0.8 %copy-start.3 = (bf16[48,256]{1,0:T(8,128)(2,1)S(1)}, bf16[48,256]{1,0:T(8,128)(2,1)}, u32[]{:S(2)}) copy-start(bf16[48,256]{1,0:T(8,128)(2,1)} %param.21) | copy-start | bytes 73732
  7.4 0.7 %copy-start.4 = (bf16[8,4,128]{2,1,0:T(4,128)(2,1)S(1)}, bf16[8,4,128]{2,1,0:T(4,128)(2,1)}, u32[]{:S(2)}) copy-start(bf16[8,4,128]{2,1,0:T(4,128)(2,1)} %param.19) | copy-start | bytes 24580
  10.0 10.0 %copy-start.1 = (bf16[2,256,128]{2,1,0:T(8,128)(2,1)S(1)}, bf16[2,256,128]{2,1,0:T(8,128)(2,1)}, u32[]{:S(2)}) copy-start(bf16[2,256,128]{2,1,0:T(8,128)(2,1)} %get-tuple-element.20.refs_1_) | copy-start | bytes 393220
  10.0 10.0 %copy-start = (bf16[2,128,256]{2,1,0:T(8,128)(2,1)S(1)}, bf16[2,128,256]{2,1,0:T(8,128)(2,1)}, u32[]{:S(2)}) copy-start(bf16[2,128,256]{2,1,0:T(8,128)(2,1)} %get-tuple-element.19.refs_0_) | copy-start | bytes 393220
  10.0 4.5 %collective-permute-start.3 = (bf16[2,16,512]{2,1,0:T(8,128)(2,1)S(1)}, bf16[2,16,512]{2,1,0:T(8,128)(2,1)S(1)}, u32[]{:S(2)}, u32[]{:S(2)}) collective-permute-start(bf16[2,16,512]{2,1,0:T(8,128)(2,1)S(1)} %pad_maximum_fusion.1), channel_id=1, source_target_pairs={{0,4},{4,0},{8,12},{12,8},{1,5},{5,1},{9,13},{13,9},{2,6},{6,2},{1... | collective-permute-start | bytes 98312 | tf_op jit(solution)/shard_map/ppermute | solution.py:281
  11.6 5.4 %collective-permute-start.4 = (bf16[2,16,512]{2,1,0:T(8,128)(2,1)S(1)}, bf16[2,16,512]{2,1,0:T(8,128)(2,1)S(1)}, u32[]{:S(2)}, u32[]{:S(2)}) collective-permute-start(bf16[2,16,512]{2,1,0:T(8,128)(2,1)S(1)} %pad_maximum_fusion.2), channel_id=1, source_target_pairs={{0,8},{4,12},{8,0},{12,4},{1,9},{5,13},{9,1},{13,5},{2,10},{6,14},... | collective-permute-start | bytes 98312 | tf_op jit(solution)/shard_map/ppermute | solution.py:281
  14.2 5.7 %collective-permute-start.5 = (bf16[2,16,512]{2,1,0:T(8,128)(2,1)S(1)}, bf16[2,16,512]{2,1,0:T(8,128)(2,1)S(1)}, u32[]{:S(2)}, u32[]{:S(2)}) collective-permute-start(bf16[2,16,512]{2,1,0:T(8,128)(2,1)S(1)} %pad_maximum_fusion.3), channel_id=1, source_target_pairs={{0,12},{4,8},{8,4},{12,0},{1,13},{5,9},{9,5},{13,1},{2,14},{6,10},... | collective-permute-start | bytes 98312 | tf_op jit(solution)/shard_map/ppermute | solution.py:281
  14.4 5.5 %copy-start.2 = (bf16[2,48,128]{2,1,0:T(8,128)(2,1)S(1)}, bf16[2,48,128]{2,1,0:T(8,128)(2,1)}, u32[]{:S(2)}) copy-start(bf16[2,48,128]{2,1,0:T(8,128)(2,1)} %get-tuple-element.21.refs_2_) | copy-start | bytes 73732
  28.4 10.9 %collective-permute-start.10 = (bf16[1152,128]{1,0:T(8,128)(2,1)S(1)}, bf16[1152,128]{1,0:T(8,128)(2,1)S(1)}, u32[]{:S(2)}, u32[]{:S(2)}) collective-permute-start(bf16[1152,128]{1,0:T(8,128)(2,1)S(1)} %get-tuple-element.27.refs_0_), channel_id=1, source_target_pairs={{0,2},{2,0},{1,3},{3,1},{4,6},{6,4},{5,7},{7,5},{8,10},{10,8},{9,1... | collective-permute-start | bytes 884744 | tf_op jit(solution)/shard_map/ppermute | solution.py:281
  29.4 5.5 %collective-permute-start.8 = (bf16[64,64]{1,0:T(8,128)(2,1)S(1)}, bf16[64,64]{1,0:T(8,128)(2,1)S(1)}, u32[]{:S(2)}, u32[]{:S(2)}) collective-permute-start(bf16[64,64]{1,0:T(8,128)(2,1)S(1)} %get-tuple-element.32), channel_id=1, source_target_pairs={{0,12},{4,8},{8,4},{12,0},{1,13},{5,9},{9,5},{13,1},{2,14},{6,10},... | collective-permute-start | bytes 24584 | tf_op jit(solution)/shard_map/ppermute | solution.py:281
  29.8 5.1 %collective-permute-start.7 = (bf16[64,64]{1,0:T(8,128)(2,1)S(1)}, bf16[64,64]{1,0:T(8,128)(2,1)S(1)}, u32[]{:S(2)}, u32[]{:S(2)}) collective-permute-start(bf16[64,64]{1,0:T(8,128)(2,1)S(1)} %get-tuple-element.33), channel_id=1, source_target_pairs={{0,8},{4,12},{8,0},{12,4},{1,9},{5,13},{9,1},{13,5},{2,10},{6,14},... | collective-permute-start | bytes 24584 | tf_op jit(solution)/shard_map/ppermute | solution.py:281
  29.8 5.7 %collective-permute-start.6 = (bf16[64,64]{1,0:T(8,128)(2,1)S(1)}, bf16[64,64]{1,0:T(8,128)(2,1)S(1)}, u32[]{:S(2)}, u32[]{:S(2)}) collective-permute-start(bf16[64,64]{1,0:T(8,128)(2,1)S(1)} %get-tuple-element.34), channel_id=1, source_target_pairs={{0,4},{4,0},{8,12},{12,8},{1,5},{5,1},{9,13},{13,9},{2,6},{6,2},{1... | collective-permute-start | bytes 24584 | tf_op jit(solution)/shard_map/ppermute | solution.py:281
  35.5 3.8 %collective-permute-start.9 = (bf16[64,64]{1,0:T(8,128)(2,1)S(1)}, bf16[64,64]{1,0:T(8,128)(2,1)S(1)}, u32[]{:S(2)}, u32[]{:S(2)}) collective-permute-start(bf16[64,64]{1,0:T(8,128)(2,1)S(1)} %shard_sum.1.refs_0_), channel_id=1, source_target_pairs={{0,2},{2,0},{1,3},{3,1},{4,6},{6,4},{5,7},{7,5},{8,10},{10,8},{9,1... | collective-permute-start | bytes 24584 | tf_op jit(solution)/shard_map/ppermute | solution.py:281
  39.4 3.5 %collective-permute-start.11 = (bf16[1216,128]{1,0:T(8,128)(2,1)S(1)}, bf16[1216,128]{1,0:T(8,128)(2,1)S(1)}, u32[]{:S(2)}, u32[]{:S(2)}) collective-permute-start(bf16[1216,128]{1,0:T(8,128)(2,1)S(1)} %relay.1.refs_1_), channel_id=1, source_target_pairs={{0,1},{1,0},{2,3},{3,2},{4,5},{5,4},{6,7},{7,6},{8,9},{9,8},{10,11... | collective-permute-start | bytes 933896 | tf_op jit(solution)/shard_map/ppermute | solution.py:281
  39.5 2.0 %collective-permute-start.12 = (bf16[1152,128]{1,0:T(8,128)(2,1)S(1)}, bf16[1152,128]{1,0:T(8,128)(2,1)S(1)}, u32[]{:S(2)}, u32[]{:S(2)}) collective-permute-start(bf16[1152,128]{1,0:T(8,128)(2,1)S(1)} %get-tuple-element.27.refs_0_), channel_id=1, source_target_pairs={{0,1},{1,0},{2,3},{3,2},{4,5},{5,4},{6,7},{7,6},{8,9},{9,8},{10,11... | collective-permute-start | bytes 884744 | tf_op jit(solution)/shard_map/ppermute | solution.py:281

commit v3 on v2

--- a/solution.py
+++ b/solution.py
@@ -34,15 +34,11 @@
     return lax.broadcasted_iota(jnp.int32, shape, dim)
 
 
-def me():
-    return lax.axis_index("cell"), lax.axis_index(PART_AXES)
-
-
 def place_kernel(cells_all, cap, n_cell, n_part, *refs):
-    sources, weights, outs, own = refs[:6], refs[6:9], refs[9:9 + n_part], refs[9 + n_part:12 + n_part]
-    arrays, (spread, placed, sems) = refs[12 + n_part:18 + n_part], refs[18 + n_part:]
+    sources, weights, placed, own = refs[:6], refs[6:9], refs[9], refs[10:13]
+    arrays, (spread, sems) = refs[13:19], refs[19:]
     points_ref, cot_ref, cell_ref, cam_ref, valid_ref, poses_ref = arrays
-    me_cell, me_part = me()
+    me_part = lax.axis_index(PART_AXES)
     lc = cells_all // (n_cell * n_part)
     pairs = list(zip(sources, arrays)) + [
         (source.at[pl.ds(me_part * lc, lc)], target) for source, target in zip(weights, own)
@@ -90,12 +86,6 @@
     for c in range(cells_all):
         spread[c * RECORD:(c + 1) * RECORD, :] = jnp.where(cell_rows == c, record, 0.0).astype(BF16)
     placed[...] = dot_nt(spread[...], rank_hot).astype(BF16)
-    rows = lc * RECORD
-    for kp in range(n_part):
-        for kc in range(n_cell):
-            owner = (me_cell ^ kc) * n_part + (me_part ^ kp)
-            start = pl.multiple_of(owner * rows, rows)
-            outs[kp][kc] = placed[pl.ds(start, rows), :]
     for copy in copies[6:]:
         copy.wait()
 
@@ -128,10 +118,15 @@
     return plus, jnp.where(x >= 0.0, r, e * r)
 
 
+def fold(table, rows):
+    return jnp.concatenate([table[r:r + rows] for r in range(0, table.shape[0], rows)], axis=1)
+
+
 def backward_samples(n_cell, freq_count, codes_ref, w_out, weights, arrived, table_in, table_ref, kept, j):
     enc_s, gt_s, trunk_s, gc_s, act_s, rec_s = kept
     w_enc, w_hidden, w_code = weights
-    width = arrived[0].shape[2]
+    blocks = arrived.shape[0] // n_cell
+    width = blocks * arrived.shape[2]
     cams = codes_ref.shape[2]
     hidden = w_hidden.shape[0]
     half = freq_count // 2
@@ -139,7 +134,9 @@
     top = 2.0 ** (half // 4)
     for kc in range(n_cell):
         cols = slice(kc * width, (kc + 1) * width)
-        rec = arrived[kc][j]
+        rec = jnp.concatenate(
+            [arrived[kc * blocks + b, j * RECORD:(j + 1) * RECORD, :] for b in range(blocks)], axis=1
+        )
         rec_s[:, cols] = rec
         recf = rec.astype(F32)
         coords = recf[0:4] + recf[4:8]
@@ -183,7 +180,9 @@
         table = dot_nt(per_sample, cam_hot)
         if table_in is not None:
             table = table + table_in[kc]
-        table_ref[kc] = table.astype(table_ref.dtype)
+        copies = table_ref.shape[0] // n_cell
+        for i in range(copies):
+            table_ref[kc * copies + i] = fold(table, table_ref.shape[1]).astype(table_ref.dtype)
 
 
 def sum_weights(kept, packed_ref):
@@ -202,8 +201,8 @@
 
 
 def cells_kernel(n_cell, freq_count, lc, codes_ref, w_out_ref, *refs):
-    weights, arrived, refs = refs[:3], refs[3:3 + n_cell], refs[3 + n_cell:]
-    packed_ref, table_ref, kept, sums = refs[0], refs[1], refs[2:8], refs[8]
+    weights, arrived = refs[:3], refs[3]
+    packed_ref, table_ref, kept, sums = refs[4], refs[5], refs[6:12], refs[12]
     rows = packed_ref.shape[0] // lc
     me_part = lax.axis_index(PART_AXES)
     for j in range(lc):
@@ -213,19 +212,9 @@
         sum_weights([k.at[j] for k in kept], packed_ref.at[j * rows:(j + 1) * rows])
 
 
-def shard_sum_kernel(count, *refs):
-    total = refs[0][0].astype(F32)
-    for k in range(1, count):
-        total = total + refs[k][...].astype(F32)
-    refs[count][...] = total.astype(BF16)
-
-
-def relay_kernel(n_rep, *refs):
-    parts, packed_ref, out_ref = refs[:n_rep], refs[n_rep], refs[n_rep + 1]
-    total = sum(part[...].astype(F32) for part in parts)
-    rows, cams = total.shape
+def relay_kernel(tables_ref, packed_ref, _, out_ref):
+    total = sum(tables_ref[k].astype(F32) for k in range(tables_ref.shape[0]))
     out_ref[0:packed_ref.shape[0], :] = packed_ref[...]
-    total = jnp.concatenate([total, jnp.zeros((rows, out_ref.shape[1] - cams), F32)], axis=1)
     out_ref[packed_ref.shape[0]:, :] = total.astype(BF16)
 
 
@@ -241,8 +230,9 @@
         total = here[first:, :].astype(F32)
         for i in tables_at:
             total = total + ins[i][first:, :].astype(F32)
-        refs[0][...] = total[code:code + 3, 0:cams]
-        refs[1][...] = total[0:code, 0:cams]
+        total = jnp.concatenate([total[:, c:c + cams] for c in range(0, total.shape[1], cams)], axis=0)
+        refs[0][...] = total[code:code + 3]
+        refs[1][...] = total[0:code]
         refs = refs[2:]
     wide, sems = refs[:-1], refs[-1]
     enc_v, hidden_v, code_v, out_v = wide
@@ -301,7 +291,7 @@
 
     inputs = (points, cotangent, cell_ids.reshape(1, n), camera_ids.reshape(1, n), valid.reshape(1, n), poses)
     weights = (w_enc, w_hidden, w_code)
-    out_shape = [jax.ShapeDtypeStruct((n_cell, lc * RECORD, cap), BF16)] * n_part + [
+    out_shape = [jax.ShapeDtypeStruct((cells_all * RECORD, cap), BF16)] + [
         jax.ShapeDtypeStruct((lc,) + w.shape[1:], BF16) for w in weights
     ]
     room = sum(2 * a.size // a.shape[-1] * max(a.shape[-1], 128) for a in out_shape) + SLACK_BYTES
@@ -312,70 +302,65 @@
         out_specs=[vmem] * len(out_shape),
         scratch_shapes=[pltpu.VMEM(a.shape, a.dtype) for a in inputs] + [
             pltpu.VMEM((cells_all * RECORD, n), BF16),
-            pltpu.VMEM((cells_all * RECORD, cap), BF16),
             pltpu.SemaphoreType.DMA((9,)),
         ],
         compiler_params=pltpu.CompilerParams(vmem_limit_bytes=ALL_VMEM_BYTES - room),
         cost_estimate=cost(3),
         name="place",
     )(*inputs, *weights)
-    sent, own_weights = placed[:n_part], placed[n_part:]
-
-    order = lax.axis_index("cell") ^ jnp.arange(n_cell, dtype=jnp.int32)
-    codes_rel = codes.reshape(code, n_cell, cams).transpose(1, 0, 2)[order]
+    sent, own_weights = placed[0], placed[1:]
+    codes_cell = codes.reshape(code, n_cell, cams).transpose(1, 0, 2)
     w_out_rows = jnp.pad(w_out, ((0, 0), (TANGENT_ROW, RECORD - TANGENT_ROW - w_out.shape[1]), (0, 0)))
 
-    near = [exchange(sent[kp], PART_AXES, n_part, kp) for kp in range(n_part)]
-    arrived = []
-    for kc in range(n_cell):
-        lanes = jnp.concatenate([near[kp][kc] for kp in range(n_part)], axis=-1)
-        arrived.append(exchange(lanes.reshape(lc, RECORD, width), "cell", n_cell, kc))
+    arrived = lax.all_to_all(
+        sent.reshape(n_cell * n_part, lc * RECORD, cap), ("cell",) + PART_AXES, 0, 0, tiled=True
+    )
+    if cap % 128:
+        arrived = arrived.reshape(n_cell, n_part, lc * RECORD, cap).transpose(0, 2, 1, 3)
+        arrived = arrived.reshape(n_cell, lc * RECORD, width)
 
     packed_rows = enc * (hidden // color) + hidden + code + RECORD
     slots = n_cell * width
     kept_rows = (enc, hidden, hidden + code, color, color, RECORD)
     table_shape = (n_cell, code + RECORD, cams)
+    folded = (table_shape[1] * cams // color, color)
     packed, table = pl.pallas_call(
         functools.partial(cells_kernel, n_cell, freq_count, lc),
-        in_specs=[vmem] * (5 + n_cell),
+        in_specs=[vmem] * 6,
         out_specs=[vmem, vmem],
         out_shape=[
             jax.ShapeDtypeStruct((lc * packed_rows, color), BF16),
-            jax.ShapeDtypeStruct(table_shape, BF16),
+            jax.ShapeDtypeStruct((n_cell * n_rep,) + folded, BF16),
         ],
         scratch_shapes=[pltpu.VMEM((lc, r, slots), BF16) for r in kept_rows] + [pltpu.VMEM(table_shape, F32)],
         compiler_params=params,
         cost_estimate=cost(10),
         name="cells",
-    )(codes_rel, w_out_rows, *own_weights, *arrived)
+    )(codes_cell, w_out_rows, *own_weights, arrived)
 
     over_rep = [exchange(packed, "rep", n_rep, kr) for kr in range(n_rep)]
-    tables = [table] + [exchange(table[kc], "cell", n_cell, kc) for kc in range(1, n_cell)]
-    mine = pl.pallas_call(
-        functools.partial(shard_sum_kernel, n_cell),
-        in_specs=[vmem] * n_cell,
+    over_sub = [exchange(packed, "sub", n_sub, ks) for ks in range(n_sub)]
+    tables = lax.all_to_all(table, ("cell", "rep"), 0, 0, tiled=True)
+    relayed = pl.pallas_call(
+        relay_kernel,
+        in_specs=[vmem] * 3,
         out_specs=vmem,
-        out_shape=jax.ShapeDtypeStruct(table_shape[1:], BF16),
-        compiler_params=params,
-        cost_estimate=cost(0),
-        name="shard_sum",
-    )(*tables)
-    parts = [exchange(mine, "rep", n_rep, kr) for kr in range(n_rep)]
-    relayed = pl.pallas_call(
-        functools.partial(relay_kernel, n_rep),
-        in_specs=[vmem] * (n_rep + 1),
-        out_specs=vmem,
-        out_shape=jax.ShapeDtypeStruct((lc * packed_rows + table_shape[1], color), BF16),
+        out_shape=jax.ShapeDtypeStruct((lc * packed_rows + folded[0], color), BF16),
         compiler_params=params,
         cost_estimate=cost(0),
         name="relay",
-    )(*parts, over_rep[1])
+    )(tables, over_rep[1], over_sub[-1])
 
     early, late = [], []
     for kr in range(n_rep):
         for ks in range(n_sub):
-            sent_on = relayed if kr == 1 and ks else over_rep[kr]
-            (late if kr and ks else early).append((kr * n_sub + ks, exchange(sent_on, "sub", n_sub, ks)))
+            if kr == 0:
+                early.append((ks, over_sub[ks]))
+            elif ks == 0:
+                early.append((kr * n_sub, over_rep[kr]))
+            else:
+                sent_on = relayed if kr == 1 else over_rep[kr]
+                late.append((kr * n_sub + ks, exchange(sent_on, "sub", n_sub, ks)))
     shapes = [
         jax.ShapeDtypeStruct((local, enc, hidden), F32),
         jax.ShapeDtypeStruct((local, hidden, color), F32),

time: 44.7 us -> 41.2 us (0.922)
  blocking collectives: 0 us -> 10.3 us
  starting transfers between devices: 14.7 us -> 7.71 us
  waiting for transfers between devices: 12.6 us -> 7.27 us
  local copies, waits for them, and re-layouts: 2.15 us -> 0.81 us
    ppermute x13 -> x3, starting transfers between devices: 14.7 us -> 0.21 us  [exchange(): return lax.ppermute(value, axes, [(i, i ^ k) for i in range(count)])]
    ppermute x13 -> x3, waiting for transfers between devices: 12.6 us -> 0.17 us  [exchange(): return lax.ppermute(value, axes, [(i, i ^ k) for i in range(count)])]
    all_to_all x0 -> x1, blocking collectives: none -> 10.3 us  [shards(): tables = lax.all_to_all(table, ('cell', 'rep'), 0, 0, tiled=True)]
    all_to_all x0 -> x1, starting transfers between devices: none -> 7.5 us  [shards(): lax.all_to_all(sent.reshape(n_cell * n_part, lc * RECORD, cap), ('cell',)...]
    all_to_all x0 -> x1, waiting for transfers between devices: none -> 7.1 us  [shards(): lax.all_to_all(sent.reshape(n_cell * n_part, lc * RECORD, cap), ('cell',)...]
    slice x4 -> x0, local copies, waits for them, and re-layouts: 0.78 us -> none  [shards(): lanes = jnp.concatenate([near[kp][kc] for kp in range(n_part)], axis=-1)]
    gather x1 -> x0, local copies, waits for them, and re-layouts: 0.56 us -> none  [shards(): codes_rel = codes.reshape(code, n_cell, cams).transpose(1, 0, 2)[order]]
  transfers between devices with their start and end apart: 13 -> 4, of which waited for: 7 -> 2; matrix products, arithmetic and copies ran while one was open for 3% -> 0% of each run, Pallas kernels for 3% -> 3%
where the time goes in v3:
time: 41.2 us; the launch traced here: 40.9 us
  Pallas kernels  14.1 us (34%)
  blocking collectives  10.3 us (25%)
  starting transfers between devices  7.71 us (19%)
  waiting for transfers between devices  7.27 us (18%)
  local copies, waits for them, and re-layouts  0.81 us (2%)
  between operations  0.75 us (2%)
    all_to_all x1, blocking collectives, shards(): tables = lax.all_to_all(table, ('cell', 'rep'), 0, 0, tiled=True)  10.3 us
    pallas_call x1, Pallas kernels, shards(): pl.pallas_call(functools.partial(cells_kernel, n_cell, freq_count, lc), i...  8.5 us
    all_to_all x1, starting transfers between devices, shards(): lax.all_to_all(sent.reshape(n_cell * n_part, lc * RECORD, cap), ('cell',)...  7.5 us
    all_to_all x1, waiting for transfers between devices, shards(): lax.all_to_all(sent.reshape(n_cell * n_part, lc * RECORD, cap), ('cell',)...  7.1 us
    pallas_call x2, Pallas kernels, shards(): pl.pallas_call(functools.partial(unpack_kernel, tuple((place for place, _...  2.9 us
    pallas_call x1, Pallas kernels, shards(): pl.pallas_call(functools.partial(place_kernel, cells_all, cap, n_cell, n_...  2.66 us
  transfers between devices with their start and end apart: 4, of which 2 were waited for; matrix products, arithmetic and copies ran while one was open for 0% of the time, Pallas kernels for 3%

profile of v3, /device:TPU:0, one launch (start us, length us, event | category | flops | bytes accessed | tf_op | source)
XLA Modules:
  0.0 40.9 jit_solution(18273213998580865633)
XLA Ops:
  0.6 2.7 %place.1 = (bf16[512,128]{1,0:T(8,128)(2,1)}, bf16[2,128,256]{2,1,0:T(8,128)(2,1)}, bf16[2,256,128]{2,1,0:T(8,128)(2,1)}, bf16[2,48,128]{2,1,0:T(8,128)(2,1)}) custom-call(f32[4,2048]{1,0:T(4,128)} %refs_0_.1, f32[4,2048]{1,0:T(4,128)} %refs_1_.1, s32[1,2048]{1,0:T(1,128)} %bitcast.9, s32[1,2048]{1,0:T(1,128)} %bitcast.10, s32[1,2048]{1,0:T(1,128)} %bitcast.11, ...), custom_call_target="tpu_custom_call" | custom-call | flops 3000000000 | bytes 9000000 | tf_op jit(solution)/shard_map/place/pallas_call | solution.py:298
  3.3 0.0 copy-start.3
  3.3 0.0 copy-start.1
  3.3 7.5 %all-to-all-start = ((bf16[16,32,128]{2,1,0:T(8,128)(2,1)}), bf16[16,32,128]{2,1,0:T(8,128)(2,1)S(1)}, u32[]{:S(2)}, u32[]{:S(2)}) async-start(bf16[16,32,128]{2,1,0:T(8,128)(2,1)} %bitcast.8), calls=%async_computation | async-start | bytes 262144 | tf_op jit(solution)/shard_map/all_to_all | solution.py:315
  10.8 0.0 copy-done.3
  10.8 0.0 copy-start
  10.9 0.1 reshape.27
  11.0 0.0 copy-start.4
  11.0 0.7 %copy-done.4 = bf16[8,4,128]{2,1,0:T(4,128)(2,1)S(1)} copy-done((bf16[8,4,128]{2,1,0:T(4,128)(2,1)S(1)}, bf16[8,4,128]{2,1,0:T(4,128)(2,1)}, u32[]{:S(2)}) %copy-start.4) | copy-done | bytes 8216
  11.7 0.0 copy-start.2
  11.7 7.1 %all-to-all-done.refs_3_ = bf16[16,32,128]{2,1,0:T(8,128)(2,1)S(1)} async-done(((bf16[16,32,128]{2,1,0:T(8,128)(2,1)}), bf16[16,32,128]{2,1,0:T(8,128)(2,1)S(1)}, u32[]{:S(2)}, u32[]{:S(2)}) %all-to-all-start) | async-done | bytes 131104 | tf_op jit(solution)/shard_map/all_to_all | solution.py:315
  18.8 0.0 copy-done.1
  18.8 0.0 copy-done
  18.8 0.0 copy-done.2
  18.8 8.5 %cells.1 = (bf16[1152,128]{1,0:T(8,128)(2,1)S(1)}, bf16[8,32,128]{2,1,0:T(8,128)(2,1)S(1)}) custom-call(bf16[4,48,64]{2,1,0:T(8,128)(2,1)S(1)} %bitcast.7, bf16[8,16,128]{2,1,0:T(8,128)(2,1)S(1)} %pad.4.w_out_ref, bf16[2,128,256]{2,1,0:T(8,128)(2,1)S(1)} %copy-done, bf16[2,256,128]{2,1,0:T(8,128)(2,1)S(1)} %copy-done.1, bf16[2,48,128]{2,1,0:T(8,128)(2,1)S(1)} %copy-done.2, ...), custom_call_target="tpu_custom_call" | custom-call | flops 10000000000 | bytes 30000000 | tf_op jit(solution)/shard_map/cells/pallas_call | solution.py:327
  27.3 0.1 collective-permute-start.1
  27.4 0.1 collective-permute-start
  27.4 10.3 %all_to_all.10.tables_ref = bf16[8,32,128]{2,1,0:T(8,128)(2,1)S(1)} all-to-all(bf16[8,32,128]{2,1,0:T(8,128)(2,1)S(1)} %get-tuple-element.20), channel_id=1, replica_groups=mesh['groups'=2,'cell'=4,'rep'=2,'sub'=2] {'cell','rep'}, dimensions={0} | all-to-all | bytes 131072 | tf_op jit(solution)/shard_map/all_to_all | solution.py:343
  37.7 0.0 collective-permute-done.1._.refs_1_
  37.7 0.0 collective-permute-done.packed_ref.refs_2_
  37.7 0.1 collective-permute-start.2
  37.8 1.4 %unpack.2 = (f32[8,128,256]{2,1,0:T(8,128)}, f32[8,256,128]{2,1,0:T(8,128)}, f32[8,48,128]{2,1,0:T(8,128)}, f32[8,4,128]{2,1,0:T(4,128)}) custom-call(bf16[1152,128]{1,0:T(8,128)(2,1)S(1)} %get-tuple-element.21.refs_0_, bf16[1152,128]{1,0:T(8,128)(2,1)S(1)} %collective-permute-done.1._.refs_1_, bf16[1152,128]{1,0:T(8,128)(2,1)S(1)} %collective-permute-done.packed_ref.refs_2_), custom_call_target="tpu_custom_call" | custom-call | tf_op jit(solution)/shard_map/unpack/pallas_call | solution.py:377
  39.2 0.2 collective-permute-done.2.refs_0_
  39.4 1.5 %unpack.3 = (f32[8,128,256]{2,1,0:T(8,128)}, f32[8,256,128]{2,1,0:T(8,128)}, f32[8,48,128]{2,1,0:T(8,128)}, f32[8,4,128]{2,1,0:T(4,128)}, f32[3,64]{1,0:T(4,128)}, /*index=5*/f32[48,64]{1,0:T(8,128)}) custom-call(bf16[1184,128]{1,0:T(8,128)(2,1)S(1)} %collective-permute-done.2.refs_0_, ...), custom_call_target="tpu_custom_call", output_to_operand_aliasing={{0}: (2, {}), {1}: (3, {}), {2}: (4, {}), {3}: (5, {})} | custom-call | tf_op jit(solution)/shard_map/unpack/pallas_call | solution.py:377
  (3 shorter events, 0.0 us)
Async XLA Ops:
  3.3 7.5 %copy-start.3 = (bf16[48,256]{1,0:T(8,128)(2,1)S(1)}, bf16[48,256]{1,0:T(8,128)(2,1)}, u32[]{:S(2)}) copy-start(bf16[48,256]{1,0:T(8,128)(2,1)} %param.21) | copy-start | bytes 73732
  3.3 15.5 %copy-start.1 = (bf16[2,256,128]{2,1,0:T(8,128)(2,1)S(1)}, bf16[2,256,128]{2,1,0:T(8,128)(2,1)}, u32[]{:S(2)}) copy-start(bf16[2,256,128]{2,1,0:T(8,128)(2,1)} %get-tuple-element.17.refs_1_) | copy-start | bytes 393220
  3.3 15.4 %all-to-all-start = ((bf16[16,32,128]{2,1,0:T(8,128)(2,1)}), bf16[16,32,128]{2,1,0:T(8,128)(2,1)S(1)}, u32[]{:S(2)}, u32[]{:S(2)}) async-start(bf16[16,32,128]{2,1,0:T(8,128)(2,1)} %bitcast.8), calls=%async_computation | async-start | bytes 262144 | tf_op jit(solution)/shard_map/all_to_all | solution.py:315
  10.8 7.9 %copy-start = (bf16[2,128,256]{2,1,0:T(8,128)(2,1)S(1)}, bf16[2,128,256]{2,1,0:T(8,128)(2,1)}, u32[]{:S(2)}) copy-start(bf16[2,128,256]{2,1,0:T(8,128)(2,1)} %get-tuple-element.16.refs_0_) | copy-start | bytes 393220
  11.0 0.7 %copy-start.4 = (bf16[8,4,128]{2,1,0:T(4,128)(2,1)S(1)}, bf16[8,4,128]{2,1,0:T(4,128)(2,1)}, u32[]{:S(2)}) copy-start(bf16[8,4,128]{2,1,0:T(4,128)(2,1)} %param.19) | copy-start | bytes 24580
  11.7 7.1 %copy-start.2 = (bf16[2,48,128]{2,1,0:T(8,128)(2,1)S(1)}, bf16[2,48,128]{2,1,0:T(8,128)(2,1)}, u32[]{:S(2)}) copy-start(bf16[2,48,128]{2,1,0:T(8,128)(2,1)} %get-tuple-element.18.refs_2_) | copy-start | bytes 73732
  27.3 10.4 %collective-permute-start.1 = (bf16[1152,128]{1,0:T(8,128)(2,1)S(1)}, bf16[1152,128]{1,0:T(8,128)(2,1)S(1)}, u32[]{:S(2)}, u32[]{:S(2)}) collective-permute-start(bf16[1152,128]{1,0:T(8,128)(2,1)S(1)} %get-tuple-element.21.refs_0_), channel_id=1, source_target_pairs={{0,1},{1,0},{2,3},{3,2},{4,5},{5,4},{6,7},{7,6},{8,9},{9,8},{10,11... | collective-permute-start | bytes 884744 | tf_op jit(solution)/shard_map/ppermute | solution.py:271
  27.4 10.3 %collective-permute-start = (bf16[1152,128]{1,0:T(8,128)(2,1)S(1)}, bf16[1152,128]{1,0:T(8,128)(2,1)S(1)}, u32[]{:S(2)}, u32[]{:S(2)}) collective-permute-start(bf16[1152,128]{1,0:T(8,128)(2,1)S(1)} %get-tuple-element.21.refs_0_), channel_id=1, source_target_pairs={{0,2},{2,0},{1,3},{3,1},{4,6},{6,4},{5,7},{7,5},{8,10},{10,8},{9,1... | collective-permute-start | bytes 884744 | tf_op jit(solution)/shard_map/ppermute | solution.py:271
  37.7 1.7 %collective-permute-start.2 = (bf16[1184,128]{1,0:T(8,128)(2,1)S(1)}, bf16[1184,128]{1,0:T(8,128)(2,1)S(1)}, u32[]{:S(2)}, u32[]{:S(2)}) collective-permute-start(bf16[1184,128]{1,0:T(8,128)(2,1)S(1)} %relay.1.refs_1_), channel_id=1, source_target_pairs={{0,1},{1,0},{2,3},{3,2},{4,5},{5,4},{6,7},{7,6},{8,9},{9,8},{10,11... | collective-permute-start | bytes 909320 | tf_op jit(solution)/shard_map/ppermute | solution.py:271

commit v4 on v3

--- a/solution.py
+++ b/solution.py
@@ -13,6 +13,7 @@
 ALL_VMEM_BYTES = 64 * 1024 * 1024
 SLACK_BYTES = 128 * 1024
 PART_AXES = ("rep", "sub")
+TOGETHER = 2
 RECORD = 16
 TANGENT_ROW = 8
 CAMERA_ROW = 12
@@ -122,94 +123,117 @@
     return jnp.concatenate([table[r:r + rows] for r in range(0, table.shape[0], rows)], axis=1)
 
 
-def backward_samples(n_cell, freq_count, codes_ref, w_out, weights, arrived, table_in, table_ref, kept, j):
+def chunk_steps(freq_count, kc, cols, rec, weights, code_part, w_out_t, kept, results):
     enc_s, gt_s, trunk_s, gc_s, act_s, rec_s = kept
-    w_enc, w_hidden, w_code = weights
-    blocks = arrived.shape[0] // n_cell
-    width = blocks * arrived.shape[2]
-    cams = codes_ref.shape[2]
-    hidden = w_hidden.shape[0]
+    w_enc, w_enc_t, w_hidden, w_hidden_t = weights
+    cams = code_part.shape[1] // 2
+    width = rec.shape[1]
     half = freq_count // 2
     scale = jnp.exp2(iota((half, 1), 0).astype(F32) * 0.25)
     top = 2.0 ** (half // 4)
-    for kc in range(n_cell):
-        cols = slice(kc * width, (kc + 1) * width)
-        rec = jnp.concatenate(
-            [arrived[kc * blocks + b, j * RECORD:(j + 1) * RECORD, :] for b in range(blocks)], axis=1
-        )
-        rec_s[:, cols] = rec
-        recf = rec.astype(F32)
-        coords = recf[0:4] + recf[4:8]
-        cam = recf[CAMERA_ROW:CAMERA_ROW + 1].astype(jnp.int32)
-        cam_hot = (iota((cams, width), 0) == cam).astype(F32).astype(BF16)
-        code_rows = dot_nn(codes_ref[kc], cam_hot).astype(BF16)
-        angles = jnp.concatenate([coords[i:i + 1] * scale for i in range(4)], axis=0)
-        s1, c1 = sin_cos(angles)
-        s2, c2 = s1, c1
-        for _ in range(half // 4):
-            s2, c2 = double_angle(s2, c2)
-        pieces = []
-        for a, b in ((s1, s2), (c1, c2)):
-            for i in range(4):
-                pieces += [a[i * half:(i + 1) * half], b[i * half:(i + 1) * half]]
-        encoded = jnp.concatenate(pieces, axis=0).astype(BF16)
-        enc_s[:, cols] = encoded
-        trunk, slope_trunk = soft(dot_tn(w_enc, encoded))
-        trunk = trunk.astype(BF16)
-        trunk_s[0:hidden, cols] = trunk
-        trunk_s[hidden:, cols] = code_rows
-        act, slope_color = soft(dot_tn(w_hidden, trunk) + dot_tn(w_code, code_rows))
-        act_s[:, cols] = act.astype(BF16)
-        gc = (dot_tn(w_out, rec) * slope_color).astype(BF16)
-        gc_s[:, cols] = gc
-        gt = (dot_nn(w_hidden, gc) * slope_trunk).astype(BF16)
-        gt_s[:, cols] = gt
-        grad_code = dot_nn(w_code, gc)
-        grad_enc = dot_nn(w_enc, gt)
-        sums = []
-        for i in range(3):
-            a, b = i * 2 * half, (4 + i) * 2 * half
-            at = slice(i * half, (i + 1) * half)
-            first = grad_enc[a:a + half] * c1[at] - grad_enc[b:b + half] * s1[at]
-            second = (grad_enc[a + half:a + 2 * half] * c2[at]
-                      - grad_enc[b + half:b + 2 * half] * s2[at])
-            sums.append(jnp.sum((first + top * second) * scale, axis=0, keepdims=True))
-        row = iota((RECORD, width), 0)
-        tail = jnp.where(row == 0, sums[0], jnp.where(row == 1, sums[1], jnp.where(row == 2, sums[2], 0.0)))
-        per_sample = jnp.concatenate([grad_code, tail], axis=0).astype(BF16)
-        table = dot_nt(per_sample, cam_hot)
-        if table_in is not None:
-            table = table + table_in[kc]
-        copies = table_ref.shape[0] // n_cell
-        for i in range(copies):
-            table_ref[kc * copies + i] = fold(table, table_ref.shape[1]).astype(table_ref.dtype)
-
-
-def sum_weights(kept, packed_ref):
-    enc_s, gt_s, trunk_s, gc_s, act_s, rec_s = kept
-    color = gc_s.shape[0]
-    g_enc = dot_nt(enc_s[...], gt_s[...]).astype(BF16)
-    enc_rows = g_enc.shape[0]
-    row = 0
-    for part in range(g_enc.shape[1] // color):
-        packed_ref[row:row + enc_rows, :] = g_enc[:, part * color:(part + 1) * color]
-        row += enc_rows
-    rows = trunk_s.shape[0]
-    packed_ref[row:row + rows, :] = dot_nt(trunk_s[...], gc_s[...]).astype(BF16)
-    row += rows
-    packed_ref[row:row + RECORD, :] = dot_nt(rec_s[...], act_s[...]).astype(BF16)
+    rec_s[:, cols] = rec
+    recf = rec.astype(F32)
+    coords = recf[0:4] + recf[4:8]
+    cam = recf[CAMERA_ROW:CAMERA_ROW + 1].astype(jnp.int32)
+    cam_hot = (iota((cams, width), 0) == cam).astype(F32).astype(BF16)
+    angles = jnp.concatenate([coords[i:i + 1] * scale for i in range(4)], axis=0)
+    s1, c1 = sin_cos(angles)
+    s2, c2 = s1, c1
+    for _ in range(half // 4):
+        s2, c2 = double_angle(s2, c2)
+    pieces = []
+    for a, b in ((s1, s2), (c1, c2)):
+        for i in range(4):
+            pieces += [a[i * half:(i + 1) * half], b[i * half:(i + 1) * half]]
+    encoded = jnp.concatenate(pieces, axis=0).astype(BF16)
+    enc_s[:, cols] = encoded
+    yield
+    trunk, slope_trunk = soft(dot_nn(w_enc_t, encoded))
+    trunk = trunk.astype(BF16)
+    trunk_s[:, cols] = trunk
+    yield
+    act, slope_color = soft(
+        dot_nn(w_hidden_t, trunk) + dot_nn(code_part, jnp.concatenate([cam_hot, cam_hot], axis=0))
+    )
+    act_s[:, cols] = act.astype(BF16)
+    gc = (dot_nn(w_out_t, rec) * slope_color).astype(BF16)
+    gc_s[:, cols] = gc
+    yield
+    gt = (dot_nn(w_hidden, gc) * slope_trunk).astype(BF16)
+    gt_s[:, cols] = gt
+    camera_color = dot_nt(cam_hot, gc)
+    yield
+    grad_enc = dot_nn(w_enc, gt)
+    sums = []
+    for i in range(3):
+        a, b = i * 2 * half, (4 + i) * 2 * half
+        at = slice(i * half, (i + 1) * half)
+        first = grad_enc[a:a + half] * c1[at] - grad_enc[b:b + half] * s1[at]
+        second = grad_enc[a + half:a + 2 * half] * c2[at] - grad_enc[b + half:b + 2 * half] * s2[at]
+        sums.append(jnp.sum((first + top * second) * scale, axis=0, keepdims=True))
+    row = iota((RECORD, width), 0)
+    tail = jnp.where(row == 0, sums[0], jnp.where(row == 1, sums[1], jnp.where(row == 2, sums[2], 0.0)))
+    results[kc] = (camera_color.astype(BF16), dot_nt(tail.astype(BF16), cam_hot))
 
 
 def cells_kernel(n_cell, freq_count, lc, codes_ref, w_out_ref, *refs):
-    weights, arrived = refs[:3], refs[3]
-    packed_ref, table_ref, kept, sums = refs[4], refs[5], refs[6:12], refs[12]
+    weights_refs, arrived = refs[:3], refs[3]
+    packed_ref, table_ref, kept_refs, sums = refs[4], refs[5], refs[6:12], refs[12]
     rows = packed_ref.shape[0] // lc
+    blocks = arrived.shape[0] // n_cell
+    width = blocks * arrived.shape[2]
+    cams = codes_ref.shape[1] // n_cell
     me_part = lax.axis_index(PART_AXES)
+    codes = codes_ref[...]
     for j in range(lc):
-        backward_samples(n_cell, freq_count, codes_ref, w_out_ref[me_part * lc + j], [w[j] for w in weights],
-                         arrived, sums if j else None, table_ref if j == lc - 1 else sums,
-                         [k.at[j] for k in kept], j)
-        sum_weights([k.at[j] for k in kept], packed_ref.at[j * rows:(j + 1) * rows])
+        kept = [k.at[j] for k in kept_refs]
+        enc_s, gt_s, trunk_s, gc_s, act_s, rec_s = kept
+        w_enc, w_hidden, w_code = (w[j] for w in weights_refs)
+        w_out_t = w_out_ref[me_part * lc + j].T
+        weights = (w_enc, w_enc.T, w_hidden, w_hidden.T)
+        coded = dot_tn(w_code, codes)
+        coded_high = coded.astype(BF16)
+        coded_low = (coded - coded_high.astype(F32)).astype(BF16)
+        results = [None] * n_cell
+        steps = []
+        for kc in range(n_cell):
+            rec = jnp.concatenate(
+                [arrived[kc * blocks + b, j * RECORD:(j + 1) * RECORD, :] for b in range(blocks)], axis=1
+            )
+            at = slice(kc * cams, (kc + 1) * cams)
+            code_part = jnp.concatenate([coded_high[:, at], coded_low[:, at]], axis=1)
+            cols = slice(kc * width, (kc + 1) * width)
+            steps.append(
+                chunk_steps(freq_count, kc, cols, rec, weights, code_part, w_out_t, kept, results)
+            )
+        for first in range(0, n_cell, TOGETHER):
+            live = steps[first:first + TOGETHER]
+            while live:
+                live = [step for step in live if next(step, live) is not live]
+        for kc in range(n_cell):
+            camera_color, camera_pose = results[kc]
+            table = jnp.concatenate([dot_nt(w_code, camera_color), camera_pose], axis=0)
+            if j:
+                table = table + sums[kc]
+            if j < lc - 1:
+                sums[kc] = table
+            else:
+                copies = table_ref.shape[0] // n_cell
+                for i in range(copies):
+                    table_ref[kc * copies + i] = fold(table, table_ref.shape[1]).astype(BF16)
+        row = j * rows
+        color = gc_s.shape[0]
+        g_enc = dot_nt(enc_s[...], gt_s[...]).astype(BF16)
+        for part in range(g_enc.shape[1] // color):
+            packed_ref[row:row + g_enc.shape[0], :] = g_enc[:, part * color:(part + 1) * color]
+            row += g_enc.shape[0]
+        hidden, code = trunk_s.shape[0], codes.shape[0]
+        packed_ref[row:row + hidden, :] = dot_nt(trunk_s[...], gc_s[...]).astype(BF16)
+        row += hidden
+        camera_color = jnp.concatenate([result[0] for result in results], axis=0)
+        packed_ref[row:row + code, :] = dot_nn(codes, camera_color).astype(BF16)
+        row += code
+        packed_ref[row:row + RECORD, :] = dot_nt(rec_s[...], act_s[...]).astype(BF16)
 
 
 def relay_kernel(tables_ref, packed_ref, _, out_ref):
@@ -309,7 +333,6 @@
         name="place",
     )(*inputs, *weights)
     sent, own_weights = placed[0], placed[1:]
-    codes_cell = codes.reshape(code, n_cell, cams).transpose(1, 0, 2)
     w_out_rows = jnp.pad(w_out, ((0, 0), (TANGENT_ROW, RECORD - TANGENT_ROW - w_out.shape[1]), (0, 0)))
 
     arrived = lax.all_to_all(
@@ -321,7 +344,7 @@
 
     packed_rows = enc * (hidden // color) + hidden + code + RECORD
     slots = n_cell * width
-    kept_rows = (enc, hidden, hidden + code, color, color, RECORD)
+    kept_rows = (enc, hidden, hidden, color, color, RECORD)
     table_shape = (n_cell, code + RECORD, cams)
     folded = (table_shape[1] * cams // color, color)
     packed, table = pl.pallas_call(
@@ -336,7 +359,7 @@
         compiler_params=params,
         cost_estimate=cost(10),
         name="cells",
-    )(codes_cell, w_out_rows, *own_weights, arrived)
+    )(codes, w_out_rows, *own_weights, arrived)
 
     over_rep = [exchange(packed, "rep", n_rep, kr) for kr in range(n_rep)]
     over_sub = [exchange(packed, "sub", n_sub, ks) for ks in range(n_sub)]

time: 41.2 us -> 40 us (0.971)
  Pallas kernels: 14.1 us -> 13 us
  waiting for transfers between devices: 7.27 us -> 8.06 us
  local copies, waits for them, and re-layouts: 0.81 us -> 0.04 us
    pallas_call x1, Pallas kernels: 8.5 us -> 7.41 us  [shards(): pl.pallas_call(functools.partial(cells_kernel, n_cell, freq_count, lc), i...]
    all_to_all x1, waiting for transfers between devices: 7.1 us -> 7.9 us  [shards(): lax.all_to_all(sent.reshape(n_cell * n_part, lc * RECORD, cap), ('cell',)...]
    unnamed x10, local copies, waits for them, and re-layouts: 0.7 us -> 0.03 us
  transfers between devices with their start and end apart: 4 -> 4, of which waited for: 2 -> 2; matrix products, arithmetic and copies ran while one was open for 0% -> 0% of each run, Pallas kernels for 3% -> 4%
where the time goes in v4:
time: 40 us; the launch traced here: 39.8 us
  Pallas kernels  13 us (32%)
  blocking collectives  10.3 us (26%)
  waiting for transfers between devices  8.06 us (20%)
  starting transfers between devices  7.63 us (19%)
  between operations  0.74 us (2%)
    all_to_all x1, blocking collectives, shards(): tables = lax.all_to_all(table, ('cell', 'rep'), 0, 0, tiled=True)  10.3 us
    all_to_all x1, waiting for transfers between devices, shards(): lax.all_to_all(sent.reshape(n_cell * n_part, lc * RECORD, cap), ('cell',)...  7.9 us
    all_to_all x1, starting transfers between devices, shards(): lax.all_to_all(sent.reshape(n_cell * n_part, lc * RECORD, cap), ('cell',)...  7.5 us
    pallas_call x1, Pallas kernels, shards(): pl.pallas_call(functools.partial(cells_kernel, n_cell, freq_count, lc), i...  7.41 us
    pallas_call x2, Pallas kernels, shards(): pl.pallas_call(functools.partial(unpack_kernel, tuple((place for place, _...  2.9 us
    pallas_call x1, Pallas kernels, shards(): pl.pallas_call(functools.partial(place_kernel, cells_all, cap, n_cell, n_...  2.66 us
  transfers between devices with their start and end apart: 4, of which 2 were waited for; matrix products, arithmetic and copies ran while one was open for 0% of the time, Pallas kernels for 4%

profile of v4, /device:TPU:0, one launch (start us, length us, event | category | flops | bytes accessed | tf_op | source)
XLA Modules:
  0.0 39.8 jit_solution(1524913877376385177)
XLA Ops:
  0.6 0.0 copy-start.4
  0.6 2.7 %place.1 = (bf16[512,128]{1,0:T(8,128)(2,1)}, bf16[2,128,256]{2,1,0:T(8,128)(2,1)}, bf16[2,256,128]{2,1,0:T(8,128)(2,1)}, bf16[2,48,128]{2,1,0:T(8,128)(2,1)}) custom-call(f32[4,2048]{1,0:T(4,128)} %refs_0_.1, f32[4,2048]{1,0:T(4,128)} %refs_1_.1, s32[1,2048]{1,0:T(1,128)} %bitcast.5, s32[1,2048]{1,0:T(1,128)} %bitcast.6, s32[1,2048]{1,0:T(1,128)} %bitcast.7, ...), custom_call_target="tpu_custom_call" | custom-call | flops 3000000000 | bytes 9000000 | tf_op jit(solution)/shard_map/place/pallas_call | solution.py:322
  3.3 0.0 copy-start.3
  3.3 0.0 copy-start.1
  3.3 0.0 copy-start.2
  3.4 7.5 %all-to-all-start = ((bf16[16,32,128]{2,1,0:T(8,128)(2,1)}), bf16[16,32,128]{2,1,0:T(8,128)(2,1)S(1)}, u32[]{:S(2)}, u32[]{:S(2)}) async-start(bf16[16,32,128]{2,1,0:T(8,128)(2,1)} %bitcast.4), calls=%async_computation | async-start | bytes 262144 | tf_op jit(solution)/shard_map/all_to_all | solution.py:338
  10.9 0.0 copy-done.4
  10.9 0.0 copy-start
  10.9 7.9 %all-to-all-done.refs_3_ = bf16[16,32,128]{2,1,0:T(8,128)(2,1)S(1)} async-done(((bf16[16,32,128]{2,1,0:T(8,128)(2,1)}), bf16[16,32,128]{2,1,0:T(8,128)(2,1)S(1)}, u32[]{:S(2)}, u32[]{:S(2)}) %all-to-all-start) | async-done | bytes 131104 | tf_op jit(solution)/shard_map/all_to_all | solution.py:338
  18.8 0.0 copy-done.3
  18.8 0.0 copy-done.1
  18.8 0.0 copy-done.2
  18.8 0.0 copy-done
  18.8 7.4 %cells.1 = (bf16[1152,128]{1,0:T(8,128)(2,1)S(1)}, bf16[8,32,128]{2,1,0:T(8,128)(2,1)S(1)}) custom-call(bf16[48,256]{1,0:T(8,128)(2,1)S(1)} %copy-done, bf16[8,16,128]{2,1,0:T(8,128)(2,1)S(1)} %pad.4.w_out_ref, bf16[2,128,256]{2,1,0:T(8,128)(2,1)S(1)} %copy-done.1, bf16[2,256,128]{2,1,0:T(8,128)(2,1)S(1)} %copy-done.2, bf16[2,48,128]{2,1,0:T(8,128)(2,1)S(1)} %copy-done.3, ...), custom_call_target="tpu_custom_call" | custom-call | flops 10000000000 | bytes 30000000 | tf_op jit(solution)/shard_map/cells/pallas_call | solution.py:350
  26.2 0.0 collective-permute-start.1
  26.2 0.1 collective-permute-start
  26.3 10.3 %all_to_all.10.tables_ref = bf16[8,32,128]{2,1,0:T(8,128)(2,1)S(1)} all-to-all(bf16[8,32,128]{2,1,0:T(8,128)(2,1)S(1)} %get-tuple-element.20), channel_id=1, replica_groups=mesh['groups'=2,'cell'=4,'rep'=2,'sub'=2] {'cell','rep'}, dimensions={0} | all-to-all | bytes 131072 | tf_op jit(solution)/shard_map/all_to_all | solution.py:366
  36.6 0.0 collective-permute-done.1._.refs_1_
  36.6 0.0 collective-permute-done.packed_ref.refs_2_
  36.6 0.1 collective-permute-start.2
  36.7 1.4 %unpack.2 = (f32[8,128,256]{2,1,0:T(8,128)}, f32[8,256,128]{2,1,0:T(8,128)}, f32[8,48,128]{2,1,0:T(8,128)}, f32[8,4,128]{2,1,0:T(4,128)}) custom-call(bf16[1152,128]{1,0:T(8,128)(2,1)S(1)} %get-tuple-element.21.refs_0_, bf16[1152,128]{1,0:T(8,128)(2,1)S(1)} %collective-permute-done.1._.refs_1_, bf16[1152,128]{1,0:T(8,128)(2,1)S(1)} %collective-permute-done.packed_ref.refs_2_), custom_call_target="tpu_custom_call" | custom-call | tf_op jit(solution)/shard_map/unpack/pallas_call | solution.py:400
  38.1 0.2 collective-permute-done.2.refs_0_
  38.3 1.5 %unpack.3 = (f32[8,128,256]{2,1,0:T(8,128)}, f32[8,256,128]{2,1,0:T(8,128)}, f32[8,48,128]{2,1,0:T(8,128)}, f32[8,4,128]{2,1,0:T(4,128)}, f32[3,64]{1,0:T(4,128)}, /*index=5*/f32[48,64]{1,0:T(8,128)}) custom-call(bf16[1184,128]{1,0:T(8,128)(2,1)S(1)} %collective-permute-done.2.refs_0_, ...), custom_call_target="tpu_custom_call", output_to_operand_aliasing={{0}: (2, {}), {1}: (3, {}), {2}: (4, {}), {3}: (5, {})} | custom-call | tf_op jit(solution)/shard_map/unpack/pallas_call | solution.py:400
  (2 shorter events, 0.0 us)
Async XLA Ops:
  0.6 10.2 %copy-start.4 = (bf16[8,4,128]{2,1,0:T(4,128)(2,1)S(1)}, bf16[8,4,128]{2,1,0:T(4,128)(2,1)}, u32[]{:S(2)}) copy-start(bf16[8,4,128]{2,1,0:T(4,128)(2,1)} %param.19) | copy-start | bytes 24580
  3.3 15.5 %copy-start.3 = (bf16[2,48,128]{2,1,0:T(8,128)(2,1)S(1)}, bf16[2,48,128]{2,1,0:T(8,128)(2,1)}, u32[]{:S(2)}) copy-start(bf16[2,48,128]{2,1,0:T(8,128)(2,1)} %get-tuple-element.18.refs_2_) | copy-start | bytes 73732
  3.3 15.5 %copy-start.1 = (bf16[2,128,256]{2,1,0:T(8,128)(2,1)S(1)}, bf16[2,128,256]{2,1,0:T(8,128)(2,1)}, u32[]{:S(2)}) copy-start(bf16[2,128,256]{2,1,0:T(8,128)(2,1)} %get-tuple-element.16.refs_0_) | copy-start | bytes 393220
  3.3 15.5 %copy-start.2 = (bf16[2,256,128]{2,1,0:T(8,128)(2,1)S(1)}, bf16[2,256,128]{2,1,0:T(8,128)(2,1)}, u32[]{:S(2)}) copy-start(bf16[2,256,128]{2,1,0:T(8,128)(2,1)} %get-tuple-element.17.refs_1_) | copy-start | bytes 393220
  3.4 15.4 %all-to-all-start = ((bf16[16,32,128]{2,1,0:T(8,128)(2,1)}), bf16[16,32,128]{2,1,0:T(8,128)(2,1)S(1)}, u32[]{:S(2)}, u32[]{:S(2)}) async-start(bf16[16,32,128]{2,1,0:T(8,128)(2,1)} %bitcast.4), calls=%async_computation | async-start | bytes 262144 | tf_op jit(solution)/shard_map/all_to_all | solution.py:338
  10.9 7.9 %copy-start = (bf16[48,256]{1,0:T(8,128)(2,1)S(1)}, bf16[48,256]{1,0:T(8,128)(2,1)}, u32[]{:S(2)}) copy-start(bf16[48,256]{1,0:T(8,128)(2,1)} %codes_ref.1) | copy-start | bytes 73732
  26.2 10.4 %collective-permute-start.1 = (bf16[1152,128]{1,0:T(8,128)(2,1)S(1)}, bf16[1152,128]{1,0:T(8,128)(2,1)S(1)}, u32[]{:S(2)}, u32[]{:S(2)}) collective-permute-start(bf16[1152,128]{1,0:T(8,128)(2,1)S(1)} %get-tuple-element.21.refs_0_), channel_id=1, source_target_pairs={{0,1},{1,0},{2,3},{3,2},{4,5},{5,4},{6,7},{7,6},{8,9},{9,8},{10,11... | collective-permute-start | bytes 884744 | tf_op jit(solution)/shard_map/ppermute | solution.py:295
  26.2 10.4 %collective-permute-start = (bf16[1152,128]{1,0:T(8,128)(2,1)S(1)}, bf16[1152,128]{1,0:T(8,128)(2,1)S(1)}, u32[]{:S(2)}, u32[]{:S(2)}) collective-permute-start(bf16[1152,128]{1,0:T(8,128)(2,1)S(1)} %get-tuple-element.21.refs_0_), channel_id=1, source_target_pairs={{0,2},{2,0},{1,3},{3,1},{4,6},{6,4},{5,7},{7,5},{8,10},{10,8},{9,1... | collective-permute-start | bytes 884744 | tf_op jit(solution)/shard_map/ppermute | solution.py:295
  36.6 1.7 %collective-permute-start.2 = (bf16[1184,128]{1,0:T(8,128)(2,1)S(1)}, bf16[1184,128]{1,0:T(8,128)(2,1)S(1)}, u32[]{:S(2)}, u32[]{:S(2)}) collective-permute-start(bf16[1184,128]{1,0:T(8,128)(2,1)S(1)} %relay.1.refs_1_), channel_id=1, source_target_pairs={{0,1},{1,0},{2,3},{3,2},{4,5},{5,4},{6,7},{7,6},{8,9},{9,8},{10,11... | collective-permute-start | bytes 909320 | tf_op jit(solution)/shard_map/ppermute | solution.py:295

commit v5 on v4

--- a/solution.py
+++ b/solution.py
@@ -85,7 +85,9 @@
     rank_hot = (iota((cap, n), 0) == rank).astype(F32).astype(BF16)
     cell_rows = jnp.broadcast_to(cell_of, (RECORD, n))
     for c in range(cells_all):
-        spread[c * RECORD:(c + 1) * RECORD, :] = jnp.where(cell_rows == c, record, 0.0).astype(BF16)
+        owner_cell, owner_part, j = c // (n_part * lc), c // lc % n_part, c % lc
+        slot = (owner_part * n_cell + owner_cell) * lc + j
+        spread[slot * RECORD:(slot + 1) * RECORD, :] = jnp.where(cell_rows == c, record, 0.0).astype(BF16)
     placed[...] = dot_nt(spread[...], rank_hot).astype(BF16)
     for copy in copies[6:]:
         copy.wait()
@@ -176,35 +178,46 @@
     results[kc] = (camera_color.astype(BF16), dot_nt(tail.astype(BF16), cam_hot))
 
 
-def cells_kernel(n_cell, freq_count, lc, codes_ref, w_out_ref, *refs):
-    weights_refs, arrived = refs[:3], refs[3]
-    packed_ref, table_ref, kept_refs, sums = refs[4], refs[5], refs[6:12], refs[12]
+def prepare_kernel(n_cell, codes_ref, w_out_ref, w_enc_ref, w_hidden_ref, w_code_ref,
+                   w_enc_t_ref, w_hidden_t_ref, w_out_t_ref, coded_ref):
+    me_part = lax.axis_index(PART_AXES)
+    lc = w_enc_ref.shape[0]
+    cams = codes_ref.shape[1] // n_cell
+    for j in range(lc):
+        w_enc_t_ref[j] = w_enc_ref[j].T
+        w_hidden_t_ref[j] = w_hidden_ref[j].T
+        w_out_t_ref[j] = w_out_ref[me_part * lc + j].T
+        coded = dot_tn(w_code_ref[j], codes_ref[...])
+        high = coded.astype(BF16)
+        low = (coded - high.astype(F32)).astype(BF16)
+        for kc in range(n_cell):
+            at = slice(kc * cams, (kc + 1) * cams)
+            coded_ref[j, kc] = jnp.concatenate([high[:, at], low[:, at]], axis=1)
+
+
+def cells_kernel(n_cell, freq_count, lc, codes_ref, *refs):
+    weights_refs, turned_refs, arrived = refs[:3], refs[3:7], refs[7]
+    packed_ref, table_ref, kept_refs, sums = refs[8], refs[9], refs[10:16], refs[16]
     rows = packed_ref.shape[0] // lc
     blocks = arrived.shape[0] // n_cell
     width = blocks * arrived.shape[2]
-    cams = codes_ref.shape[1] // n_cell
-    me_part = lax.axis_index(PART_AXES)
     codes = codes_ref[...]
     for j in range(lc):
         kept = [k.at[j] for k in kept_refs]
         enc_s, gt_s, trunk_s, gc_s, act_s, rec_s = kept
         w_enc, w_hidden, w_code = (w[j] for w in weights_refs)
-        w_out_t = w_out_ref[me_part * lc + j].T
-        weights = (w_enc, w_enc.T, w_hidden, w_hidden.T)
-        coded = dot_tn(w_code, codes)
-        coded_high = coded.astype(BF16)
-        coded_low = (coded - coded_high.astype(F32)).astype(BF16)
+        w_enc_t, w_hidden_t, w_out_t, coded = (w.at[j] for w in turned_refs)
+        w_out_t = w_out_t[...]
+        weights = (w_enc, w_enc_t[...], w_hidden, w_hidden_t[...])
         results = [None] * n_cell
         steps = []
         for kc in range(n_cell):
             rec = jnp.concatenate(
-                [arrived[kc * blocks + b, j * RECORD:(j + 1) * RECORD, :] for b in range(blocks)], axis=1
+                [arrived[b * n_cell + kc, j * RECORD:(j + 1) * RECORD, :] for b in range(blocks)], axis=1
             )
-            at = slice(kc * cams, (kc + 1) * cams)
-            code_part = jnp.concatenate([coded_high[:, at], coded_low[:, at]], axis=1)
             cols = slice(kc * width, (kc + 1) * width)
             steps.append(
-                chunk_steps(freq_count, kc, cols, rec, weights, code_part, w_out_t, kept, results)
+                chunk_steps(freq_count, kc, cols, rec, weights, coded[kc], w_out_t, kept, results)
             )
         for first in range(0, n_cell, TOGETHER):
             live = steps[first:first + TOGETHER]
@@ -247,40 +260,45 @@
     if tables_at:
         here, refs = refs[0], refs[1:]
     outs, refs = refs[n_prev:n_prev + 4], refs[n_prev + 4:]
-    code = outs[2].shape[1]
-    if tables_at:
-        cams = refs[0].shape[1]
-        first = lc * packed_rows
-        total = here[first:, :].astype(F32)
-        for i in tables_at:
-            total = total + ins[i][first:, :].astype(F32)
-        total = jnp.concatenate([total[:, c:c + cams] for c in range(0, total.shape[1], cams)], axis=0)
-        refs[0][...] = total[code:code + 3]
-        refs[1][...] = total[0:code]
-        refs = refs[2:]
+    camera_outs, refs = (refs[:2], refs[2:]) if tables_at else ((), refs)
     wide, sems = refs[:-1], refs[-1]
     enc_v, hidden_v, code_v, out_v = wide
     enc_rows, enc_cols = enc_v.shape[1:]
     hidden, color = hidden_v.shape[1:]
-    out_rows = out_v.shape[1]
+    code, out_rows = code_v.shape[1], out_v.shape[1]
     me_part = lax.axis_index(PART_AXES)
     copies = []
     for i in range(len(places) * lc):
         cell = (me_part ^ places[i // lc]) * lc + i % lc
         src = ins[i // lc]
         row = i % lc * packed_rows
+
+        def send(m):
+            copy = pltpu.make_async_copy(wide[m].at[i], outs[m].at[cell], sems.at[i, m])
+            copy.start()
+            copies.append(copy)
+
         for part in range(enc_cols // color):
             enc_v[i, :, part * color:(part + 1) * color] = src[row:row + enc_rows, :].astype(F32)
             row += enc_rows
+        send(0)
         hidden_v[i] = src[row:row + hidden, :].astype(F32)
         row += hidden
+        send(1)
         code_v[i] = src[row:row + code, :].astype(F32)
         row += code
         out_v[i] = src[row:row + RECORD, :].astype(F32)[TANGENT_ROW:TANGENT_ROW + out_rows]
-        for m in range(4):
-            copy = pltpu.make_async_copy(wide[m].at[i], outs[m].at[cell], sems.at[i, m])
-            copy.start()
-            copies.append(copy)
+        send(2)
+        send(3)
+    if tables_at:
+        cams = camera_outs[0].shape[1]
+        first = lc * packed_rows
+        total = here[first:, :].astype(F32)
+        for i in tables_at:
+            total = total + ins[i][first:, :].astype(F32)
+        total = jnp.concatenate([total[:, c:c + cams] for c in range(0, total.shape[1], cams)], axis=0)
+        camera_outs[0][...] = total[code:code + 3]
+        camera_outs[1][...] = total[0:code]
     for copy in copies:
         copy.wait()
 
@@ -336,10 +354,10 @@
     w_out_rows = jnp.pad(w_out, ((0, 0), (TANGENT_ROW, RECORD - TANGENT_ROW - w_out.shape[1]), (0, 0)))
 
     arrived = lax.all_to_all(
-        sent.reshape(n_cell * n_part, lc * RECORD, cap), ("cell",) + PART_AXES, 0, 0, tiled=True
+        sent.reshape(n_cell * n_part, lc * RECORD, cap), PART_AXES + ("cell",), 0, 0, tiled=True
     )
     if cap % 128:
-        arrived = arrived.reshape(n_cell, n_part, lc * RECORD, cap).transpose(0, 2, 1, 3)
+        arrived = arrived.reshape(n_part, n_cell, lc * RECORD, cap).transpose(1, 2, 0, 3)
         arrived = arrived.reshape(n_cell, lc * RECORD, width)
 
     packed_rows = enc * (hidden // color) + hidden + code + RECORD
@@ -347,9 +365,23 @@
     kept_rows = (enc, hidden, hidden, color, color, RECORD)
     table_shape = (n_cell, code + RECORD, cams)
     folded = (table_shape[1] * cams // color, color)
+    turned = pl.pallas_call(
+        functools.partial(prepare_kernel, n_cell),
+        in_specs=[vmem] * 5,
+        out_specs=[vmem] * 4,
+        out_shape=[
+            jax.ShapeDtypeStruct((lc, hidden, enc), BF16),
+            jax.ShapeDtypeStruct((lc, color, hidden), BF16),
+            jax.ShapeDtypeStruct((lc, color, RECORD), BF16),
+            jax.ShapeDtypeStruct((lc, n_cell, color, 2 * cams), BF16),
+        ],
+        compiler_params=params,
+        cost_estimate=cost(2),
+        name="prepare",
+    )(codes, w_out_rows, *own_weights)
     packed, table = pl.pallas_call(
         functools.partial(cells_kernel, n_cell, freq_count, lc),
-        in_specs=[vmem] * 6,
+        in_specs=[vmem] * 9,
         out_specs=[vmem, vmem],
         out_shape=[
             jax.ShapeDtypeStruct((lc * packed_rows, color), BF16),
@@ -359,7 +391,7 @@
         compiler_params=params,
         cost_estimate=cost(10),
         name="cells",
-    )(codes, w_out_rows, *own_weights, arrived)
+    )(codes, *own_weights, *turned, arrived)
 
     over_rep = [exchange(packed, "rep", n_rep, kr) for kr in range(n_rep)]
     over_sub = [exchange(packed, "sub", n_sub, ks) for ks in range(n_sub)]

time: 40 us -> 39.5 us (0.988)
  waiting for transfers between devices: 8.06 us -> 6.42 us
  starting transfers between devices: 7.63 us -> 8.59 us
  blocking collectives: 10.3 us -> 9.44 us
  local copies, waits for them, and re-layouts: 0.04 us -> 0.72 us
    all_to_all x1, waiting for transfers between devices: 7.9 us -> 6.26 us  [shards(): lax.all_to_all(sent.reshape(n_cell * n_part, lc * RECORD, cap), PART_AXES...]
    ppermute x3, starting transfers between devices: 0.13 us -> 1.09 us  [exchange(): return lax.ppermute(value, axes, [(i, i ^ k) for i in range(count)])]
    all_to_all x1, blocking collectives: 10.3 us -> 9.44 us  [shards(): tables = lax.all_to_all(table, ('cell', 'rep'), 0, 0, tiled=True)]
    unnamed x10, local copies, waits for them, and re-layouts: 0.03 us -> 0.71 us
where the time goes in v5:
time: 39.5 us; the launch traced here: 39.2 us
  Pallas kernels  13.2 us (33%)
  blocking collectives  9.44 us (24%)
  starting transfers between devices  8.59 us (22%)
  waiting for transfers between devices  6.42 us (16%)
  between operations  0.76 us (2%)
  local copies, waits for them, and re-layouts  0.72 us (2%)
    all_to_all x1, blocking collectives, shards(): tables = lax.all_to_all(table, ('cell', 'rep'), 0, 0, tiled=True)  9.44 us
    all_to_all x1, starting transfers between devices, shards(): lax.all_to_all(sent.reshape(n_cell * n_part, lc * RECORD, cap), PART_AXES...  7.5 us
    pallas_call x1, Pallas kernels, shards(): pl.pallas_call(functools.partial(cells_kernel, n_cell, freq_count, lc), i...  7.29 us
    all_to_all x1, waiting for transfers between devices, shards(): lax.all_to_all(sent.reshape(n_cell * n_part, lc * RECORD, cap), PART_AXES...  6.26 us
    pallas_call x2, Pallas kernels, shards(): pl.pallas_call(functools.partial(unpack_kernel, tuple((place for place, _...  2.9 us
    pallas_call x1, Pallas kernels, shards(): pl.pallas_call(functools.partial(place_kernel, cells_all, cap, n_cell, n_...  2.66 us
    ppermute x3, starting transfers between devices, exchange(): return lax.ppermute(value, axes, [(i, i ^ k) for i in range(count)])  1.09 us
  transfers between devices with their start and end apart: 4, of which 2 were waited for; matrix products, arithmetic and copies ran while one was open for 0% of the time, Pallas kernels for 4%

profile of v5, /device:TPU:0, one launch (start us, length us, event | category | flops | bytes accessed | tf_op | source)
XLA Modules:
  0.0 39.2 jit_solution(8469281942877435697)
XLA Ops:
  0.6 0.0 copy-start.4
  0.6 2.7 %place.1 = (bf16[512,128]{1,0:T(8,128)(2,1)}, bf16[2,128,256]{2,1,0:T(8,128)(2,1)}, bf16[2,256,128]{2,1,0:T(8,128)(2,1)}, bf16[2,48,128]{2,1,0:T(8,128)(2,1)}) custom-call(f32[4,2048]{1,0:T(4,128)} %refs_0_.1, f32[4,2048]{1,0:T(4,128)} %refs_1_.1, s32[1,2048]{1,0:T(1,128)} %bitcast.5, s32[1,2048]{1,0:T(1,128)} %bitcast.6, s32[1,2048]{1,0:T(1,128)} %bitcast.7, ...), custom_call_target="tpu_custom_call" | custom-call | flops 3000000000 | bytes 9000000 | tf_op jit(solution)/shard_map/place/pallas_call | solution.py:340
  3.3 0.0 copy-start.3
  3.3 0.0 copy-start.1
  3.3 0.0 copy-start.2
  3.4 7.5 %all-to-all-start = ((bf16[16,32,128]{2,1,0:T(8,128)(2,1)}), bf16[16,32,128]{2,1,0:T(8,128)(2,1)S(1)}, u32[]{:S(2)}, u32[]{:S(2)}) async-start(bf16[16,32,128]{2,1,0:T(8,128)(2,1)} %bitcast.4), calls=%async_computation | async-start | bytes 262144 | tf_op jit(solution)/shard_map/all_to_all | solution.py:356
  10.9 0.0 copy-done.4
  10.9 0.0 copy-start
  10.9 0.0 copy-done.3
  10.9 0.0 copy-done.1
  10.9 0.0 copy-done.2
  10.9 0.7 %copy-done = bf16[48,256]{1,0:T(8,128)(2,1)S(1)} copy-done((bf16[48,256]{1,0:T(8,128)(2,1)S(1)}, bf16[48,256]{1,0:T(8,128)(2,1)}, u32[]{:S(2)}) %copy-start) | copy-done | bytes 24600
  11.6 0.3 prepare.1
  12.0 6.3 %all-to-all-done.refs_7_ = bf16[16,32,128]{2,1,0:T(8,128)(2,1)S(1)} async-done(((bf16[16,32,128]{2,1,0:T(8,128)(2,1)}), bf16[16,32,128]{2,1,0:T(8,128)(2,1)S(1)}, u32[]{:S(2)}, u32[]{:S(2)}) %all-to-all-start) | async-done | bytes 131104 | tf_op jit(solution)/shard_map/all_to_all | solution.py:356
  18.2 7.3 %cells.1 = (bf16[1152,128]{1,0:T(8,128)(2,1)S(1)}, bf16[8,32,128]{2,1,0:T(8,128)(2,1)S(1)}) custom-call(bf16[48,256]{1,0:T(8,128)(2,1)S(1)} %copy-done, bf16[2,128,256]{2,1,0:T(8,128)(2,1)S(1)} %copy-done.1, bf16[2,256,128]{2,1,0:T(8,128)(2,1)S(1)} %copy-done.2, bf16[2,48,128]{2,1,0:T(8,128)(2,1)S(1)} %copy-done.3, ...), custom_call_target="tpu_custom_call" | custom-call | flops 10000000000 | bytes 30000000 | tf_op jit(solution)/shard_map/cells/pallas_call | solution.py:382
  25.5 0.1 collective-permute-start.1
  25.7 0.9 %collective-permute-start = (bf16[1152,128]{1,0:T(8,128)(2,1)S(1)}, bf16[1152,128]{1,0:T(8,128)(2,1)S(1)}, u32[]{:S(2)}, u32[]{:S(2)}) collective-permute-start(bf16[1152,128]{1,0:T(8,128)(2,1)S(1)} %get-tuple-element.29.refs_0_), channel_id=1, source_target_pairs={{0,2},{2,0},{1,3},{3,1},{4,6},{6,4},{5,7},{7,5},{8,10},{10,8},{9,1... | collective-permute-start | bytes 884744 | tf_op jit(solution)/shard_map/ppermute | solution.py:313
  26.5 9.4 %all_to_all.10.tables_ref = bf16[8,32,128]{2,1,0:T(8,128)(2,1)S(1)} all-to-all(bf16[8,32,128]{2,1,0:T(8,128)(2,1)S(1)} %get-tuple-element.28), channel_id=1, replica_groups=mesh['groups'=2,'cell'=4,'rep'=2,'sub'=2] {'cell','rep'}, dimensions={0} | all-to-all | bytes 131072 | tf_op jit(solution)/shard_map/all_to_all | solution.py:398
  36.0 0.0 collective-permute-done.1._.refs_1_
  36.0 0.0 collective-permute-done.packed_ref.refs_2_
  36.0 0.1 collective-permute-start.2
  36.1 1.4 %unpack.2 = (f32[8,128,256]{2,1,0:T(8,128)}, f32[8,256,128]{2,1,0:T(8,128)}, f32[8,48,128]{2,1,0:T(8,128)}, f32[8,4,128]{2,1,0:T(4,128)}) custom-call(bf16[1152,128]{1,0:T(8,128)(2,1)S(1)} %get-tuple-element.29.refs_0_, bf16[1152,128]{1,0:T(8,128)(2,1)S(1)} %collective-permute-done.1._.refs_1_, bf16[1152,128]{1,0:T(8,128)(2,1)S(1)} %collective-permute-done.packed_ref.refs_2_), custom_call_target="tpu_custom_call" | custom-call | tf_op jit(solution)/shard_map/unpack/pallas_call | solution.py:432
  37.5 0.2 collective-permute-done.2.refs_0_
  37.7 1.5 %unpack.3 = (f32[8,128,256]{2,1,0:T(8,128)}, f32[8,256,128]{2,1,0:T(8,128)}, f32[8,48,128]{2,1,0:T(8,128)}, f32[8,4,128]{2,1,0:T(4,128)}, f32[3,64]{1,0:T(4,128)}, /*index=5*/f32[48,64]{1,0:T(8,128)}) custom-call(bf16[1184,128]{1,0:T(8,128)(2,1)S(1)} %collective-permute-done.2.refs_0_, ...), custom_call_target="tpu_custom_call", output_to_operand_aliasing={{0}: (2, {}), {1}: (3, {}), {2}: (4, {}), {3}: (5, {})} | custom-call | tf_op jit(solution)/shard_map/unpack/pallas_call | solution.py:432
  (2 shorter events, 0.0 us)
Async XLA Ops:
  0.6 10.2 %copy-start.4 = (bf16[8,4,128]{2,1,0:T(4,128)(2,1)S(1)}, bf16[8,4,128]{2,1,0:T(4,128)(2,1)}, u32[]{:S(2)}) copy-start(bf16[8,4,128]{2,1,0:T(4,128)(2,1)} %param.19) | copy-start | bytes 24580
  3.3 7.6 %copy-start.3 = (bf16[2,48,128]{2,1,0:T(8,128)(2,1)S(1)}, bf16[2,48,128]{2,1,0:T(8,128)(2,1)}, u32[]{:S(2)}) copy-start(bf16[2,48,128]{2,1,0:T(8,128)(2,1)} %get-tuple-element.22.w_code_ref.refs_2_) | copy-start | bytes 73732
  3.3 7.6 %copy-start.1 = (bf16[2,128,256]{2,1,0:T(8,128)(2,1)S(1)}, bf16[2,128,256]{2,1,0:T(8,128)(2,1)}, u32[]{:S(2)}) copy-start(bf16[2,128,256]{2,1,0:T(8,128)(2,1)} %get-tuple-element.20.w_enc_ref.refs_0_) | copy-start | bytes 393220
  3.3 7.6 %copy-start.2 = (bf16[2,256,128]{2,1,0:T(8,128)(2,1)S(1)}, bf16[2,256,128]{2,1,0:T(8,128)(2,1)}, u32[]{:S(2)}) copy-start(bf16[2,256,128]{2,1,0:T(8,128)(2,1)} %get-tuple-element.21.w_hidden_ref.refs_1_) | copy-start | bytes 393220
  3.4 14.9 %all-to-all-start = ((bf16[16,32,128]{2,1,0:T(8,128)(2,1)}), bf16[16,32,128]{2,1,0:T(8,128)(2,1)S(1)}, u32[]{:S(2)}, u32[]{:S(2)}) async-start(bf16[16,32,128]{2,1,0:T(8,128)(2,1)} %bitcast.4), calls=%async_computation | async-start | bytes 262144 | tf_op jit(solution)/shard_map/all_to_all | solution.py:356
  10.9 0.7 %copy-start = (bf16[48,256]{1,0:T(8,128)(2,1)S(1)}, bf16[48,256]{1,0:T(8,128)(2,1)}, u32[]{:S(2)}) copy-start(bf16[48,256]{1,0:T(8,128)(2,1)} %codes_ref.3) | copy-start | bytes 73732
  25.5 10.5 %collective-permute-start.1 = (bf16[1152,128]{1,0:T(8,128)(2,1)S(1)}, bf16[1152,128]{1,0:T(8,128)(2,1)S(1)}, u32[]{:S(2)}, u32[]{:S(2)}) collective-permute-start(bf16[1152,128]{1,0:T(8,128)(2,1)S(1)} %get-tuple-element.29.refs_0_), channel_id=1, source_target_pairs={{0,1},{1,0},{2,3},{3,2},{4,5},{5,4},{6,7},{7,6},{8,9},{9,8},{10,11... | collective-permute-start | bytes 884744 | tf_op jit(solution)/shard_map/ppermute | solution.py:313
  25.7 10.3 %collective-permute-start = (bf16[1152,128]{1,0:T(8,128)(2,1)S(1)}, bf16[1152,128]{1,0:T(8,128)(2,1)S(1)}, u32[]{:S(2)}, u32[]{:S(2)}) collective-permute-start(bf16[1152,128]{1,0:T(8,128)(2,1)S(1)} %get-tuple-element.29.refs_0_), channel_id=1, source_target_pairs={{0,2},{2,0},{1,3},{3,1},{4,6},{6,4},{5,7},{7,5},{8,10},{10,8},{9,1... | collective-permute-start | bytes 884744 | tf_op jit(solution)/shard_map/ppermute | solution.py:313
  36.0 1.7 %collective-permute-start.2 = (bf16[1184,128]{1,0:T(8,128)(2,1)S(1)}, bf16[1184,128]{1,0:T(8,128)(2,1)S(1)}, u32[]{:S(2)}, u32[]{:S(2)}) collective-permute-start(bf16[1184,128]{1,0:T(8,128)(2,1)S(1)} %relay.1.refs_1_), channel_id=1, source_target_pairs={{0,1},{1,0},{2,3},{3,2},{4,5},{5,4},{6,7},{7,6},{8,9},{9,8},{10,11... | collective-permute-start | bytes 909320 | tf_op jit(solution)/shard_map/ppermute | solution.py:313

commit v6 on v5

--- a/solution.py
+++ b/solution.py
@@ -36,18 +36,16 @@
 
 
 def place_kernel(cells_all, cap, n_cell, n_part, *refs):
-    sources, weights, placed, own = refs[:6], refs[6:9], refs[9], refs[10:13]
-    arrays, (spread, sems) = refs[13:19], refs[19:]
+    sources, placed, arrays, (spread, sems) = refs[:6], refs[6], refs[7:13], refs[13:]
     points_ref, cot_ref, cell_ref, cam_ref, valid_ref, poses_ref = arrays
-    me_part = lax.axis_index(PART_AXES)
     lc = cells_all // (n_cell * n_part)
-    pairs = list(zip(sources, arrays)) + [
-        (source.at[pl.ds(me_part * lc, lc)], target) for source, target in zip(weights, own)
+    copies = [
+        pltpu.make_async_copy(source, target, sems.at[i])
+        for i, (source, target) in enumerate(zip(sources, arrays))
     ]
-    copies = [pltpu.make_async_copy(source, target, sems.at[i]) for i, (source, target) in enumerate(pairs)]
     for copy in copies:
         copy.start()
-    for copy in copies[:6]:
+    for copy in copies:
         copy.wait()
     n = points_ref.shape[1]
     cams = poses_ref.shape[1]
@@ -89,8 +87,6 @@
         slot = (owner_part * n_cell + owner_cell) * lc + j
         spread[slot * RECORD:(slot + 1) * RECORD, :] = jnp.where(cell_rows == c, record, 0.0).astype(BF16)
     placed[...] = dot_nt(spread[...], rank_hot).astype(BF16)
-    for copy in copies[6:]:
-        copy.wait()
 
 
 def sin_cos(x):
@@ -178,11 +174,20 @@
     results[kc] = (camera_color.astype(BF16), dot_nt(tail.astype(BF16), cam_hot))
 
 
-def prepare_kernel(n_cell, codes_ref, w_out_ref, w_enc_ref, w_hidden_ref, w_code_ref,
-                   w_enc_t_ref, w_hidden_t_ref, w_out_t_ref, coded_ref):
+def prepare_kernel(n_cell, codes_ref, w_out_ref, *refs):
+    sources, own, (w_enc_t_ref, w_hidden_t_ref, w_out_t_ref, coded_ref, sems) = refs[:3], refs[3:6], refs[6:]
+    w_enc_ref, w_hidden_ref, w_code_ref = own
     me_part = lax.axis_index(PART_AXES)
     lc = w_enc_ref.shape[0]
     cams = codes_ref.shape[1] // n_cell
+    copies = [
+        pltpu.make_async_copy(source.at[pl.ds(me_part * lc, lc)], target, sems.at[i])
+        for i, (source, target) in enumerate(zip(sources, own))
+    ]
+    for copy in copies:
+        copy.start()
+    for copy in copies:
+        copy.wait()
     for j in range(lc):
         w_enc_t_ref[j] = w_enc_ref[j].T
         w_hidden_t_ref[j] = w_hidden_ref[j].T
@@ -333,24 +338,20 @@
 
     inputs = (points, cotangent, cell_ids.reshape(1, n), camera_ids.reshape(1, n), valid.reshape(1, n), poses)
     weights = (w_enc, w_hidden, w_code)
-    out_shape = [jax.ShapeDtypeStruct((cells_all * RECORD, cap), BF16)] + [
-        jax.ShapeDtypeStruct((lc,) + w.shape[1:], BF16) for w in weights
-    ]
-    room = sum(2 * a.size // a.shape[-1] * max(a.shape[-1], 128) for a in out_shape) + SLACK_BYTES
-    placed = pl.pallas_call(
+    slots_all = cells_all * RECORD
+    room = 2 * slots_all * max(cap, 128) + SLACK_BYTES
+    sent = pl.pallas_call(
         functools.partial(place_kernel, cells_all, cap, n_cell, n_part),
-        out_shape=out_shape,
-        in_specs=[hbm] * 9,
-        out_specs=[vmem] * len(out_shape),
-        scratch_shapes=[pltpu.VMEM(a.shape, a.dtype) for a in inputs] + [
-            pltpu.VMEM((cells_all * RECORD, n), BF16),
-            pltpu.SemaphoreType.DMA((9,)),
-        ],
+        out_shape=jax.ShapeDtypeStruct((slots_all, cap), BF16),
+        in_specs=[hbm] * 6,
+        out_specs=vmem,
+        scratch_shapes=[pltpu.VMEM(a.shape, a.dtype) for a in inputs]
+        + [pltpu.VMEM((slots_all, n), BF16), pltpu.SemaphoreType.DMA((6,))],
         compiler_params=pltpu.CompilerParams(vmem_limit_bytes=ALL_VMEM_BYTES - room),
         cost_estimate=cost(3),
         name="place",
-    )(*inputs, *weights)
-    sent, own_weights = placed[0], placed[1:]
+    )(*inputs)
+
     w_out_rows = jnp.pad(w_out, ((0, 0), (TANGENT_ROW, RECORD - TANGENT_ROW - w_out.shape[1]), (0, 0)))
 
     arrived = lax.all_to_all(
@@ -365,20 +366,21 @@
     kept_rows = (enc, hidden, hidden, color, color, RECORD)
     table_shape = (n_cell, code + RECORD, cams)
     folded = (table_shape[1] * cams // color, color)
-    turned = pl.pallas_call(
+    own_weights = pl.pallas_call(
         functools.partial(prepare_kernel, n_cell),
-        in_specs=[vmem] * 5,
-        out_specs=[vmem] * 4,
-        out_shape=[
+        in_specs=[vmem] * 2 + [hbm] * 3,
+        out_specs=[vmem] * 7,
+        out_shape=[jax.ShapeDtypeStruct((lc,) + w.shape[1:], BF16) for w in weights] + [
             jax.ShapeDtypeStruct((lc, hidden, enc), BF16),
             jax.ShapeDtypeStruct((lc, color, hidden), BF16),
             jax.ShapeDtypeStruct((lc, color, RECORD), BF16),
             jax.ShapeDtypeStruct((lc, n_cell, color, 2 * cams), BF16),
         ],
+        scratch_shapes=[pltpu.SemaphoreType.DMA((3,))],
         compiler_params=params,
         cost_estimate=cost(2),
         name="prepare",
-    )(codes, w_out_rows, *own_weights)
+    )(codes, w_out_rows, *weights)
     packed, table = pl.pallas_call(
         functools.partial(cells_kernel, n_cell, freq_count, lc),
         in_specs=[vmem] * 9,
@@ -391,7 +393,7 @@
         compiler_params=params,
         cost_estimate=cost(10),
         name="cells",
-    )(codes, *own_weights, *turned, arrived)
+    )(codes, *own_weights, arrived)
 
     over_rep = [exchange(packed, "rep", n_rep, kr) for kr in range(n_rep)]
     over_sub = [exchange(packed, "sub", n_sub, ks) for ks in range(n_sub)]

time: 39.5 us -> 39.5 us (level)
  waiting for transfers between devices: 6.42 us -> 3.97 us
  local copies, waits for them, and re-layouts: 0.72 us -> 2.81 us
    all_to_all x1, waiting for transfers between devices: 6.26 us -> 3.8 us  [shards(): lax.all_to_all(sent.reshape(n_cell * n_part, lc * RECORD, cap), PART_AXES...]
    unnamed x10, local copies, waits for them, and re-layouts: 0.71 us -> 2.8 us
  transfers between devices with their start and end apart: 4 -> 4, of which waited for: 2 -> 2; matrix products, arithmetic and copies ran while one was open for 0% -> 0% of each run, Pallas kernels for 4% -> 5%
where the time goes in v6:
time: 39.5 us; the launch traced here: 39.1 us
  Pallas kernels  13.5 us (34%)
  blocking collectives  9.44 us (24%)
  starting transfers between devices  8.59 us (22%)
  waiting for transfers between devices  3.97 us (10%)
  local copies, waits for them, and re-layouts  2.81 us (7%)
  between operations  0.73 us (2%)
    all_to_all x1, blocking collectives, shards(): tables = lax.all_to_all(table, ('cell', 'rep'), 0, 0, tiled=True)  9.44 us
    all_to_all x1, starting transfers between devices, shards(): lax.all_to_all(sent.reshape(n_cell * n_part, lc * RECORD, cap), PART_AXES...  7.5 us
    pallas_call x1, Pallas kernels, shards(): pl.pallas_call(functools.partial(cells_kernel, n_cell, freq_count, lc), i...  7.34 us
    all_to_all x1, waiting for transfers between devices, shards(): lax.all_to_all(sent.reshape(n_cell * n_part, lc * RECORD, cap), PART_AXES...  3.8 us
    pallas_call x2, Pallas kernels, shards(): pl.pallas_call(functools.partial(unpack_kernel, tuple((place for place, _...  2.9 us
    unnamed x10, local copies, waits for them, and re-layouts  2.8 us
    pallas_call x1, Pallas kernels, shards(): pl.pallas_call(functools.partial(place_kernel, cells_all, cap, n_cell, n_...  2.54 us
    ppermute x3, starting transfers between devices, exchange(): return lax.ppermute(value, axes, [(i, i ^ k) for i in range(count)])  1.09 us
  transfers between devices with their start and end apart: 4, of which 2 were waited for; matrix products, arithmetic and copies ran while one was open for 0% of the time, Pallas kernels for 5%

profile of v6, /device:TPU:0, one launch (start us, length us, event | category | flops | bytes accessed | tf_op | source)
XLA Modules:
  0.0 39.1 jit_solution(11817504151559519882)
XLA Ops:
  0.6 2.5 %place.1 = bf16[512,128]{1,0:T(8,128)(2,1)} custom-call(f32[4,2048]{1,0:T(4,128)} %refs_0_.3, f32[4,2048]{1,0:T(4,128)} %refs_1_.3, s32[1,2048]{1,0:T(1,128)} %bitcast.5, s32[1,2048]{1,0:T(1,128)} %bitcast.6, s32[1,2048]{1,0:T(1,128)} %bitcast.7, f32[3,64]{1,0:T(4,128)} %refs_5_.1), custom_call_target="tpu_custom_call" | custom-call | flops 3000000000 | bytes 9000000 | tf_op jit(solution)/shard_map/place/pallas_call | solution.py:343
  3.2 0.0 copy-start.4
  3.2 0.0 copy-start.2
  3.2 7.5 %all-to-all-start = ((bf16[16,32,128]{2,1,0:T(8,128)(2,1)}), bf16[16,32,128]{2,1,0:T(8,128)(2,1)S(1)}, u32[]{:S(2)}, u32[]{:S(2)}) async-start(bf16[16,32,128]{2,1,0:T(8,128)(2,1)} %bitcast.4), calls=%async_computation | async-start | bytes 262144 | tf_op jit(solution)/shard_map/all_to_all | solution.py:357
  10.7 0.0 copy-done.4
  10.7 0.0 copy-start.3
  10.7 0.0 copy-done.2
  10.8 0.7 %copy-done.3 = bf16[48,256]{1,0:T(8,128)(2,1)S(1)} copy-done((bf16[48,256]{1,0:T(8,128)(2,1)S(1)}, bf16[48,256]{1,0:T(8,128)(2,1)}, u32[]{:S(2)}) %copy-start.3) | copy-done | bytes 24600
  11.5 0.0 copy-start
  11.5 1.0 %copy-done = bf16[8,128,256]{2,1,0:T(8,128)(2,1)S(1)} copy-done((bf16[8,128,256]{2,1,0:T(8,128)(2,1)S(1)}, bf16[8,128,256]{2,1,0:T(8,128)(2,1)}, u32[]{:S(2)}) %copy-start) | copy-done | bytes 524312
  12.5 0.0 copy-start.1
  12.5 1.0 %copy-done.1 = bf16[8,256,128]{2,1,0:T(8,128)(2,1)S(1)} copy-done((bf16[8,256,128]{2,1,0:T(8,128)(2,1)S(1)}, bf16[8,256,128]{2,1,0:T(8,128)(2,1)}, u32[]{:S(2)}) %copy-start.1) | copy-done | bytes 524312
  13.5 0.7 %prepare.1 = (bf16[2,128,256]{2,1,0:T(8,128)(2,1)S(1)}, bf16[2,256,128]{2,1,0:T(8,128)(2,1)S(1)}, bf16[2,48,128]{2,1,0:T(8,128)(2,1)S(1)}, bf16[2,256,128]{2,1,0...) custom-call(bf16[48,256]{1,0:T(8,128)(2,1)S(1)} %copy-done.3, ...), custom_call_target="tpu_custom_call" | custom-call | flops 2000000000 | bytes 6000000 | tf_op jit(solution)/shard_map/prepare/pallas_call | solution.py:369
  14.3 3.8 %all-to-all-done.refs_7_ = bf16[16,32,128]{2,1,0:T(8,128)(2,1)S(1)} async-done(((bf16[16,32,128]{2,1,0:T(8,128)(2,1)}), bf16[16,32,128]{2,1,0:T(8,128)(2,1)S(1)}, u32[]{:S(2)}, u32[]{:S(2)}) %all-to-all-start) | async-done | bytes 131104 | tf_op jit(solution)/shard_map/all_to_all | solution.py:357
  18.1 7.3 %cells.1 = (bf16[1152,128]{1,0:T(8,128)(2,1)S(1)}, bf16[8,32,128]{2,1,0:T(8,128)(2,1)S(1)}) custom-call(bf16[48,256]{1,0:T(8,128)(2,1)S(1)} %copy-done.3, bf16[2,128,256]{2,1,0:T(8,128)(2,1)S(1)} %get-tuple-element.19.refs_0_, bf16[2,256,128]{2,1,0:T(8,128)(2,1)S(1)} %get-tuple-element.20.refs_1_, bf16[2,48,128]{2,1,0:T(8,128)(2,1)S(1)} %get-tuple-element.21.refs_2_, ...), custom_call_target="tpu_custom_call" | custom-call | flops 10000000000 | bytes 30000000 | tf_op jit(solution)/shard_map/cells/pallas_call | solution.py:384
  25.4 0.1 collective-permute-start.1
  25.6 0.9 %collective-permute-start = (bf16[1152,128]{1,0:T(8,128)(2,1)S(1)}, bf16[1152,128]{1,0:T(8,128)(2,1)S(1)}, u32[]{:S(2)}, u32[]{:S(2)}) collective-permute-start(bf16[1152,128]{1,0:T(8,128)(2,1)S(1)} %get-tuple-element.27.refs_0_), channel_id=1, source_target_pairs={{0,2},{2,0},{1,3},{3,1},{4,6},{6,4},{5,7},{7,5},{8,10},{10,8},{9,1... | collective-permute-start | bytes 884744 | tf_op jit(solution)/shard_map/ppermute | solution.py:318
  26.4 9.4 %all_to_all.10.tables_ref = bf16[8,32,128]{2,1,0:T(8,128)(2,1)S(1)} all-to-all(bf16[8,32,128]{2,1,0:T(8,128)(2,1)S(1)} %get-tuple-element.26), channel_id=1, replica_groups=mesh['groups'=2,'cell'=4,'rep'=2,'sub'=2] {'cell','rep'}, dimensions={0} | all-to-all | bytes 131072 | tf_op jit(solution)/shard_map/all_to_all | solution.py:400
  35.9 0.0 collective-permute-done.1._.refs_1_
  35.9 0.0 collective-permute-done.packed_ref.refs_2_
  35.9 0.1 collective-permute-start.2
  36.0 1.4 %unpack.2 = (f32[8,128,256]{2,1,0:T(8,128)}, f32[8,256,128]{2,1,0:T(8,128)}, f32[8,48,128]{2,1,0:T(8,128)}, f32[8,4,128]{2,1,0:T(4,128)}) custom-call(bf16[1152,128]{1,0:T(8,128)(2,1)S(1)} %get-tuple-element.27.refs_0_, bf16[1152,128]{1,0:T(8,128)(2,1)S(1)} %collective-permute-done.1._.refs_1_, bf16[1152,128]{1,0:T(8,128)(2,1)S(1)} %collective-permute-done.packed_ref.refs_2_), custom_call_target="tpu_custom_call" | custom-call | tf_op jit(solution)/shard_map/unpack/pallas_call | solution.py:434
  37.4 0.2 collective-permute-done.2.refs_0_
  37.6 1.5 %unpack.3 = (f32[8,128,256]{2,1,0:T(8,128)}, f32[8,256,128]{2,1,0:T(8,128)}, f32[8,48,128]{2,1,0:T(8,128)}, f32[8,4,128]{2,1,0:T(4,128)}, f32[3,64]{1,0:T(4,128)}, /*index=5*/f32[48,64]{1,0:T(8,128)}) custom-call(bf16[1184,128]{1,0:T(8,128)(2,1)S(1)} %collective-permute-done.2.refs_0_, ...), custom_call_target="tpu_custom_call", output_to_operand_aliasing={{0}: (2, {}), {1}: (3, {}), {2}: (4, {}), {3}: (5, {})} | custom-call | tf_op jit(solution)/shard_map/unpack/pallas_call | solution.py:434
  (2 shorter events, 0.0 us)
Async XLA Ops:
  3.2 7.5 %copy-start.4 = (bf16[8,4,128]{2,1,0:T(4,128)(2,1)S(1)}, bf16[8,4,128]{2,1,0:T(4,128)(2,1)}, u32[]{:S(2)}) copy-start(bf16[8,4,128]{2,1,0:T(4,128)(2,1)} %param.19) | copy-start | bytes 24580
  3.2 7.6 %copy-start.2 = (bf16[8,48,128]{2,1,0:T(8,128)(2,1)S(1)}, bf16[8,48,128]{2,1,0:T(8,128)(2,1)}, u32[]{:S(2)}) copy-start(bf16[8,48,128]{2,1,0:T(8,128)(2,1)} %refs_2_.1) | copy-start | bytes 294916
  3.2 14.9 %all-to-all-start = ((bf16[16,32,128]{2,1,0:T(8,128)(2,1)}), bf16[16,32,128]{2,1,0:T(8,128)(2,1)S(1)}, u32[]{:S(2)}, u32[]{:S(2)}) async-start(bf16[16,32,128]{2,1,0:T(8,128)(2,1)} %bitcast.4), calls=%async_computation | async-start | bytes 262144 | tf_op jit(solution)/shard_map/all_to_all | solution.py:357
  10.7 0.7 %copy-start.3 = (bf16[48,256]{1,0:T(8,128)(2,1)S(1)}, bf16[48,256]{1,0:T(8,128)(2,1)}, u32[]{:S(2)}) copy-start(bf16[48,256]{1,0:T(8,128)(2,1)} %codes_ref.3) | copy-start | bytes 73732
  11.5 1.0 %copy-start = (bf16[8,128,256]{2,1,0:T(8,128)(2,1)S(1)}, bf16[8,128,256]{2,1,0:T(8,128)(2,1)}, u32[]{:S(2)}) copy-start(bf16[8,128,256]{2,1,0:T(8,128)(2,1)} %refs_0_.2) | copy-start | bytes 1572868
  12.5 1.0 %copy-start.1 = (bf16[8,256,128]{2,1,0:T(8,128)(2,1)S(1)}, bf16[8,256,128]{2,1,0:T(8,128)(2,1)}, u32[]{:S(2)}) copy-start(bf16[8,256,128]{2,1,0:T(8,128)(2,1)} %refs_1_.2) | copy-start | bytes 1572868
  25.4 10.5 %collective-permute-start.1 = (bf16[1152,128]{1,0:T(8,128)(2,1)S(1)}, bf16[1152,128]{1,0:T(8,128)(2,1)S(1)}, u32[]{:S(2)}, u32[]{:S(2)}) collective-permute-start(bf16[1152,128]{1,0:T(8,128)(2,1)S(1)} %get-tuple-element.27.refs_0_), channel_id=1, source_target_pairs={{0,1},{1,0},{2,3},{3,2},{4,5},{5,4},{6,7},{7,6},{8,9},{9,8},{10,11... | collective-permute-start | bytes 884744 | tf_op jit(solution)/shard_map/ppermute | solution.py:318
  25.6 10.3 %collective-permute-start = (bf16[1152,128]{1,0:T(8,128)(2,1)S(1)}, bf16[1152,128]{1,0:T(8,128)(2,1)S(1)}, u32[]{:S(2)}, u32[]{:S(2)}) collective-permute-start(bf16[1152,128]{1,0:T(8,128)(2,1)S(1)} %get-tuple-element.27.refs_0_), channel_id=1, source_target_pairs={{0,2},{2,0},{1,3},{3,1},{4,6},{6,4},{5,7},{7,5},{8,10},{10,8},{9,1... | collective-permute-start | bytes 884744 | tf_op jit(solution)/shard_map/ppermute | solution.py:318
  35.9 1.7 %collective-permute-start.2 = (bf16[1184,128]{1,0:T(8,128)(2,1)S(1)}, bf16[1184,128]{1,0:T(8,128)(2,1)S(1)}, u32[]{:S(2)}, u32[]{:S(2)}) collective-permute-start(bf16[1184,128]{1,0:T(8,128)(2,1)S(1)} %relay.1.refs_1_), channel_id=1, source_target_pairs={{0,1},{1,0},{2,3},{3,2},{4,5},{5,4},{6,7},{7,6},{8,9},{9,8},{10,11... | collective-permute-start | bytes 909320 | tf_op jit(solution)/shard_map/ppermute | solution.py:318

commit v7 on v6

--- a/solution.py
+++ b/solution.py
@@ -266,13 +266,27 @@
         here, refs = refs[0], refs[1:]
     outs, refs = refs[n_prev:n_prev + 4], refs[n_prev + 4:]
     camera_outs, refs = (refs[:2], refs[2:]) if tables_at else ((), refs)
-    wide, sems = refs[:-1], refs[-1]
+    wide, sems, refs = refs[:4], refs[4], refs[5:]
     enc_v, hidden_v, code_v, out_v = wide
     enc_rows, enc_cols = enc_v.shape[1:]
     hidden, color = hidden_v.shape[1:]
     code, out_rows = code_v.shape[1], out_v.shape[1]
     me_part = lax.axis_index(PART_AXES)
     copies = []
+    if tables_at:
+        cams = camera_outs[0].shape[1]
+        first = lc * packed_rows
+        total = here[first:, :].astype(F32)
+        for i in tables_at:
+            total = total + ins[i][first:, :].astype(F32)
+        total = jnp.concatenate([total[:, c:c + cams] for c in range(0, total.shape[1], cams)], axis=0)
+        camera_sems = refs[2]
+        refs[0][...] = total[code:code + 3]
+        refs[1][...] = total[0:code]
+        for m in range(2):
+            copy = pltpu.make_async_copy(refs[m], camera_outs[m], camera_sems.at[m])
+            copy.start()
+            copies.append(copy)
     for i in range(len(places) * lc):
         cell = (me_part ^ places[i // lc]) * lc + i % lc
         src = ins[i // lc]
@@ -295,15 +309,6 @@
         out_v[i] = src[row:row + RECORD, :].astype(F32)[TANGENT_ROW:TANGENT_ROW + out_rows]
         send(2)
         send(3)
-    if tables_at:
-        cams = camera_outs[0].shape[1]
-        first = lc * packed_rows
-        total = here[first:, :].astype(F32)
-        for i in tables_at:
-            total = total + ins[i][first:, :].astype(F32)
-        total = jnp.concatenate([total[:, c:c + cams] for c in range(0, total.shape[1], cams)], axis=0)
-        camera_outs[0][...] = total[code:code + 3]
-        camera_outs[1][...] = total[0:code]
     for copy in copies:
         copy.wait()
 
@@ -437,9 +442,11 @@
             ),
             out_shape=shapes + sums_shape,
             in_specs=[vmem] * (len(group) + len(here)) + [hbm] * len(grads),
-            out_specs=[hbm] * 4 + [vmem] * len(sums_shape),
+            out_specs=[hbm] * (4 + len(sums_shape)),
             scratch_shapes=[pltpu.VMEM((len(group) * lc,) + a.shape[1:], F32) for a in shapes]
-            + [pltpu.SemaphoreType.DMA((len(group) * lc, 4))],
+            + [pltpu.SemaphoreType.DMA((len(group) * lc, 4))]
+            + [pltpu.VMEM(a.shape, a.dtype) for a in sums_shape]
+            + ([pltpu.SemaphoreType.DMA((2,))] if sums_shape else []),
             input_output_aliases={len(group) + len(here) + i: i for i in range(len(grads))},
             compiler_params=params,
             cost_estimate=cost(0),

time: 39.5 us -> 39 us (0.987)
  Pallas kernels: 13.5 us -> 12.9 us
    pallas_call x2, Pallas kernels: 2.9 us -> 2.33 us  [shards(): pl.pallas_call(functools.partial(unpack_kernel, tuple((place for place, _...]
  transfers between devices with their start and end apart: 4 -> 4, of which waited for: 2 -> 2; matrix products, arithmetic and copies ran while one was open for 0% -> 0% of each run, Pallas kernels for 5% -> 6%
where the time goes in v7:
time: 39 us; the launch traced here: 38.5 us
  Pallas kernels  12.9 us (33%)
  blocking collectives  9.44 us (24%)
  starting transfers between devices  8.59 us (22%)
  waiting for transfers between devices  3.97 us (10%)
  local copies, waits for them, and re-layouts  2.81 us (7%)
  between operations  0.73 us (2%)
    all_to_all x1, blocking collectives, shards(): tables = lax.all_to_all(table, ('cell', 'rep'), 0, 0, tiled=True)  9.44 us
    all_to_all x1, starting transfers between devices, shards(): lax.all_to_all(sent.reshape(n_cell * n_part, lc * RECORD, cap), PART_AXES...  7.5 us
    pallas_call x1, Pallas kernels, shards(): pl.pallas_call(functools.partial(cells_kernel, n_cell, freq_count, lc), i...  7.34 us
    all_to_all x1, waiting for transfers between devices, shards(): lax.all_to_all(sent.reshape(n_cell * n_part, lc * RECORD, cap), PART_AXES...  3.8 us
    unnamed x10, local copies, waits for them, and re-layouts  2.8 us
    pallas_call x1, Pallas kernels, shards(): pl.pallas_call(functools.partial(place_kernel, cells_all, cap, n_cell, n_...  2.54 us
    pallas_call x2, Pallas kernels, shards(): pl.pallas_call(functools.partial(unpack_kernel, tuple((place for place, _...  2.33 us
    ppermute x3, starting transfers between devices, exchange(): return lax.ppermute(value, axes, [(i, i ^ k) for i in range(count)])  1.09 us
  transfers between devices with their start and end apart: 4, of which 2 were waited for; matrix products, arithmetic and copies ran while one was open for 0% of the time, Pallas kernels for 6%

profile of v7, /device:TPU:0, one launch (start us, length us, event | category | flops | bytes accessed | tf_op | source)
XLA Modules:
  0.0 38.5 jit_solution(18239372728428056611)
XLA Ops:
  0.6 2.5 %place.1 = bf16[512,128]{1,0:T(8,128)(2,1)} custom-call(f32[4,2048]{1,0:T(4,128)} %refs_0_.3, f32[4,2048]{1,0:T(4,128)} %refs_1_.3, s32[1,2048]{1,0:T(1,128)} %bitcast.5, s32[1,2048]{1,0:T(1,128)} %bitcast.6, s32[1,2048]{1,0:T(1,128)} %bitcast.7, f32[3,64]{1,0:T(4,128)} %refs_5_.1), custom_call_target="tpu_custom_call" | custom-call | flops 3000000000 | bytes 9000000 | tf_op jit(solution)/shard_map/place/pallas_call | solution.py:348
  3.2 0.0 copy-start.4
  3.2 0.0 copy-start.2
  3.2 7.5 %all-to-all-start = ((bf16[16,32,128]{2,1,0:T(8,128)(2,1)}), bf16[16,32,128]{2,1,0:T(8,128)(2,1)S(1)}, u32[]{:S(2)}, u32[]{:S(2)}) async-start(bf16[16,32,128]{2,1,0:T(8,128)(2,1)} %bitcast.4), calls=%async_computation | async-start | bytes 262144 | tf_op jit(solution)/shard_map/all_to_all | solution.py:362
  10.7 0.0 copy-done.4
  10.7 0.0 copy-start.3
  10.7 0.0 copy-done.2
  10.8 0.7 %copy-done.3 = bf16[48,256]{1,0:T(8,128)(2,1)S(1)} copy-done((bf16[48,256]{1,0:T(8,128)(2,1)S(1)}, bf16[48,256]{1,0:T(8,128)(2,1)}, u32[]{:S(2)}) %copy-start.3) | copy-done | bytes 24600
  11.5 0.0 copy-start
  11.5 1.0 %copy-done = bf16[8,128,256]{2,1,0:T(8,128)(2,1)S(1)} copy-done((bf16[8,128,256]{2,1,0:T(8,128)(2,1)S(1)}, bf16[8,128,256]{2,1,0:T(8,128)(2,1)}, u32[]{:S(2)}) %copy-start) | copy-done | bytes 524312
  12.5 0.0 copy-start.1
  12.5 1.0 %copy-done.1 = bf16[8,256,128]{2,1,0:T(8,128)(2,1)S(1)} copy-done((bf16[8,256,128]{2,1,0:T(8,128)(2,1)S(1)}, bf16[8,256,128]{2,1,0:T(8,128)(2,1)}, u32[]{:S(2)}) %copy-start.1) | copy-done | bytes 524312
  13.5 0.7 %prepare.1 = (bf16[2,128,256]{2,1,0:T(8,128)(2,1)S(1)}, bf16[2,256,128]{2,1,0:T(8,128)(2,1)S(1)}, bf16[2,48,128]{2,1,0:T(8,128)(2,1)S(1)}, bf16[2,256,128]{2,1,0...) custom-call(bf16[48,256]{1,0:T(8,128)(2,1)S(1)} %copy-done.3, ...), custom_call_target="tpu_custom_call" | custom-call | flops 2000000000 | bytes 6000000 | tf_op jit(solution)/shard_map/prepare/pallas_call | solution.py:374
  14.3 3.8 %all-to-all-done.refs_7_ = bf16[16,32,128]{2,1,0:T(8,128)(2,1)S(1)} async-done(((bf16[16,32,128]{2,1,0:T(8,128)(2,1)}), bf16[16,32,128]{2,1,0:T(8,128)(2,1)S(1)}, u32[]{:S(2)}, u32[]{:S(2)}) %all-to-all-start) | async-done | bytes 131104 | tf_op jit(solution)/shard_map/all_to_all | solution.py:362
  18.1 7.3 %cells.1 = (bf16[1152,128]{1,0:T(8,128)(2,1)S(1)}, bf16[8,32,128]{2,1,0:T(8,128)(2,1)S(1)}) custom-call(bf16[48,256]{1,0:T(8,128)(2,1)S(1)} %copy-done.3, bf16[2,128,256]{2,1,0:T(8,128)(2,1)S(1)} %get-tuple-element.19.refs_0_, bf16[2,256,128]{2,1,0:T(8,128)(2,1)S(1)} %get-tuple-element.20.refs_1_, bf16[2,48,128]{2,1,0:T(8,128)(2,1)S(1)} %get-tuple-element.21.refs_2_, ...), custom_call_target="tpu_custom_call" | custom-call | flops 10000000000 | bytes 30000000 | tf_op jit(solution)/shard_map/cells/pallas_call | solution.py:389
  25.4 0.1 collective-permute-start.1
  25.6 0.9 %collective-permute-start = (bf16[1152,128]{1,0:T(8,128)(2,1)S(1)}, bf16[1152,128]{1,0:T(8,128)(2,1)S(1)}, u32[]{:S(2)}, u32[]{:S(2)}) collective-permute-start(bf16[1152,128]{1,0:T(8,128)(2,1)S(1)} %get-tuple-element.27.refs_0_), channel_id=1, source_target_pairs={{0,2},{2,0},{1,3},{3,1},{4,6},{6,4},{5,7},{7,5},{8,10},{10,8},{9,1... | collective-permute-start | bytes 884744 | tf_op jit(solution)/shard_map/ppermute | solution.py:323
  26.4 9.4 %all_to_all.10.tables_ref = bf16[8,32,128]{2,1,0:T(8,128)(2,1)S(1)} all-to-all(bf16[8,32,128]{2,1,0:T(8,128)(2,1)S(1)} %get-tuple-element.26), channel_id=1, replica_groups=mesh['groups'=2,'cell'=4,'rep'=2,'sub'=2] {'cell','rep'}, dimensions={0} | all-to-all | bytes 131072 | tf_op jit(solution)/shard_map/all_to_all | solution.py:405
  35.9 0.0 collective-permute-done.1._.refs_1_
  35.9 0.0 collective-permute-done.packed_ref.refs_2_
  35.9 0.1 collective-permute-start.2
  36.0 1.4 %unpack.2 = (f32[8,128,256]{2,1,0:T(8,128)}, f32[8,256,128]{2,1,0:T(8,128)}, f32[8,48,128]{2,1,0:T(8,128)}, f32[8,4,128]{2,1,0:T(4,128)}) custom-call(bf16[1152,128]{1,0:T(8,128)(2,1)S(1)} %get-tuple-element.27.refs_0_, bf16[1152,128]{1,0:T(8,128)(2,1)S(1)} %collective-permute-done.1._.refs_1_, bf16[1152,128]{1,0:T(8,128)(2,1)S(1)} %collective-permute-done.packed_ref.refs_2_), custom_call_target="tpu_custom_call" | custom-call | tf_op jit(solution)/shard_map/unpack/pallas_call | solution.py:439
  37.4 0.2 collective-permute-done.2.refs_0_
  37.6 0.9 %unpack.3 = (f32[8,128,256]{2,1,0:T(8,128)}, f32[8,256,128]{2,1,0:T(8,128)}, f32[8,48,128]{2,1,0:T(8,128)}, f32[8,4,128]{2,1,0:T(4,128)}, f32[3,64]{1,0:T(4,128)}, /*index=5*/f32[48,64]{1,0:T(8,128)}) custom-call(bf16[1184,128]{1,0:T(8,128)(2,1)S(1)} %collective-permute-done.2.refs_0_, ...), custom_call_target="tpu_custom_call", output_to_operand_aliasing={{0}: (2, {}), {1}: (3, {}), {2}: (4, {}), {3}: (5, {})} | custom-call | tf_op jit(solution)/shard_map/unpack/pallas_call | solution.py:439
  (2 shorter events, 0.0 us)
Async XLA Ops:
  3.2 7.5 %copy-start.4 = (bf16[8,4,128]{2,1,0:T(4,128)(2,1)S(1)}, bf16[8,4,128]{2,1,0:T(4,128)(2,1)}, u32[]{:S(2)}) copy-start(bf16[8,4,128]{2,1,0:T(4,128)(2,1)} %param.19) | copy-start | bytes 24580
  3.2 7.6 %copy-start.2 = (bf16[8,48,128]{2,1,0:T(8,128)(2,1)S(1)}, bf16[8,48,128]{2,1,0:T(8,128)(2,1)}, u32[]{:S(2)}) copy-start(bf16[8,48,128]{2,1,0:T(8,128)(2,1)} %refs_2_.1) | copy-start | bytes 294916
  3.2 14.9 %all-to-all-start = ((bf16[16,32,128]{2,1,0:T(8,128)(2,1)}), bf16[16,32,128]{2,1,0:T(8,128)(2,1)S(1)}, u32[]{:S(2)}, u32[]{:S(2)}) async-start(bf16[16,32,128]{2,1,0:T(8,128)(2,1)} %bitcast.4), calls=%async_computation | async-start | bytes 262144 | tf_op jit(solution)/shard_map/all_to_all | solution.py:362
  10.7 0.7 %copy-start.3 = (bf16[48,256]{1,0:T(8,128)(2,1)S(1)}, bf16[48,256]{1,0:T(8,128)(2,1)}, u32[]{:S(2)}) copy-start(bf16[48,256]{1,0:T(8,128)(2,1)} %codes_ref.3) | copy-start | bytes 73732
  11.5 1.0 %copy-start = (bf16[8,128,256]{2,1,0:T(8,128)(2,1)S(1)}, bf16[8,128,256]{2,1,0:T(8,128)(2,1)}, u32[]{:S(2)}) copy-start(bf16[8,128,256]{2,1,0:T(8,128)(2,1)} %refs_0_.2) | copy-start | bytes 1572868
  12.5 1.0 %copy-start.1 = (bf16[8,256,128]{2,1,0:T(8,128)(2,1)S(1)}, bf16[8,256,128]{2,1,0:T(8,128)(2,1)}, u32[]{:S(2)}) copy-start(bf16[8,256,128]{2,1,0:T(8,128)(2,1)} %refs_1_.2) | copy-start | bytes 1572868
  25.4 10.5 %collective-permute-start.1 = (bf16[1152,128]{1,0:T(8,128)(2,1)S(1)}, bf16[1152,128]{1,0:T(8,128)(2,1)S(1)}, u32[]{:S(2)}, u32[]{:S(2)}) collective-permute-start(bf16[1152,128]{1,0:T(8,128)(2,1)S(1)} %get-tuple-element.27.refs_0_), channel_id=1, source_target_pairs={{0,1},{1,0},{2,3},{3,2},{4,5},{5,4},{6,7},{7,6},{8,9},{9,8},{10,11... | collective-permute-start | bytes 884744 | tf_op jit(solution)/shard_map/ppermute | solution.py:323
  25.6 10.3 %collective-permute-start = (bf16[1152,128]{1,0:T(8,128)(2,1)S(1)}, bf16[1152,128]{1,0:T(8,128)(2,1)S(1)}, u32[]{:S(2)}, u32[]{:S(2)}) collective-permute-start(bf16[1152,128]{1,0:T(8,128)(2,1)S(1)} %get-tuple-element.27.refs_0_), channel_id=1, source_target_pairs={{0,2},{2,0},{1,3},{3,1},{4,6},{6,4},{5,7},{7,5},{8,10},{10,8},{9,1... | collective-permute-start | bytes 884744 | tf_op jit(solution)/shard_map/ppermute | solution.py:323
  35.9 1.7 %collective-permute-start.2 = (bf16[1184,128]{1,0:T(8,128)(2,1)S(1)}, bf16[1184,128]{1,0:T(8,128)(2,1)S(1)}, u32[]{:S(2)}, u32[]{:S(2)}) collective-permute-start(bf16[1184,128]{1,0:T(8,128)(2,1)S(1)} %relay.1.refs_1_), channel_id=1, source_target_pairs={{0,1},{1,0},{2,3},{3,2},{4,5},{5,4},{6,7},{7,6},{8,9},{9,8},{10,11... | collective-permute-start | bytes 909320 | tf_op jit(solution)/shard_map/ppermute | solution.py:323
